TPU v7x, 32 devices: a whole 2x2x4 slice. The times are simulated.
32 devices in a mesh: groups: 2 (over y), rows: 4 (over z), cols: 2 (over x), rhs: 2 (over core).
Axes of the slice: x: 2, y: 2, z: 4, core: 2. Of those that a mesh axis runs over, the one named last changes fastest.
Arguments:
- influence: bfloat16 [32768, 16384], P(('groups', 'rows'), 'cols'), parts along dimension 0, may hold values from -0.046875 to 0.046875
- wake_influence: bfloat16 [32768, 1024], P(('groups', 'rows'), 'cols'), parts along dimension 0, may hold values from -0.0234375 to 0.0234375
- self_term: float32 [32768], P(('groups', 'rows')), parts along dimension 0, may hold values from 2 to 4
- wake_upper: int32 [2048], P(('groups', 'cols')), parts along dimension 0, may hold values from 0 to 16383, as said below
- wake_lower: int32 [2048], P(('groups', 'cols')), parts along dimension 0, may hold values from 0 to 16383, as said below
- blade_of: int32 [32768], P(('groups', 'rows')), parts along dimension 0, may hold values from 0 to 4, never falling along the last dimension, each value on 1 to 4096 neighbouring positions
- mode_shapes: float32 [16, 16384], P(None, 'rows'), may hold values from -100 to 100
- blade_pitch: float32 [5, 16], P(None, 'rhs'), may hold values from 0.5 to 2
- design_map: int32 [16], P('rhs'), may hold values from 0 to 15
- objectives: float32 [16, 16384], P('rhs', 'rows'), may hold values from -6 to 6
Outputs:
- solution: float32 [16, 32768], P('rhs', ('groups', 'rows', 'cols')), parts along dimension 1
- adjoint: float32 [16, 32768], P('rhs', ('groups', 'rows', 'cols')), parts along dimension 1
There are 2 independent parts, one for each index of `groups`. A program takes and returns all parts, laid end to end along the dimension named above; an argument that names none is the same for every part. Nothing has to cross between parts.
Inputs may be any that keep to these rules, and one draw needn't show every extreme that they name: `wake_upper`: the two trailing-edge panels of wake panel j differ and both lie among panels c * 8192 to (c + 1) * 8192 - 1, where c = j // 512. `wake_lower`: the two trailing-edge panels of wake panel j differ and both lie among panels c * 8192 to (c + 1) * 8192 - 1, where c = j // 512.
All inputs are finite; a program needn't handle non-finite values.
Results may differ from a plain program's by a relative error of at most 0.0013.
Values may be sent and summed in bfloat16 or wider, within the bound.
No kernel may reach another device: no remote copies, remote signals or barrier semaphores. Data moves between devices by JAX's collectives and lax.ppermute only.
A program may use at most 192 MiB of HBM per device.

v0:
```python
import functools

import jax
import jax.numpy as jnp
from jax import lax
from jax.experimental import pallas as pl
from jax.experimental.pallas import tpu as pltpu
from jax.sharding import PartitionSpec as P

BLOCK = 8
LANES = 128
SHIFT = 3.0
GRID = ("rows", "cols", "rhs")
F32 = jnp.float32
BF16 = jnp.bfloat16

VMEM = pl.BlockSpec(memory_space=pltpu.VMEM)
SMEM = pl.BlockSpec(memory_space=pltpu.SMEM)
ANY = pl.BlockSpec(memory_space=pl.ANY)

CORE, CHUNKS = 0, 1


def dot(left, right, dims):
    return lax.dot_general(left, right, (dims, ((), ())), preferred_element_type=F32)


def precise(left, right, dims):
    return lax.dot_general(
        left, right, (dims, ((), ())), precision=lax.Precision.HIGHEST, preferred_element_type=F32
    )


def low_onehot(index):
    low = jnp.bitwise_and(index, LANES - 1)
    hit = lax.broadcasted_iota(jnp.int32, (LANES, index.shape[1]), 0) == low
    return jnp.where(hit, 1.0, 0.0).astype(BF16)


def take_columns(field, index):
    rows, width = field.shape
    chunks = width // LANES
    stacked = jnp.concatenate(
        [field[:, i * LANES : (i + 1) * LANES] for i in range(chunks)], axis=0
    )
    picked = dot(stacked, low_onehot(index), ((1,), (0,)))
    high = jnp.right_shift(index, 7)
    total = jnp.zeros((rows, index.shape[1]), F32)
    for i in range(chunks):
        total = total + jnp.where(high == i, picked[i * rows : (i + 1) * rows], 0.0)
    return total


def put_columns(values, index, width):
    rows = values.shape[0]
    chunks = width // LANES
    upper = values.astype(BF16).astype(F32)
    parts = (upper, values - upper)
    high = jnp.right_shift(index, 7)
    onehot = low_onehot(index)
    total = None
    for part in parts:
        stacked = jnp.concatenate(
            [jnp.where(high == i, part, 0.0).astype(BF16) for i in range(chunks)], axis=0
        )
        spread = dot(stacked, onehot, ((1,), (1,)))
        total = spread if total is None else total + spread
    return jnp.concatenate([total[i * rows : (i + 1) * rows] for i in range(chunks)], axis=1)


def both_cores(core, own, other):
    first = jnp.where(core == 0, own, other)
    second = jnp.where(core == 0, other, own)
    return jnp.concatenate([first, second], axis=0)


def load_copies(influence, wake, held, sems, first, base, chunk):
    def copies(i):
        source = pl.ds(pl.multiple_of(first + base + i * chunk, 16), chunk)
        target = pl.ds(i * chunk, chunk)
        panels = influence.shape[1]
        return (
            pltpu.make_async_copy(
                influence.at[source], held.at[target, pl.ds(0, panels)], sems.at[0, i]
            ),
            pltpu.make_async_copy(
                wake.at[source], held.at[target, pl.ds(panels, wake.shape[1])], sems.at[1, i]
            ),
        )

    return copies


def right_kernel(
    chunk, half, scalars, pitch, pitch_other, modes, modes_other, blade, shapes, influence, wake,
    right, gram, held, sems
):
    core = scalars[CORE]
    copies = load_copies(influence, wake, held, sems, core * half, 0, chunk)
    steps = held.shape[0] // chunk
    for i in range(steps):
        for copy in copies(i):
            copy.start()
    blades = pitch.shape[0]
    blade_onehot = jnp.where(
        lax.broadcasted_iota(jnp.int32, (blades, blade.shape[1]), 0) == blade[...], 1.0, 0.0
    )
    for b in range(2):
        own = core == b
        amount = jnp.where(own, pitch[...], pitch_other[...])
        mode = jnp.where(own, modes[...], modes_other[...])
        mode_onehot = jnp.where(
            lax.broadcasted_iota(jnp.int32, (shapes.shape[0], BLOCK), 0) == mode, 1.0, 0.0
        )
        pattern = precise(mode_onehot, shapes[...], ((0,), (0,)))
        factor = precise(amount, blade_onehot, ((0,), (0,)))
        right[b * BLOCK : (b + 1) * BLOCK, :] = pattern * factor
    gram[...] = precise(right[...], right[...], ((1,), (1,)))
    for i in range(steps):
        for copy in copies(i):
            copy.wait()


def finish_adjoint(scalars, upper, lower, whole, keep, give):
    piece = keep.shape[1]
    panels = 2 * piece
    carried = whole[:, panels:]
    whole[:, 0:panels] += put_columns(carried, upper[...], panels) - put_columns(
        carried, lower[...], panels
    )
    core = scalars[CORE]
    keep[...] = whole[:, pl.ds(pl.multiple_of(core * piece, LANES), piece)]
    give[...] = whole[:, pl.ds(pl.multiple_of((1 - core) * piece, LANES), piece)]


def load_adjoint_kernel(
    chunk, scalars, objectives, objectives_other, self_term, upper, lower, held_first, influence,
    wake, keep, give, start, target, self_half, held, whole, sems
):
    half = start.shape[1]
    first_rows = held_first.shape[0]
    core = scalars[CORE]
    copies = load_copies(influence, wake, held, sems, core * half, first_rows, chunk)
    steps = held.shape[0] // chunk
    for i in range(steps):
        for copy in copies(i):
            copy.start()
    span = pl.ds(pl.multiple_of(core * half, LANES), half)
    target[...] = both_cores(core, objectives[:, span], objectives_other[:, span])
    self_half[...] = self_term[:, span]
    start[...] = target[...] / self_half[...]
    field = start[...].astype(BF16)
    whole[...] = dot(field[:, 0:first_rows], held_first[...], ((1,), (0,)))
    for i in range(steps):
        for copy in copies(i):
            copy.wait()
        begin = first_rows + i * chunk
        whole[...] += dot(
            field[:, begin : begin + chunk],
            held[i * chunk : (i + 1) * chunk, :],
            ((1,), (0,)),
        )
    finish_adjoint(scalars, upper, lower, whole, keep, give)


def adjoint_kernel(
    tile, n_in, scalars, previous, target, self_half, upper, lower, held_first, held, *rest
):
    parts, (keep, give, adjoint, whole) = rest[:n_in], rest[n_in:]
    image = self_half[...] * previous[...]
    for part in parts:
        image = image + part[...].astype(F32)
    adjoint[...] = previous[...] + (target[...] - image) / self_half[...]
    field = adjoint[...].astype(BF16)
    width = held.shape[1]
    first_rows = held_first.shape[0]
    for start in range(0, width, tile):
        stop = min(width, start + tile)
        whole[:, start:stop] = dot(
            field[:, 0:first_rows], held_first[:, start:stop], ((1,), (0,))
        ) + dot(field[:, first_rows:], held[:, start:stop], ((1,), (0,)))
    finish_adjoint(scalars, upper, lower, whole, keep, give)


def forward_kernel(tile, places, scalars, upper, lower, held_first, held, *rest):
    shards, (out, field) = rest[: len(places)], rest[len(places) :]
    for place, ref in zip(places, shards):
        begin = pl.multiple_of(scalars[place], LANES)
        field[:, pl.ds(begin, ref.shape[1])] = ref[...]
    panels = held.shape[1] - upper.shape[1]
    source = field[:, 0:panels]
    strength = take_columns(source, upper[...]) - take_columns(source, lower[...])
    field[:, panels:] = strength.astype(BF16)
    base = 0
    for part in (held_first, held):
        for start in range(0, part.shape[0], tile):
            stop = min(part.shape[0], start + tile)
            out[:, base + start : base + stop] = dot(
                field[...], part[start:stop, :], ((1,), (1,))
            )
        base += part.shape[0]


def inverse_factor(gram):
    size = gram.shape[0]
    row = lax.broadcasted_iota(jnp.int32, (size, size), 0)
    col = lax.broadcasted_iota(jnp.int32, (size, size), 1)
    left = jnp.where(row == col, 1.0, 0.0)
    for j in range(size - 1):
        scale = jnp.where(
            row[:, 0:1] > j, gram[:, j : j + 1] / gram[j : j + 1, j : j + 1], 0.0
        )
        left = left - scale * left[j : j + 1, :]
        gram = gram - scale * gram[j : j + 1, :]
    pivots = jnp.sum(jnp.where(row == col, gram, 0.0), axis=1, keepdims=True)
    return left / jnp.sqrt(pivots)


def start_kernel(n_parts, scalars, right_piece, right, *rest):
    parts, (rounded, basis, right_half) = rest[:n_parts], rest[n_parts:]
    half = basis.shape[1]
    span = pl.ds(pl.multiple_of(scalars[CORE] * half, LANES), half)
    gram = parts[0][...]
    for part in parts[1:]:
        gram = gram + part[...]
    right_half[...] = right[:, span]
    for b in range(gram.shape[0] // BLOCK):
        rows = slice(b * BLOCK, (b + 1) * BLOCK)
        inverse = inverse_factor(gram[rows, rows])
        rounded[rows, :] = precise(inverse, right_piece[rows, :], ((1,), (0,))).astype(BF16)
        basis[rows, :] = precise(inverse, right_half[rows, :], ((1,), (0,)))


def system_kernel(n_parts, scalars, basis, image, right, self_half, *rest):
    parts, (keep, give) = rest[:n_parts], rest[n_parts:]
    second = self_half[...] * image[...]
    for part in parts:
        second = second + part[...]
    first = image[...] + SHIFT * basis[...]
    core = scalars[CORE]
    keep[...] = jnp.zeros_like(keep)
    give[...] = jnp.zeros_like(give)
    for b in range(2):
        rows = slice(b * BLOCK, (b + 1) * BLOCK)
        images = jnp.concatenate([first[rows], second[rows]], axis=0)
        full = jnp.concatenate([images, right[rows, :]], axis=0)
        system = precise(images, full, ((1,), (1,)))
        size = system.shape[1]

        @pl.when(core == b)
        def _():
            keep[:, 0:size] = system

        @pl.when(core != b)
        def _():
            give[:, 0:size] = system


def solve_kernel(n_parts, basis, *rest):
    parts, out = rest[:n_parts], rest[n_parts]
    system = parts[0][...]
    for part in parts[1:]:
        system = system + part[...]
    size = basis.shape[0]
    row = lax.broadcasted_iota(jnp.int32, (size, 1), 0)
    for j in range(size):
        pivot_row = system[j : j + 1, :] / system[j : j + 1, j : j + 1]
        factor = jnp.where(row == j, 0.0, system[:, j : j + 1])
        system = jnp.where(row == j, pivot_row, system - factor * pivot_row)
    weights = system[:, size : size + BLOCK]
    out[...] = precise(weights, basis[...], ((0,), (0,)))


def params(mib=20):
    return pltpu.CompilerParams(vmem_limit_bytes=mib << 20)


def cost(flops, size):
    return pl.CostEstimate(flops=flops, bytes_accessed=size, transcendentals=0)


def per_device(
    influence,
    wake_influence,
    self_term,
    wake_upper,
    wake_lower,
    blade_of,
    mode_shapes,
    blade_pitch,
    design_map,
    objectives,
):
    influence = pltpu.with_memory_space_constraint(influence, pltpu.HBM)
    wake_influence = pltpu.with_memory_space_constraint(wake_influence, pltpu.HBM)
    n_rows, n_cols, n_rhs = (lax.axis_size(name) for name in GRID)
    side = n_cols * n_rhs
    piece, panels = influence.shape
    wake = wake_influence.shape[1]
    half = piece // n_rhs
    out_width = piece // n_cols
    count = 2 * BLOCK
    width = panels + wake
    if n_rows != side or n_rhs != 2 or panels != 2 * piece:
        raise ValueError("unsupported mesh")
    row_index = lax.axis_index("rows")
    col_index = lax.axis_index("cols")
    core = lax.axis_index("rhs")

    def cross(k):
        return [(a * side + b, b * side + (a ^ k)) for a in range(side) for b in range(side)]

    def fetch(j):
        return [
            (a * side + c * n_rhs + h, ((h ^ j) * n_cols + c) * side + a)
            for a in range(side)
            for c in range(n_cols)
            for h in range(n_rhs)
        ]

    def flip(k, size):
        return [(i, i ^ k) for i in range(size)]

    def swap(value):
        return lax.ppermute(value, "rhs", flip(1, 2))

    def cols_parts(value):
        return [value] + [lax.ppermute(value, "cols", flip(k, n_cols)) for k in range(1, n_cols)]

    near = core * piece
    far = (1 - core) * piece
    chunk_half = row_index // n_cols
    places = [
        near + chunk_half * half,
        near + (1 - chunk_half) * half,
        far + chunk_half * half,
        far + (1 - chunk_half) * half,
        near,
        far,
    ]
    scalars = jnp.stack([core] + places).astype(jnp.int32)
    col_start = col_index * panels
    local_upper = (wake_upper - col_start)[None, :]
    local_lower = (wake_lower - col_start)[None, :]
    self_row = self_term[None, :]

    first_rows = half // 4
    chunk = half // 8
    struct = jax.ShapeDtypeStruct

    modes = design_map[None, :]
    objectives_other = swap(objectives)
    right, gram, held_first = pl.pallas_call(
        functools.partial(right_kernel, chunk, half),
        in_specs=[SMEM] + [VMEM] * 6 + [ANY, ANY],
        out_specs=[VMEM] * 3,
        out_shape=[
            struct((count, piece), F32),
            struct((count, count), F32),
            pltpu.VMEM((first_rows, width), BF16),
        ],
        scratch_shapes=[pltpu.SemaphoreType.DMA((2, first_rows // chunk))],
        compiler_params=params(),
        cost_estimate=cost(0, 2 * first_rows * width),
        name="right",
    )(
        scalars, blade_pitch, swap(blade_pitch), modes, swap(modes), blade_of[None, :], mode_shapes,
        influence, wake_influence,
    )
    right_piece = lax.ppermute(right, GRID, cross(0))
    grams = [gram] + [lax.ppermute(gram, "rows", flip(k, n_rows)) for k in range(1, n_rows)]

    held_first = pltpu.with_memory_space_constraint(held_first, pltpu.VMEM)
    rest_rows = half - first_rows
    keep, give, start, target, self_half, held = pl.pallas_call(
        functools.partial(load_adjoint_kernel, chunk),
        in_specs=[SMEM] + [VMEM] * 6 + [ANY, ANY],
        out_specs=[VMEM] * 6,
        out_shape=[
            struct((count, piece), F32),
            struct((count, piece), F32),
            struct((count, half), F32),
            struct((count, half), F32),
            struct((1, half), F32),
            pltpu.VMEM((rest_rows, width), BF16),
        ],
        scratch_shapes=[
            pltpu.VMEM((count, width), F32),
            pltpu.SemaphoreType.DMA((2, rest_rows // chunk)),
        ],
        compiler_params=params(),
        cost_estimate=cost(2 * count * half * width, 2 * rest_rows * width),
        name="adjoint_one",
    )(
        scalars, objectives, objectives_other, self_row, local_upper, local_lower, held_first,
        influence, wake_influence,
    )
    held = pltpu.with_memory_space_constraint(held, pltpu.VMEM)
    product_cost = cost(2 * count * half * width, 2 * half * width)

    def forward(places, shards, name):
        return pl.pallas_call(
            functools.partial(forward_kernel, 512, places),
            in_specs=[SMEM] + [VMEM] * (4 + len(shards)),
            out_specs=VMEM,
            out_shape=struct((count, half), F32),
            scratch_shapes=[pltpu.VMEM((count, width), BF16)],
            compiler_params=params(),
            cost_estimate=product_cost,
            name=name,
        )(scalars, local_upper, local_lower, held_first, held, *shards)

    rounded, basis, right_half = pl.pallas_call(
        functools.partial(start_kernel, len(grams)),
        in_specs=[SMEM] + [VMEM] * (2 + len(grams)),
        out_specs=[VMEM] * 3,
        out_shape=[
            struct((count, piece), BF16),
            struct((count, half), F32),
            struct((count, half), F32),
        ],
        compiler_params=params(),
        name="start",
    )(scalars, right_piece, right, *grams)
    induced = forward((CHUNKS + 4, CHUNKS + 5), [rounded, swap(rounded)], "forward_one")

    total = keep + swap(give)
    sides = total[:, :half].astype(BF16), total[:, half:].astype(BF16)
    odd = row_index % 2 == 1
    sends = jnp.where(odd, sides[1], sides[0]), jnp.where(odd, sides[0], sides[1])
    parts = [lax.ppermute(sends[k % 2], GRID, cross(k)) for k in range(side)]

    image = sum(cols_parts(induced)) + (self_half - SHIFT) * basis
    image_rounded = image.astype(BF16)

    keep, give, adjoint = pl.pallas_call(
        functools.partial(adjoint_kernel, 512, len(parts)),
        in_specs=[SMEM] + [VMEM] * (7 + len(parts)),
        out_specs=[VMEM] * 3,
        out_shape=[
            struct((count, piece), F32),
            struct((count, piece), F32),
            struct((count, half), F32),
        ],
        scratch_shapes=[pltpu.VMEM((count, width), F32)],
        compiler_params=params(),
        cost_estimate=product_cost,
        name="adjoint_two",
    )(scalars, start, target, self_half, local_upper, local_lower, held_first, held, *parts)

    shards = [lax.ppermute(image_rounded, GRID, fetch(j)) for j in range(2)]
    shards = shards + [swap(value) for value in shards]
    induced = forward(tuple(CHUNKS + i for i in range(4)), shards, "forward_two")

    induced = cols_parts(induced)
    system_keep, system_give = pl.pallas_call(
        functools.partial(system_kernel, len(induced)),
        in_specs=[SMEM] + [VMEM] * (4 + len(induced)),
        out_specs=[VMEM] * 2,
        out_shape=[struct((count, LANES), F32)] * 2,
        compiler_params=params(),
        name="system",
    )(scalars, basis, image, right_half, self_half, *induced)
    system = system_keep + swap(system_give)
    systems = [system] + [lax.ppermute(system, "rows", flip(k, n_rows)) for k in range(1, n_rows)]

    begin = col_index * out_width
    holder = begin // half
    begin = begin % half

    def to_output(*values):
        mine = [lax.dynamic_slice_in_dim(value, begin, out_width, 1) for value in values]

        def rows(which):
            return jnp.concatenate(
                [lax.dynamic_slice_in_dim(v, which * BLOCK, BLOCK, 0) for v in mine], axis=0
            )

        return jnp.where(core == holder, rows(core), swap(rows(1 - core)))

    bases = to_output(basis, image)
    solution = pl.pallas_call(
        functools.partial(solve_kernel, len(systems)),
        in_specs=[VMEM] * (1 + len(systems)),
        out_specs=VMEM,
        out_shape=struct((BLOCK, out_width), F32),
        compiler_params=params(),
        name="solve",
    )(bases, *systems)

    total = keep + swap(give)
    previous = to_output(adjoint)
    span = col_index * out_width
    self_out = lax.dynamic_slice_in_dim(self_term, span, out_width, 0)[None, :]
    target_out = lax.dynamic_slice_in_dim(objectives, span, out_width, 1)
    image = self_out * previous
    for k in range(side):
        goal = jnp.bitwise_xor(row_index, k)
        part = lax.dynamic_slice(
            total, ((goal % n_rhs) * BLOCK, (goal // n_rhs) * out_width), (BLOCK, out_width)
        )
        image = image + lax.ppermute(part, GRID, cross(k))
    adjoint = previous + (target_out - image) / self_out
    return (solution, adjoint)


def solution(mesh):
    in_specs = (
        P(("groups", "rows"), "cols"),
        P(("groups", "rows"), "cols"),
        P(("groups", "rows")),
        P(("groups", "cols")),
        P(("groups", "cols")),
        P(("groups", "rows")),
        P(None, "rows"),
        P(None, "rhs"),
        P("rhs"),
        P("rhs", "rows"),
    )
    out_specs = (P("rhs", ("groups", "rows", "cols")), P("rhs", ("groups", "rows", "cols")))
    return jax.shard_map(
        per_device, mesh=mesh, in_specs=in_specs, out_specs=out_specs, check_vma=False
    )
```

profile of v0, /device:TPU:0, one launch (start us, length us, event | category | flops | bytes accessed | tf_op | source)
XLA Modules:
  0.0 122.6 jit_solution(12828520094219425753)
XLA Ops:
  2.4 1.3 %broadcast_subtract_fusion = (s32[512]{0:T(512)}, s32[512]{0:T(512)}) fusion(s32[512]{0:T(512)} %param.14, s32[]{:T(128)S(6)} %mul.77, s32[512]{0:T(512)} %param.13), kind=kLoop, calls=%fused_computation.13 | loop fusion | flops 1024 | bytes 8196 | tf_op jit(solution)/shard_map/sub | solution.py:344
  6.8 5.4 %right.1 = (f32[16,4096]{1,0:T(8,128)S(1)}, f32[16,16]{1,0:T(8,128)S(1)}, bf16[512,8704]{1,0:T(8,128)(2,1)S(1)}) custom-call(s32[7]{0:T(128)S(1)} %stack.31.scalars, f32[5,8]{1,0:T(8,128)S(1)} %copy-done.8, f32[5,8]{1,0:T(8,128)S(1)} %collective-permute-done.pitch_other, s32[1,8]{1,0:T(1,128)S(1)} %bitcast.15, ...), custom_call_target="tpu_custom_call" | custom-call | bytes 8912896 | tf_op jit(solution)/shard_map/right/pallas_call | solution.py:353
  12.2 2.7 %collective-permute-start.3 = (f32[16,16]{1,0:T(8,128)S(1)}, f32[16,16]{1,0:T(8,128)S(1)}, u32[]{:S(2)}, u32[]{:S(2)}) collective-permute-start(f32[16,16]{1,0:T(8,128)S(1)} %get-tuple-element.20.rest_0_), channel_id=1, source_target_pairs={{0,4},{4,0},{8,12},{12,8},{1,5},{5,1},{9,13},{13,9},{2,6},{6,2},{1... | collective-permute-start | bytes 3080 | tf_op jit(solution)/shard_map/ppermute | solution.py:371
  14.9 2.6 %collective-permute-start.4 = (f32[16,16]{1,0:T(8,128)S(1)}, f32[16,16]{1,0:T(8,128)S(1)}, u32[]{:S(2)}, u32[]{:S(2)}) collective-permute-start(f32[16,16]{1,0:T(8,128)S(1)} %get-tuple-element.20.rest_0_), channel_id=1, source_target_pairs={{0,8},{4,12},{8,0},{12,4},{1,9},{5,13},{9,1},{13,5},{2,10},{6,14},... | collective-permute-start | bytes 3080 | tf_op jit(solution)/shard_map/ppermute | solution.py:371
  18.9 12.6 %adjoint_one.1 = (f32[16,4096]{1,0:T(8,128)}, f32[16,4096]{1,0:T(8,128)}, f32[16,2048]{1,0:T(8,128)}, f32[16,2048]{1,0:T(8,128)}, f32[1,2048]{1,0:T(1,128)}, /*index=5*/bf16[1536,8704]{1,0:T(8,128)(2,1)S(1)}) custom-call(s32[7]{0:T(128)} %copy-done.4, f32[8,4096]{1,0:T(8,128)} %objectives.1, f32[8,4096]{1,0:T(8,128)} %copy-done.13, f32[1,4096]{1,0:T(1,128)} %bitcast.24, ...), custom_call_target="tpu_custom_call" | custom-call | flops 570425344 | bytes 26738688 | tf_op jit(solution)/shard_map/adjoint_one/pallas_call | solution.py:375
  31.4 2.3 %collective-permute-start.19 = (f32[16,4096]{1,0:T(8,128)}, f32[16,4096]{1,0:T(8,128)S(1)}, u32[]{:S(2)}, u32[]{:S(2)}) collective-permute-start(f32[16,4096]{1,0:T(8,128)} %get-tuple-element.32), channel_id=1, source_target_pairs={{0,1},{1,0},{2,3},{3,2},{4,5},{5,4},{6,7},{7,6},{8,9},{9,8},{10,11... | collective-permute-start | bytes 786440 | tf_op jit(solution)/shard_map/ppermute | solution.py:325
  34.5 2.1 %start.1 = (bf16[16,4096]{1,0:T(8,128)(2,1)S(1)}, f32[16,2048]{1,0:T(8,128)S(1)}, f32[16,2048]{1,0:T(8,128)S(1)}) custom-call(s32[7]{0:T(128)S(1)} %copy-done.5, f32[16,4096]{1,0:T(8,128)S(1)} %collective-permute-done.2.right_piece, f32[16,4096]{1,0:T(8,128)S(1)} %get-tuple-element.19.right, f32[16,16]{1,0:T(8,128)S(1)} %get-tuple-element.20.rest_0_, ...), custom_call_target="tpu_custom_call" | custom-call | tf_op jit(solution)/shard_map/start/pallas_call | solution.py:413
  38.4 6.3 %collective-permute-start.22 = (bf16[16,2048]{1,0:T(8,128)(2,1)S(1)}, bf16[16,2048]{1,0:T(8,128)(2,1)S(1)}, u32[]{:S(2)}, u32[]{:S(2)}) collective-permute-start(bf16[16,2048]{1,0:T(8,128)(2,1)S(1)} %get-tuple-element.43), channel_id=1, source_target_pairs={{0,2},{1,6},{2,10},{3,14},{4,3},{5,7},{6,11},{7,15},{8,0},{9,4},{1... | collective-permute-start | bytes 196616 | tf_op jit(solution)/shard_map/ppermute | solution.py:431
  44.7 2.0 %collective-permute-start.23 = (bf16[16,2048]{1,0:T(8,128)(2,1)S(1)}, bf16[16,2048]{1,0:T(8,128)(2,1)S(1)}, u32[]{:S(2)}, u32[]{:S(2)}) collective-permute-start(bf16[16,2048]{1,0:T(8,128)(2,1)S(1)} %get-tuple-element.42), channel_id=1, source_target_pairs={{0,3},{1,7},{2,11},{3,15},{4,2},{5,6},{6,10},{7,14},{8,1},{9,5},{1... | collective-permute-start | bytes 196616 | tf_op jit(solution)/shard_map/ppermute | solution.py:431
  47.3 11.4 %forward_one.1 = f32[16,2048]{1,0:T(8,128)} custom-call(s32[7]{0:T(128)} %copy-done.4, s32[1,512]{1,0:T(1,128)} %bitcast.21, s32[1,512]{1,0:T(1,128)} %bitcast.17, bf16[512,8704]{1,0:T(8,128)(2,1)S(1)} %get-tuple-element.22.held_first, bf16[1536,8704]{1,0:T(8,128)(2,1)S(1)} %get-tuple-element.23.held, bf16[16,4096]{1,0:T(8,128)(2,1)} %copy-done.2, ...), custom_call_target="tpu_custom_call" | custom-call | flops 570425344 | bytes 35651584 | tf_op jit(solution)/shard_map/forward_one/pallas_call | solution.py:402
  58.8 2.5 %collective-permute-start.8 = (f32[16,2048]{1,0:T(8,128)}, f32[16,2048]{1,0:T(8,128)S(1)}, u32[]{:S(2)}, u32[]{:S(2)}) collective-permute-start(f32[16,2048]{1,0:T(8,128)} %forward_one.1), channel_id=1, source_target_pairs={{0,2},{2,0},{1,3},{3,1},{4,6},{6,4},{5,7},{7,5},{8,10},{10,8},{9,1... | collective-permute-start | bytes 393224 | tf_op jit(solution)/shard_map/ppermute | solution.py:328
  62.0 7.9 %adjoint_two.1 = (f32[16,4096]{1,0:T(8,128)}, f32[16,4096]{1,0:T(8,128)}, f32[16,2048]{1,0:T(8,128)}) custom-call(s32[7]{0:T(128)} %copy-done.4, f32[16,2048]{1,0:T(8,128)} %get-tuple-element.29.previous, f32[16,2048]{1,0:T(8,128)} %get-tuple-element.30.target, f32[1,2048]{1,0:T(1,128)} %get-tuple-element.25.self_half, s32[1,512]{1,0:T(1,128)} %bitcast.22, ...), custom_call_target="tpu_custom_call" | custom-call | flops 570425344 | bytes 35651584 | tf_op jit(solution)/shard_map/adjoint_two/pallas_call | solution.py:436
  70.9 5.1 %collective-permute-start.11 = (bf16[16,2048]{1,0:T(8,128)(2,1)S(1)}, bf16[16,2048]{1,0:T(8,128)(2,1)S(1)}, u32[]{:S(2)}, u32[]{:S(2)}) collective-permute-start(bf16[16,2048]{1,0:T(8,128)(2,1)S(1)} %get-tuple-element.36), channel_id=1, source_target_pairs={{0,8},{1,0},{2,12},{3,4},{4,9},{5,1},{6,13},{7,5},{8,10},{9,2},{10... | collective-permute-start | bytes 196616 | tf_op jit(solution)/shard_map/ppermute | solution.py:451
  79.8 11.4 %forward_two.1.rest_0_ = f32[16,2048]{1,0:T(8,128)} custom-call(s32[7]{0:T(128)} %copy-done.4, s32[1,512]{1,0:T(1,128)} %bitcast.23, s32[1,512]{1,0:T(1,128)} %bitcast.19, bf16[512,8704]{1,0:T(8,128)(2,1)S(1)} %get-tuple-element.22.held_first, bf16[1536,8704]{1,0:T(8,128)(2,1)S(1)} %get-tuple-element.23.held, bf16[16,2048]{1,0:T(8,128)(2,1)} %copy-done.19, ...), custom_call_target="tpu_custom_call" | custom-call | flops 570425344 | bytes 35651584 | tf_op jit(solution)/shard_map/forward_two/pallas_call | solution.py:402
  91.2 3.6 %collective-permute-start.14 = (f32[16,2048]{1,0:T(8,128)}, f32[16,2048]{1,0:T(8,128)S(1)}, u32[]{:S(2)}, u32[]{:S(2)}) collective-permute-start(f32[16,2048]{1,0:T(8,128)} %forward_two.1.rest_0_), channel_id=1, source_target_pairs={{0,2},{2,0},{1,3},{3,1},{4,6},{6,4},{5,7},{7,5},{8,10},{10,8},{9,1... | collective-permute-start | bytes 393224 | tf_op jit(solution)/shard_map/ppermute | solution.py:328
  95.0 4.0 %collective-permute-done.14.rest_1_ = f32[16,2048]{1,0:T(8,128)S(1)} collective-permute-done((f32[16,2048]{1,0:T(8,128)}, f32[16,2048]{1,0:T(8,128)S(1)}, u32[]{:S(2)}, u32[]{:S(2)}) %collective-permute-start.14) | collective-permute-done | bytes 131104 | tf_op jit(solution)/shard_map/ppermute | solution.py:328
  99.9 1.4 %system.1 = (f32[16,128]{1,0:T(8,128)S(1)}, f32[16,128]{1,0:T(8,128)S(1)}) custom-call(s32[7]{0:T(128)S(1)} %copy-done.6, f32[16,2048]{1,0:T(8,128)S(1)} %get-tuple-element.21.basis, f32[16,2048]{1,0:T(8,128)S(1)} %get-tuple-element.37.image, f32[16,2048]{1,0:T(8,128)S(1)} %get-tuple-element.26.right, f32[1,2048]{1,0:T(1,128)S(1)} %copy-done.3, ...), custom_call_target="tpu_custom_call" | custom-call | tf_op jit(solution)/shard_map/system/pallas_call | solution.py:456
  102.1 1.8 %collective-permute-start.27 = (f32[8,2048]{1,0:T(8,128)S(1)}, f32[8,2048]{1,0:T(8,128)S(1)}, u32[]{:S(2)}, u32[]{:S(2)}) collective-permute-start(f32[8,2048]{1,0:T(8,128)S(1)} %get-tuple-element.41), channel_id=1, source_target_pairs={{0,1},{1,5},{2,9},{3,13},{4,0},{5,4},{6,8},{7,12},{8,3},{9,7},{10,... | collective-permute-start | bytes 196616 | tf_op jit(solution)/shard_map/ppermute | solution.py:502
  103.9 2.3 %collective-permute-start.28 = (f32[8,2048]{1,0:T(8,128)S(1)}, f32[8,2048]{1,0:T(8,128)S(1)}, u32[]{:S(2)}, u32[]{:S(2)}) collective-permute-start(f32[8,2048]{1,0:T(8,128)S(1)} %get-tuple-element.40), channel_id=1, source_target_pairs={{0,2},{1,6},{2,10},{3,14},{4,3},{5,7},{6,11},{7,15},{8,0},{9,4},{1... | collective-permute-start | bytes 196616 | tf_op jit(solution)/shard_map/ppermute | solution.py:502
  106.2 2.2 %collective-permute-start.29 = (f32[8,2048]{1,0:T(8,128)S(1)}, f32[8,2048]{1,0:T(8,128)S(1)}, u32[]{:S(2)}, u32[]{:S(2)}) collective-permute-start(f32[8,2048]{1,0:T(8,128)S(1)} %get-tuple-element.39), channel_id=1, source_target_pairs={{0,3},{1,7},{2,11},{3,15},{4,2},{5,6},{6,10},{7,14},{8,1},{9,5},{1... | collective-permute-start | bytes 196616 | tf_op jit(solution)/shard_map/ppermute | solution.py:502
  108.5 1.5 %collective-permute-start.16 = (f32[16,128]{1,0:T(8,128)S(1)}, f32[16,128]{1,0:T(8,128)S(1)}, u32[]{:S(2)}, u32[]{:S(2)}) collective-permute-start(f32[16,128]{1,0:T(8,128)S(1)} %add.112.rest_0_), channel_id=1, source_target_pairs={{0,4},{4,0},{8,12},{12,8},{1,5},{5,1},{9,13},{13,9},{2,6},{6,2},{1... | collective-permute-start | bytes 24584 | tf_op jit(solution)/shard_map/ppermute | solution.py:465
  109.9 1.9 %collective-permute-start.17 = (f32[16,128]{1,0:T(8,128)S(1)}, f32[16,128]{1,0:T(8,128)S(1)}, u32[]{:S(2)}, u32[]{:S(2)}) collective-permute-start(f32[16,128]{1,0:T(8,128)S(1)} %add.112.rest_0_), channel_id=1, source_target_pairs={{0,8},{4,12},{8,0},{12,4},{1,9},{5,13},{9,1},{13,5},{2,10},{6,14},... | collective-permute-start | bytes 24584 | tf_op jit(solution)/shard_map/ppermute | solution.py:465
  111.8 6.9 %collective-permute-start.18 = (f32[16,128]{1,0:T(8,128)S(1)}, f32[16,128]{1,0:T(8,128)S(1)}, u32[]{:S(2)}, u32[]{:S(2)}) collective-permute-start(f32[16,128]{1,0:T(8,128)S(1)} %add.112.rest_0_), channel_id=1, source_target_pairs={{0,12},{4,8},{8,4},{12,0},{1,13},{5,9},{9,5},{13,1},{2,14},{6,10},... | collective-permute-start | bytes 24584 | tf_op jit(solution)/shard_map/ppermute | solution.py:465
  120.4 2.3 %solve.1 = f32[8,2048]{1,0:T(8,128)} custom-call(f32[16,2048]{1,0:T(8,128)S(1)} %maximum_select_fusion.basis, f32[16,128]{1,0:T(8,128)S(1)} %add.112.rest_0_, f32[16,128]{1,0:T(8,128)S(1)} %collective-permute-done.16.rest_1_, f32[16,128]{1,0:T(8,128)S(1)} %collective-permute-done.17.rest_2_, f32[16,128]{1,0:T(8,128)S(1)} %collective-permute-done.18.rest_3_), custom_call_target="tpu_custom_call" | custom-call | tf_op jit(solution)/shard_map/solve/pallas_call | solution.py:482
  (108 shorter events, 18.0 us)
Async XLA Ops:
  1.2 17.0 %collective-permute-start.6 = (f32[8,4096]{1,0:T(8,128)}, f32[8,4096]{1,0:T(8,128)S(1)}, u32[]{:S(2)}, u32[]{:S(2)}) collective-permute-start(f32[8,4096]{1,0:T(8,128)} %objectives.1), channel_id=1, source_target_pairs={{0,1},{1,0},{2,3},{3,2},{4,5},{5,4},{6,7},{7,6},{8,9},{9,8},{10,11... | collective-permute-start | bytes 393224 | tf_op jit(solution)/shard_map/ppermute | solution.py:325
  12.2 22.2 %collective-permute-start.3 = (f32[16,16]{1,0:T(8,128)S(1)}, f32[16,16]{1,0:T(8,128)S(1)}, u32[]{:S(2)}, u32[]{:S(2)}) collective-permute-start(f32[16,16]{1,0:T(8,128)S(1)} %get-tuple-element.20.rest_0_), channel_id=1, source_target_pairs={{0,4},{4,0},{8,12},{12,8},{1,5},{5,1},{9,13},{13,9},{2,6},{6,2},{1... | collective-permute-start | bytes 3080 | tf_op jit(solution)/shard_map/ppermute | solution.py:371
  14.9 19.5 %collective-permute-start.4 = (f32[16,16]{1,0:T(8,128)S(1)}, f32[16,16]{1,0:T(8,128)S(1)}, u32[]{:S(2)}, u32[]{:S(2)}) collective-permute-start(f32[16,16]{1,0:T(8,128)S(1)} %get-tuple-element.20.rest_0_), channel_id=1, source_target_pairs={{0,8},{4,12},{8,0},{12,4},{1,9},{5,13},{9,1},{13,5},{2,10},{6,14},... | collective-permute-start | bytes 3080 | tf_op jit(solution)/shard_map/ppermute | solution.py:371
  17.5 16.9 %collective-permute-start.5 = (f32[16,16]{1,0:T(8,128)S(1)}, f32[16,16]{1,0:T(8,128)S(1)}, u32[]{:S(2)}, u32[]{:S(2)}) collective-permute-start(f32[16,16]{1,0:T(8,128)S(1)} %get-tuple-element.20.rest_0_), channel_id=1, source_target_pairs={{0,12},{4,8},{8,4},{12,0},{1,13},{5,9},{9,5},{13,1},{2,14},{6,10},... | collective-permute-start | bytes 3080 | tf_op jit(solution)/shard_map/ppermute | solution.py:371
  17.5 17.0 %collective-permute-start.2 = (f32[16,4096]{1,0:T(8,128)S(1)}, f32[16,4096]{1,0:T(8,128)S(1)}, u32[]{:S(2)}, u32[]{:S(2)}) collective-permute-start(f32[16,4096]{1,0:T(8,128)S(1)} %get-tuple-element.19.right), channel_id=1, source_target_pairs={{0,0},{1,4},{2,8},{3,12},{4,1},{5,5},{6,9},{7,13},{8,2},{9,6},{10,... | collective-permute-start | bytes 786440 | tf_op jit(solution)/shard_map/ppermute | solution.py:370
  36.6 10.0 %collective-permute-start.7 = (bf16[16,4096]{1,0:T(8,128)(2,1)S(1)}, bf16[16,4096]{1,0:T(8,128)(2,1)S(1)}, u32[]{:S(2)}, u32[]{:S(2)}) collective-permute-start(bf16[16,4096]{1,0:T(8,128)(2,1)S(1)} %get-tuple-element.24.rest_0_), channel_id=1, source_target_pairs={{0,1},{1,0},{2,3},{3,2},{4,5},{5,4},{6,7},{7,6},{8,9},{9,8},{10,11... | collective-permute-start | bytes 393224 | tf_op jit(solution)/shard_map/ppermute | solution.py:325
  37.7 23.6 %collective-permute-start.20 = (bf16[16,2048]{1,0:T(8,128)(2,1)S(1)}, bf16[16,2048]{1,0:T(8,128)(2,1)S(1)}, u32[]{:S(2)}, u32[]{:S(2)}) collective-permute-start(bf16[16,2048]{1,0:T(8,128)(2,1)S(1)} %get-tuple-element.43), channel_id=1, source_target_pairs={{0,0},{1,4},{2,8},{3,12},{4,1},{5,5},{6,9},{7,13},{8,2},{9,6},{10,... | collective-permute-start | bytes 196616 | tf_op jit(solution)/shard_map/ppermute | solution.py:431
  38.4 22.9 %collective-permute-start.22 = (bf16[16,2048]{1,0:T(8,128)(2,1)S(1)}, bf16[16,2048]{1,0:T(8,128)(2,1)S(1)}, u32[]{:S(2)}, u32[]{:S(2)}) collective-permute-start(bf16[16,2048]{1,0:T(8,128)(2,1)S(1)} %get-tuple-element.43), channel_id=1, source_target_pairs={{0,2},{1,6},{2,10},{3,14},{4,3},{5,7},{6,11},{7,15},{8,0},{9,4},{1... | collective-permute-start | bytes 196616 | tf_op jit(solution)/shard_map/ppermute | solution.py:431
  44.7 16.6 %collective-permute-start.21 = (bf16[16,2048]{1,0:T(8,128)(2,1)S(1)}, bf16[16,2048]{1,0:T(8,128)(2,1)S(1)}, u32[]{:S(2)}, u32[]{:S(2)}) collective-permute-start(bf16[16,2048]{1,0:T(8,128)(2,1)S(1)} %get-tuple-element.42), channel_id=1, source_target_pairs={{0,1},{1,5},{2,9},{3,13},{4,0},{5,4},{6,8},{7,12},{8,3},{9,7},{10,... | collective-permute-start | bytes 196616 | tf_op jit(solution)/shard_map/ppermute | solution.py:431
  44.7 16.7 %collective-permute-start.23 = (bf16[16,2048]{1,0:T(8,128)(2,1)S(1)}, bf16[16,2048]{1,0:T(8,128)(2,1)S(1)}, u32[]{:S(2)}, u32[]{:S(2)}) collective-permute-start(bf16[16,2048]{1,0:T(8,128)(2,1)S(1)} %get-tuple-element.42), channel_id=1, source_target_pairs={{0,3},{1,7},{2,11},{3,15},{4,2},{5,6},{6,10},{7,14},{8,1},{9,5},{1... | collective-permute-start | bytes 196616 | tf_op jit(solution)/shard_map/ppermute | solution.py:431
  58.8 11.2 %collective-permute-start.8 = (f32[16,2048]{1,0:T(8,128)}, f32[16,2048]{1,0:T(8,128)S(1)}, u32[]{:S(2)}, u32[]{:S(2)}) collective-permute-start(f32[16,2048]{1,0:T(8,128)} %forward_one.1), channel_id=1, source_target_pairs={{0,2},{2,0},{1,3},{3,1},{4,6},{6,4},{5,7},{7,5},{8,10},{10,8},{9,1... | collective-permute-start | bytes 393224 | tf_op jit(solution)/shard_map/ppermute | solution.py:328
  69.9 25.0 %collective-permute-start.25 = (f32[16,4096]{1,0:T(8,128)}, f32[16,4096]{1,0:T(8,128)S(1)}, u32[]{:S(2)}, u32[]{:S(2)}) collective-permute-start(f32[16,4096]{1,0:T(8,128)} %get-tuple-element.35), channel_id=1, source_target_pairs={{0,1},{1,0},{2,3},{3,2},{4,5},{5,4},{6,7},{7,6},{8,9},{9,8},{10,11... | collective-permute-start | bytes 786440 | tf_op jit(solution)/shard_map/ppermute | solution.py:325
  70.1 6.7 %collective-permute-start.10 = (bf16[16,2048]{1,0:T(8,128)(2,1)S(1)}, bf16[16,2048]{1,0:T(8,128)(2,1)S(1)}, u32[]{:S(2)}, u32[]{:S(2)}) collective-permute-start(bf16[16,2048]{1,0:T(8,128)(2,1)S(1)} %get-tuple-element.36), channel_id=1, source_target_pairs={{0,0},{1,8},{2,4},{3,12},{4,1},{5,9},{6,5},{7,13},{8,2},{9,10},{10... | collective-permute-start | bytes 196616 | tf_op jit(solution)/shard_map/ppermute | solution.py:451
  70.9 7.0 %collective-permute-start.11 = (bf16[16,2048]{1,0:T(8,128)(2,1)S(1)}, bf16[16,2048]{1,0:T(8,128)(2,1)S(1)}, u32[]{:S(2)}, u32[]{:S(2)}) collective-permute-start(bf16[16,2048]{1,0:T(8,128)(2,1)S(1)} %get-tuple-element.36), channel_id=1, source_target_pairs={{0,8},{1,0},{2,12},{3,4},{4,9},{5,1},{6,13},{7,5},{8,10},{9,2},{10... | collective-permute-start | bytes 196616 | tf_op jit(solution)/shard_map/ppermute | solution.py:451
  76.8 31.7 %collective-permute-start.24 = (f32[8,2048]{1,0:T(8,128)S(1)}, f32[8,2048]{1,0:T(8,128)S(1)}, u32[]{:S(2)}, u32[]{:S(2)}) collective-permute-start(f32[8,2048]{1,0:T(8,128)S(1)} %constant_dynamic-slice_fusion), channel_id=1, source_target_pairs={{0,1},{1,0},{2,3},{3,2},{4,5},{5,4},{6,7},{7,6},{8,9},{9,8},{10,11... | collective-permute-start | bytes 196616 | tf_op jit(solution)/shard_map/ppermute | solution.py:325
  91.2 7.8 %collective-permute-start.14 = (f32[16,2048]{1,0:T(8,128)}, f32[16,2048]{1,0:T(8,128)S(1)}, u32[]{:S(2)}, u32[]{:S(2)}) collective-permute-start(f32[16,2048]{1,0:T(8,128)} %forward_two.1.rest_0_), channel_id=1, source_target_pairs={{0,2},{2,0},{1,3},{3,1},{4,6},{6,4},{5,7},{7,5},{8,10},{10,8},{9,1... | collective-permute-start | bytes 393224 | tf_op jit(solution)/shard_map/ppermute | solution.py:328
  94.8 9.1 %collective-permute-start.9 = (f32[16,2048]{1,0:T(8,128)S(1)}, f32[16,2048]{1,0:T(8,128)S(1)}, u32[]{:S(2)}, u32[]{:S(2)}) collective-permute-start(f32[16,2048]{1,0:T(8,128)S(1)} %pad_maximum_fusion), channel_id=1, source_target_pairs={{0,1},{1,0},{2,3},{3,2},{4,5},{5,4},{6,7},{7,6},{8,9},{9,8},{10,11... | collective-permute-start | bytes 393224 | tf_op jit(solution)/shard_map/ppermute | solution.py:325
  101.4 8.5 %collective-permute-start.26 = (f32[8,2048]{1,0:T(8,128)S(1)}, f32[8,2048]{1,0:T(8,128)S(1)}, u32[]{:S(2)}, u32[]{:S(2)}) collective-permute-start(f32[8,2048]{1,0:T(8,128)S(1)} %get-tuple-element.38), channel_id=1, source_target_pairs={{0,0},{1,4},{2,8},{3,12},{4,1},{5,5},{6,9},{7,13},{8,2},{9,6},{10,... | collective-permute-start | bytes 196616 | tf_op jit(solution)/shard_map/ppermute | solution.py:502
  102.1 9.7 %collective-permute-start.27 = (f32[8,2048]{1,0:T(8,128)S(1)}, f32[8,2048]{1,0:T(8,128)S(1)}, u32[]{:S(2)}, u32[]{:S(2)}) collective-permute-start(f32[8,2048]{1,0:T(8,128)S(1)} %get-tuple-element.41), channel_id=1, source_target_pairs={{0,1},{1,5},{2,9},{3,13},{4,0},{5,4},{6,8},{7,12},{8,3},{9,7},{10,... | collective-permute-start | bytes 196616 | tf_op jit(solution)/shard_map/ppermute | solution.py:502
  103.9 14.8 %collective-permute-start.28 = (f32[8,2048]{1,0:T(8,128)S(1)}, f32[8,2048]{1,0:T(8,128)S(1)}, u32[]{:S(2)}, u32[]{:S(2)}) collective-permute-start(f32[8,2048]{1,0:T(8,128)S(1)} %get-tuple-element.40), channel_id=1, source_target_pairs={{0,2},{1,6},{2,10},{3,14},{4,3},{5,7},{6,11},{7,15},{8,0},{9,4},{1... | collective-permute-start | bytes 196616 | tf_op jit(solution)/shard_map/ppermute | solution.py:502
  106.2 12.6 %collective-permute-start.29 = (f32[8,2048]{1,0:T(8,128)S(1)}, f32[8,2048]{1,0:T(8,128)S(1)}, u32[]{:S(2)}, u32[]{:S(2)}) collective-permute-start(f32[8,2048]{1,0:T(8,128)S(1)} %get-tuple-element.39), channel_id=1, source_target_pairs={{0,3},{1,7},{2,11},{3,15},{4,2},{5,6},{6,10},{7,14},{8,1},{9,5},{1... | collective-permute-start | bytes 196616 | tf_op jit(solution)/shard_map/ppermute | solution.py:502
  108.5 11.0 %collective-permute-start.16 = (f32[16,128]{1,0:T(8,128)S(1)}, f32[16,128]{1,0:T(8,128)S(1)}, u32[]{:S(2)}, u32[]{:S(2)}) collective-permute-start(f32[16,128]{1,0:T(8,128)S(1)} %add.112.rest_0_), channel_id=1, source_target_pairs={{0,4},{4,0},{8,12},{12,8},{1,5},{5,1},{9,13},{13,9},{2,6},{6,2},{1... | collective-permute-start | bytes 24584 | tf_op jit(solution)/shard_map/ppermute | solution.py:465
  109.9 9.5 %collective-permute-start.17 = (f32[16,128]{1,0:T(8,128)S(1)}, f32[16,128]{1,0:T(8,128)S(1)}, u32[]{:S(2)}, u32[]{:S(2)}) collective-permute-start(f32[16,128]{1,0:T(8,128)S(1)} %add.112.rest_0_), channel_id=1, source_target_pairs={{0,8},{4,12},{8,0},{12,4},{1,9},{5,13},{9,1},{13,5},{2,10},{6,14},... | collective-permute-start | bytes 24584 | tf_op jit(solution)/shard_map/ppermute | solution.py:465
  111.8 8.5 %collective-permute-start.18 = (f32[16,128]{1,0:T(8,128)S(1)}, f32[16,128]{1,0:T(8,128)S(1)}, u32[]{:S(2)}, u32[]{:S(2)}) collective-permute-start(f32[16,128]{1,0:T(8,128)S(1)} %add.112.rest_0_), channel_id=1, source_target_pairs={{0,12},{4,8},{8,4},{12,0},{1,13},{5,9},{9,5},{13,1},{2,14},{6,10},... | collective-permute-start | bytes 24584 | tf_op jit(solution)/shard_map/ppermute | solution.py:465
  (30 other events, 257.6 us)
where the time goes:
time: 123 us
  Pallas kernels  54.6 us (44%)
  starting transfers between devices  48.2 us (39%)
  local copies, waits for them, and re-layouts  8.18 us (7%)
  waiting for transfers between devices  6.81 us (6%)
  other arithmetic  3.8 us (3%)
    pallas_call x2, Pallas kernels, forward(): pl.pallas_call(functools.partial(forward_kernel, 512, places), in_specs=[...  22.9 us
    pallas_call x1, Pallas kernels, per_device(): pl.pallas_call(functools.partial(load_adjoint_kernel, chunk), in_specs=[S...  12.6 us
    ppermute x3, starting transfers between devices, per_device(): lax.ppermute(system, 'rows', flip(k, n_rows))  10.2 us
    ppermute x4, starting transfers between devices, per_device(): parts = [lax.ppermute(sends[k % 2], GRID, cross(k)) for k in range(side)]  8.95 us
    pallas_call x1, Pallas kernels, per_device(): pl.pallas_call(functools.partial(adjoint_kernel, 512, len(parts)), in_spe...  7.91 us
    ppermute x4, starting transfers between devices, per_device(): image = image + lax.ppermute(part, GRID, cross(k))  7 us
    unnamed x48, local copies, waits for them, and re-layouts  6.5 us
    ppermute x2, starting transfers between devices, cols_parts(): lax.ppermute(value, 'cols', flip(k, n_cols))  6.09 us
  transfers between devices with their start and end apart: 30, of which 5 were waited for; matrix products, arithmetic and copies ran while one was open for 4% of the time, Pallas kernels for 43%

commit v1 on v0

v1 whole, which is shorter than its diff:
```python
import functools

import jax
import jax.numpy as jnp
from jax import lax
from jax.experimental import pallas as pl
from jax.experimental.pallas import tpu as pltpu
from jax.sharding import PartitionSpec as P

BLOCK = 8
LANES = 128
SHIFT = 3.0
GRID = ("rows", "cols", "rhs")
F32 = jnp.float32
BF16 = jnp.bfloat16

VMEM = pl.BlockSpec(memory_space=pltpu.VMEM)
SMEM = pl.BlockSpec(memory_space=pltpu.SMEM)
ANY = pl.BlockSpec(memory_space=pl.ANY)

CORE, COLUMNS, ROW, BEGIN, HOLDER, SPAN, CHUNKS = range(7)


def dot(left, right, dims):
    return lax.dot_general(left, right, (dims, ((), ())), preferred_element_type=F32)


def precise(left, right, dims):
    return lax.dot_general(
        left, right, (dims, ((), ())), precision=lax.Precision.HIGHEST, preferred_element_type=F32
    )


def low_onehot(index):
    low = jnp.bitwise_and(index, LANES - 1)
    hit = lax.broadcasted_iota(jnp.int32, (LANES, index.shape[1]), 0) == low
    return jnp.where(hit, 1.0, 0.0).astype(BF16)


def take_columns(field, index):
    rows, width = field.shape
    chunks = width // LANES
    stacked = jnp.concatenate(
        [field[:, i * LANES : (i + 1) * LANES] for i in range(chunks)], axis=0
    )
    picked = dot(stacked, low_onehot(index), ((1,), (0,)))
    high = jnp.right_shift(index, 7)
    total = jnp.zeros((rows, index.shape[1]), F32)
    for i in range(chunks):
        total = total + jnp.where(high == i, picked[i * rows : (i + 1) * rows], 0.0)
    return total


def put_columns(values, index, width):
    rows = values.shape[0]
    chunks = width // LANES
    high = jnp.right_shift(index, 7)
    stacked = jnp.concatenate(
        [jnp.where(high == i, values, 0.0).astype(BF16) for i in range(chunks)], axis=0
    )
    spread = dot(stacked, low_onehot(index), ((1,), (1,)))
    return jnp.concatenate([spread[i * rows : (i + 1) * rows] for i in range(chunks)], axis=1)


def both_cores(core, own, other):
    first = jnp.where(core == 0, own, other)
    second = jnp.where(core == 0, other, own)
    return jnp.concatenate([first, second], axis=0)


def load_copies(influence, wake, held, sems, first, chunk):
    def copies(i):
        source = pl.ds(pl.multiple_of(first + i * chunk, 16), chunk)
        target = pl.ds(i * chunk, chunk)
        panels = influence.shape[1]
        return (
            pltpu.make_async_copy(
                influence.at[source], held.at[target, pl.ds(0, panels)], sems.at[0, i]
            ),
            pltpu.make_async_copy(
                wake.at[source], held.at[target, pl.ds(panels, wake.shape[1])], sems.at[1, i]
            ),
        )

    return copies


def right_kernel(
    half, scalars, pitch, pitch_other, modes, modes_other, blade, shapes, right, right_half
):
    core = scalars[CORE]
    blades = pitch.shape[0]
    blade_onehot = jnp.where(
        lax.broadcasted_iota(jnp.int32, (blades, blade.shape[1]), 0) == blade[...], 1.0, 0.0
    )
    for b in range(2):
        own = core == b
        amount = jnp.where(own, pitch[...], pitch_other[...])
        mode = jnp.where(own, modes[...], modes_other[...])
        mode_onehot = jnp.where(
            lax.broadcasted_iota(jnp.int32, (shapes.shape[0], BLOCK), 0) == mode, 1.0, 0.0
        )
        pattern = precise(mode_onehot, shapes[...], ((0,), (0,)))
        factor = precise(amount, blade_onehot, ((0,), (0,)))
        right[b * BLOCK : (b + 1) * BLOCK, :] = pattern * factor
    right_half[...] = right[:, pl.ds(pl.multiple_of(core * half, LANES), half)]


def local_wake(scalars, upper, lower):
    start = scalars[COLUMNS]
    return upper[...] - start, lower[...] - start


def load_first_kernel(
    chunk, steps, scalars, objectives, objectives_other, self_term, influence, wake,
    start, target, self_half, whole, held, sems
):
    half = start.shape[1]
    core = scalars[CORE]
    copies = load_copies(influence, wake, held, sems, core * half, chunk)
    for i in range(steps):
        for copy in copies(i):
            copy.start()
    span = pl.ds(pl.multiple_of(core * half, LANES), half)
    target[...] = both_cores(core, objectives[:, span], objectives_other[:, span])
    self_half[...] = self_term[:, span]
    start[...] = target[...] / self_half[...]
    for i in range(steps):
        for copy in copies(i):
            copy.wait()
        rows = slice(i * chunk, (i + 1) * chunk)
        part = dot(start[:, rows].astype(BF16), held[rows, :], ((1,), (0,)))
        if i == 0:
            whole[...] = part
        else:
            whole[...] += part


def load_rest_kernel(
    chunk, steps, scalars, start, upper, lower, whole_first, influence, wake, held_first,
    keep, give, held, whole, sems
):
    half = start.shape[1]
    piece = keep.shape[1]
    panels = 2 * piece
    core = scalars[CORE]
    copies = load_copies(influence, wake, held, sems, core * half, chunk)
    for i in range(*steps):
        for copy in copies(i):
            copy.start()
    whole[...] = whole_first[...]
    for i in range(*steps):
        for copy in copies(i):
            copy.wait()
        rows = slice(i * chunk, (i + 1) * chunk)
        whole[...] += dot(start[:, rows].astype(BF16), held[rows, :], ((1,), (0,)))
    upper_local, lower_local = local_wake(scalars, upper, lower)
    carried = whole[:, panels:]
    whole[:, 0:panels] += put_columns(carried, upper_local, panels) - put_columns(
        carried, lower_local, panels
    )
    keep[...] = whole[:, pl.ds(pl.multiple_of(core * piece, LANES), piece)]
    give[...] = whole[:, pl.ds(pl.multiple_of((1 - core) * piece, LANES), piece)]


def adjoint_piece(tile, scalars, field, which, carried, upper, lower, held, out):
    width = out.shape[1]
    piece = out.shape[0] // (2 * BLOCK) * width
    begin = which * piece
    upper_local, lower_local = local_wake(scalars, upper, lower)
    spread = put_columns(carried, upper_local - begin, piece) - put_columns(
        carried, lower_local - begin, piece
    )
    for start in range(0, piece, tile):
        span = pl.ds(pl.multiple_of(begin + start, LANES), tile)
        part = (
            dot(field, held[:, span], ((1,), (0,)))
            + spread[:, start : start + tile]
        )
        col, offset = divmod(start, width)
        for b in range(2):
            goal = (col * 2 + b) * BLOCK
            out[goal : goal + BLOCK, offset : offset + tile] = part[b * BLOCK : (b + 1) * BLOCK]


def adjoint_give_kernel(
    tile, n_in, scalars, previous, target, self_half, upper, lower, held, *rest
):
    parts, (give, adjoint, carried, mine, send) = rest[:n_in], rest[n_in:]
    image = self_half[...] * previous[...]
    for part in parts:
        image = image + part[...].astype(F32)
    adjoint[...] = previous[...] + (target[...] - image) / self_half[...]
    to_output(scalars, (adjoint,), mine, send)
    field = adjoint[...].astype(BF16)
    panels = held.shape[1] - carried.shape[1]
    carried[...] = dot(field, held[:, panels:], ((1,), (0,)))
    which = 1 - scalars[CORE]
    adjoint_piece(
        tile, scalars, field, which, carried[...], upper, lower, held, give
    )


def adjoint_keep_kernel(
    tile, scalars, adjoint, carried, upper, lower, held, ready, keep
):
    field = adjoint[...].astype(BF16)
    which = scalars[CORE]
    adjoint_piece(
        tile, scalars, field, which, carried[...], upper, lower, held, keep
    )


def forward_kernel(tile, places, split, scalars, upper, lower, held, *rest):
    shards, (out, field) = rest[: len(places)], rest[len(places) :]
    count = out.shape[0]
    for place, ref in zip(places, shards):
        span = pl.ds(pl.multiple_of(scalars[place], LANES), ref.shape[1])
        if split:
            high = ref[...].astype(BF16)
            field[0:count, span] = high
            field[count:, span] = (ref[...] - high.astype(F32)).astype(BF16)
        else:
            field[:, span] = ref[...]
    panels = held.shape[1] - upper.shape[1]
    source = field[:, 0:panels]
    upper_local, lower_local = local_wake(scalars, upper, lower)
    strength = take_columns(source, upper_local) - take_columns(source, lower_local)
    if split:
        strength = strength[0:count] + strength[count:]
        high = strength.astype(BF16)
        field[0:count, panels:] = high
        field[count:, panels:] = (strength - high.astype(F32)).astype(BF16)
    else:
        field[:, panels:] = strength.astype(BF16)
    for start in range(0, held.shape[0], tile):
        result = dot(field[...], held[start : start + tile, :], ((1,), (1,)))
        if split:
            result = result[0:count] + result[count:]
        out[:, start : start + tile] = result


def system_kernel(n_parts, scalars, basis, image, self_half, *rest):
    parts, (keep, give) = rest[:n_parts], rest[n_parts:]
    second = self_half[...] * image[...]
    for part in parts:
        second = second + part[...]
    first = image[...] + SHIFT * basis[...]
    core = scalars[CORE]
    keep[...] = jnp.zeros_like(keep)
    give[...] = jnp.zeros_like(give)
    for b in range(2):
        rows = slice(b * BLOCK, (b + 1) * BLOCK)
        images = jnp.concatenate([first[rows], second[rows]], axis=0)
        full = jnp.concatenate([images, basis[rows, :]], axis=0)
        system = precise(images, full, ((1,), (1,)))
        size = system.shape[1]

        @pl.when(core == b)
        def _():
            keep[:, 0:size] = system

        @pl.when(core != b)
        def _():
            give[:, 0:size] = system


def to_output(scalars, values, mine, send):
    width = mine.shape[1]
    core = scalars[CORE]
    span = pl.ds(pl.multiple_of(scalars[BEGIN], LANES), width)
    for i, value in enumerate(values):
        first = value[0:BLOCK, span]
        second = value[BLOCK : 2 * BLOCK, span]
        rows = slice(i * BLOCK, (i + 1) * BLOCK)
        mine[rows, :] = jnp.where(core == 0, first, second)
        send[rows, :] = jnp.where(core == 0, second, first)


def combine_kernel(scalars, keep, other, first, second):
    half = first.shape[1]
    low = (keep[:, 0:half] + other[:, 0:half]).astype(BF16)
    high = (keep[:, half:] + other[:, half:]).astype(BF16)
    odd = scalars[ROW] % 2 == 1
    first[...] = jnp.where(odd, high, low)
    second[...] = jnp.where(odd, low, high)


def image_kernel(n_parts, scalars, right_half, self_half, *rest):
    parts, (image, rounded, mine, send) = rest[:n_parts], rest[n_parts:]
    total = (self_half[...] - SHIFT) * right_half[...]
    for part in parts:
        total = total + part[...]
    image[...] = total
    rounded[...] = total.astype(BF16)
    to_output(scalars, (right_half, image), mine, send)


def collect_kernel(scalars, keep, other, ready, *outs):
    for k, out in enumerate(outs):
        rows = pl.ds(pl.multiple_of(jnp.bitwise_xor(scalars[ROW], k) * BLOCK, BLOCK), BLOCK)
        out[...] = keep[rows, :] + other[rows, :]


def update_kernel(n_parts, scalars, mine, received, self_term, objectives, *rest):
    parts, out = rest[:n_parts], rest[n_parts]
    span = pl.ds(pl.multiple_of(scalars[SPAN], LANES), out.shape[1])
    previous = jnp.where(scalars[HOLDER] == 1, mine[...], received[...])
    scale = self_term[:, span]
    image = scale * previous
    for part in parts:
        image = image + part[...]
    out[...] = previous + (objectives[:, span] - image) / scale


def solve_kernel(n_parts, scalars, mine, received, *rest):
    parts, out = rest[:n_parts], rest[n_parts]
    basis = jnp.where(scalars[HOLDER] == 1, mine[...], received[...])
    system = parts[0][...]
    for part in parts[1:]:
        system = system + part[...]
    size = basis.shape[0]
    row = lax.broadcasted_iota(jnp.int32, (size, 1), 0)
    for j in range(size):
        pivot_row = system[j : j + 1, :] / system[j : j + 1, j : j + 1]
        factor = jnp.where(row == j, 0.0, system[:, j : j + 1])
        system = jnp.where(row == j, pivot_row, system - factor * pivot_row)
    weights = system[:, size : size + BLOCK]
    out[...] = precise(weights, basis, ((0,), (0,)))


def argument(value):
    return pltpu.with_memory_space_constraint(value, pltpu.HBM)


def keep_in_vmem(value):
    return pltpu.with_memory_space_constraint(value, pltpu.VMEM)


def params(mib=20):
    return pltpu.CompilerParams(vmem_limit_bytes=mib << 20)


def cost(flops, size):
    return pl.CostEstimate(flops=flops, bytes_accessed=size, transcendentals=0)


def per_device(
    influence,
    wake_influence,
    self_term,
    wake_upper,
    wake_lower,
    blade_of,
    mode_shapes,
    blade_pitch,
    design_map,
    objectives,
):
    influence = argument(influence)
    wake_influence = argument(wake_influence)
    n_rows, n_cols, n_rhs = (lax.axis_size(name) for name in GRID)
    side = n_cols * n_rhs
    piece, panels = influence.shape
    wake = wake_influence.shape[1]
    half = piece // n_rhs
    out_width = piece // n_cols
    count = 2 * BLOCK
    width = panels + wake
    if n_rows != side or n_rhs != 2 or panels != 2 * piece:
        raise ValueError("unsupported mesh")
    row_index = lax.axis_index("rows")
    col_index = lax.axis_index("cols")
    core = lax.axis_index("rhs")

    def cross(k):
        return [(a * side + b, b * side + (a ^ k)) for a in range(side) for b in range(side)]

    def fetch(j):
        return [
            (a * side + c * n_rhs + h, ((h ^ j) * n_cols + c) * side + a)
            for a in range(side)
            for c in range(n_cols)
            for h in range(n_rhs)
        ]

    def flip(k, size):
        return [(i, i ^ k) for i in range(size)]

    def swap(value):
        return lax.ppermute(value, "rhs", flip(1, 2))

    def cols_parts(value):
        return [value] + [lax.ppermute(value, "cols", flip(k, n_cols)) for k in range(1, n_cols)]

    near = core * piece
    far = (1 - core) * piece
    chunk_half = row_index // n_cols
    places = [
        near + chunk_half * half,
        near + (1 - chunk_half) * half,
        far + chunk_half * half,
        far + (1 - chunk_half) * half,
        near,
        far,
    ]
    span = col_index * out_width
    holder = (core == span // half).astype(jnp.int32)
    scalars = jnp.stack(
        [core, col_index * panels, row_index, span % half, holder, span] + places
    ).astype(jnp.int32)
    self_row = argument(self_term[None, :])
    objectives = argument(objectives)
    upper = argument(wake_upper[None, :])
    lower = argument(wake_lower[None, :])

    first_rows = half // 2
    parts_first, parts_all = first_rows // (half // 8), 8
    chunk = half // 8
    struct = jax.ShapeDtypeStruct

    modes = design_map[None, :]
    objectives_other = swap(objectives)
    right, right_half = pl.pallas_call(
        functools.partial(right_kernel, half),
        in_specs=[SMEM] + [VMEM] * 6,
        out_specs=[VMEM] * 2,
        out_shape=[struct((count, piece), F32), struct((count, half), F32)],
        compiler_params=params(4),
        name="right",
    )(
        scalars, argument(blade_pitch), (swap(blade_pitch)), argument(modes),
        (swap(modes)),
        argument(blade_of[None, :]), argument(mode_shapes),
    )
    right_near = lax.ppermute(right, GRID, cross(0))

    start, target, self_half, whole, held = pl.pallas_call(
        functools.partial(load_first_kernel, chunk, parts_first),
        in_specs=[SMEM] + [VMEM] * 3 + [ANY, ANY],
        out_specs=[VMEM] * 5,
        out_shape=[
            struct((count, half), F32),
            struct((count, half), F32),
            struct((1, half), F32),
            struct((count, width), F32),
            pltpu.VMEM((half, width), BF16),
        ],
        scratch_shapes=[pltpu.SemaphoreType.DMA((2, parts_first))],
        compiler_params=params(),
        cost_estimate=cost(count * half * width, 2 * first_rows * width),
        name="adjoint_one_first",
    )(
        scalars, objectives, objectives_other, self_row, influence,
        wake_influence,
    )
    right_near, start = lax.optimization_barrier((right_near, start))
    right_far = swap(right_near)
    keep, give, held = pl.pallas_call(
        functools.partial(load_rest_kernel, chunk, (parts_first, parts_all)),
        in_specs=[SMEM] + [VMEM] * 4 + [ANY, ANY, VMEM],
        out_specs=[VMEM] * 3,
        out_shape=[
            struct((count, piece), F32),
            struct((count, piece), F32),
            pltpu.VMEM((half, width), BF16),
        ],
        scratch_shapes=[
            pltpu.VMEM((count, width), F32),
            pltpu.SemaphoreType.DMA((2, parts_all)),
        ],
        compiler_params=params(),
        input_output_aliases={7: 2},
        cost_estimate=cost(count * half * width, half * width),
        name="adjoint_one_rest",
    )(
        scalars, start, upper, lower, whole, influence, wake_influence,
        keep_in_vmem(held),
    )
    held = keep_in_vmem(held)

    def forward(places, shards, split, name):
        rows = 2 * count if split else count
        return pl.pallas_call(
            functools.partial(forward_kernel, 512, places, split),
            in_specs=[SMEM] + [VMEM] * (3 + len(shards)),
            out_specs=VMEM,
            out_shape=struct((count, half), F32),
            scratch_shapes=[pltpu.VMEM((rows, width), BF16)],
            compiler_params=params(),
            cost_estimate=cost(2 * count * half * width, 2 * half * width),
            name=name,
        )(scalars, upper, lower, held, *shards)

    sends = pl.pallas_call(
        combine_kernel,
        in_specs=[SMEM] + [VMEM] * 2,
        out_specs=[VMEM] * 2,
        out_shape=[struct((count, half), BF16)] * 2,
        compiler_params=params(4),
        name="combine",
    )(scalars, keep, swap(give))

    right_far, *sends = lax.optimization_barrier((right_far, *sends))
    induced = forward(
        (CHUNKS + 4, CHUNKS + 5), [right_near, right_far], True, "forward_one"
    )
    parts = [lax.ppermute(sends[k % 2], GRID, cross(k)) for k in range(side)]
    induced, *parts = lax.optimization_barrier((induced, *parts))

    tile = min(512, out_width)
    give, adjoint, carried, adjoint_mine, adjoint_send = pl.pallas_call(
        functools.partial(adjoint_give_kernel, tile, len(parts)),
        in_specs=[SMEM] + [VMEM] * (6 + len(parts)),
        out_specs=[VMEM] * 5,
        out_shape=[
            struct((side * BLOCK, out_width), F32),
            struct((count, half), F32),
            struct((count, wake), F32),
            struct((BLOCK, out_width), F32),
            struct((BLOCK, out_width), F32),
        ],
        compiler_params=params(),
        cost_estimate=cost(count * half * width, half * width),
        name="adjoint_two_give",
    )(
        scalars, start, target, self_half, upper, lower, held,
        *parts,
    )
    induced = cols_parts(induced)
    give, *induced = lax.optimization_barrier((give, *induced))
    give = swap(give)
    image, image_rounded, bases_mine, bases_send = pl.pallas_call(
        functools.partial(image_kernel, len(induced)),
        in_specs=[SMEM] + [VMEM] * (2 + len(induced)),
        out_specs=[VMEM] * 4,
        out_shape=[
            struct((count, half), F32),
            struct((count, half), BF16),
            struct((count, out_width), F32),
            struct((count, out_width), F32),
        ],
        compiler_params=params(4),
        name="image",
    )(scalars, right_half, self_half, *induced)
    shards = [lax.ppermute(image_rounded, GRID, fetch(j)) for j in range(2)]
    keep = pl.pallas_call(
        functools.partial(adjoint_keep_kernel, tile),
        in_specs=[SMEM] + [VMEM] * 5 + [ANY],
        out_specs=VMEM,
        out_shape=struct((side * BLOCK, out_width), F32),
        compiler_params=params(),
        cost_estimate=cost(count * half * width, half * width),
        name="adjoint_two_keep",
    )(scalars, adjoint, carried, upper, lower, held, image_rounded)

    keep, *shards = lax.optimization_barrier((keep, *shards))
    shards = shards + [swap(value) for value in shards]
    induced = forward(tuple(CHUNKS + i for i in range(4)), shards, False, "forward_two")

    totals = pl.pallas_call(
        collect_kernel,
        in_specs=[SMEM, VMEM, VMEM, ANY],
        out_specs=[VMEM] * side,
        out_shape=[struct((BLOCK, out_width), F32)] * side,
        compiler_params=params(4),
        name="collect",
    )(scalars, keep, give, induced)

    induced = cols_parts(induced)
    system_keep, system_give = pl.pallas_call(
        functools.partial(system_kernel, len(induced)),
        in_specs=[SMEM] + [VMEM] * (3 + len(induced)),
        out_specs=[VMEM] * 2,
        out_shape=[struct((count, LANES), F32)] * 2,
        compiler_params=params(4),
        name="system",
    )(scalars, right_half, image, self_half, *induced)
    system = system_keep + swap(system_give)
    systems = [system] + [lax.ppermute(system, "rows", flip(k, n_rows)) for k in range(1, n_rows)]
    solution = pl.pallas_call(
        functools.partial(solve_kernel, len(systems)),
        in_specs=[SMEM] + [VMEM] * (2 + len(systems)),
        out_specs=VMEM,
        out_shape=struct((BLOCK, out_width), F32),
        compiler_params=params(4),
        name="solve",
    )(scalars, bases_mine, swap(bases_send), *systems)

    totals = [lax.ppermute(totals[k], GRID, cross(k)) for k in range(side)]
    adjoint = pl.pallas_call(
        functools.partial(update_kernel, len(totals)),
        in_specs=[SMEM] + [VMEM] * (4 + len(totals)),
        out_specs=VMEM,
        out_shape=struct((BLOCK, out_width), F32),
        compiler_params=params(4),
        name="update",
    )(scalars, adjoint_mine, swap(adjoint_send), self_row, objectives, *totals)
    return (solution, adjoint)


def solution(mesh):
    in_specs = (
        P(("groups", "rows"), "cols"),
        P(("groups", "rows"), "cols"),
        P(("groups", "rows")),
        P(("groups", "cols")),
        P(("groups", "cols")),
        P(("groups", "rows")),
        P(None, "rows"),
        P(None, "rhs"),
        P("rhs"),
        P("rhs", "rows"),
    )
    out_specs = (P("rhs", ("groups", "rows", "cols")), P("rhs", ("groups", "rows", "cols")))
    return jax.shard_map(
        per_device, mesh=mesh, in_specs=in_specs, out_specs=out_specs, check_vma=False
    )
```

time: 123 us -> 122 us (level)
  starting transfers between devices: 48.2 us -> 36.6 us
  waiting for transfers between devices: 6.81 us -> 17.7 us
  Pallas kernels: 54.6 us -> 61.5 us
  other arithmetic: 3.8 us -> 0.01 us
  local copies, waits for them, and re-layouts: 8.18 us -> 4.43 us
    ppermute x8 -> x5, waiting for transfers between devices: 0.02 us -> 7.01 us  [the longest x4 7 us: per_device(): totals = [lax.ppermute(totals[k], GRID, cross(k)) for k in range(side)]]
    pallas_call x7 -> x12, Pallas kernels: 53.2 us -> 60.1 us  [the longest x2 24.5 us: forward(): pl.pallas_call(functools.partial(forward_kernel, 512, places, split), in_...]
    ppermute x3, starting transfers between devices: 10.2 us -> 4.39 us  [per_device(): lax.ppermute(system, 'rows', flip(k, n_rows))]
    ppermute x8 -> x5, starting transfers between devices: 13 us -> 7.33 us  [the longest x4 6.65 us: per_device(): totals = [lax.ppermute(totals[k], GRID, cross(k)) for k in range(side)]]
    ppermute x11, waiting for transfers between devices: 1.26 us -> 5.57 us  [swap(): return lax.ppermute(value, 'rhs', flip(1, 2))]
    ppermute x11, starting transfers between devices: 4.07 us -> 7.8 us  [swap(): return lax.ppermute(value, 'rhs', flip(1, 2))]
    ppermute x2, starting transfers between devices: 5.89 us -> 3.23 us  [per_device(): shards = [lax.ppermute(image_rounded, GRID, fetch(j)) for j in range(2)]]
    unnamed x48 -> x50, local copies, waits for them, and re-layouts: 6.5 us -> 4.35 us
  transfers between devices with their start and end apart: 30 -> 27, of which waited for: 5 -> 10; matrix products, arithmetic and copies ran while one was open for 4% -> 0% of each run, Pallas kernels for 43% -> 39%
where the time goes in v1:
time: 122 us; the launch traced here: 121 us
  Pallas kernels  61.5 us (50%)
  starting transfers between devices  36.6 us (30%)
  waiting for transfers between devices  17.7 us (15%)
  local copies, waits for them, and re-layouts  4.43 us (4%)
    pallas_call x2, Pallas kernels, forward(): pl.pallas_call(functools.partial(forward_kernel, 512, places, split), in_...  24.5 us
    pallas_call x1, Pallas kernels, per_device(): pl.pallas_call(functools.partial(load_rest_kernel, chunk, (parts_first, p...  9.68 us
    ppermute x4, starting transfers between devices, per_device(): parts = [lax.ppermute(sends[k % 2], GRID, cross(k)) for k in range(side)]  9.59 us
    pallas_call x1, Pallas kernels, per_device(): pl.pallas_call(functools.partial(load_first_kernel, chunk, parts_first),...  8.66 us
    ppermute x11, starting transfers between devices, swap(): return lax.ppermute(value, 'rhs', flip(1, 2))  7.8 us
    ppermute x4, waiting for transfers between devices, per_device(): totals = [lax.ppermute(totals[k], GRID, cross(k)) for k in range(side)]  7 us
    ppermute x4, starting transfers between devices, per_device(): totals = [lax.ppermute(totals[k], GRID, cross(k)) for k in range(side)]  6.65 us
    ppermute x11, waiting for transfers between devices, swap(): return lax.ppermute(value, 'rhs', flip(1, 2))  5.57 us
  transfers between devices with their start and end apart: 27, of which 10 were waited for; matrix products, arithmetic and copies ran while one was open for 0% of the time, Pallas kernels for 39%

profile of v1, /device:TPU:0, one launch (start us, length us, event | category | flops | bytes accessed | tf_op | source)
XLA Modules:
  0.0 121.2 jit_solution(10364177695968715822)
XLA Ops:
  2.5 2.1 %right.1 = (f32[16,4096]{1,0:T(8,128)S(1)}, f32[16,2048]{1,0:T(8,128)S(1)}) custom-call(s32[12]{0:T(128)S(1)} %stack.55.scalars, f32[5,8]{1,0:T(8,128)} %pitch.1, f32[5,8]{1,0:T(8,128)S(1)} %collective-permute-done.pitch_other, s32[1,8]{1,0:T(1,128)} %bitcast.31, s32[1,8]{1,0:T(1,128)S(1)} %collective-permute-done.1.modes_other, s32[1,4096]{1,0:T(1,128)} %bitcast.29, ...), custom_call_target="tpu_custom_call" | custom-call | tf_op jit(solution)/shard_map/right/pallas_call | solution.py:424
  5.3 4.1 %collective-permute-start.2 = (f32[8,4096]{1,0:T(8,128)}, f32[8,4096]{1,0:T(8,128)S(1)}, u32[]{:S(2)}, u32[]{:S(2)}) collective-permute-start(f32[8,4096]{1,0:T(8,128)} %objectives.3), channel_id=1, source_target_pairs={{0,1},{1,0},{2,3},{3,2},{4,5},{5,4},{6,7},{7,6},{8,9},{9,8},{10,11... | collective-permute-start | bytes 393224 | tf_op jit(solution)/shard_map/ppermute | solution.py:391
  9.4 1.2 collective-permute-done.2.objectives_other
  11.3 8.7 %adjoint_one_first.1 = (f32[16,2048]{1,0:T(8,128)}, f32[16,2048]{1,0:T(8,128)}, f32[1,2048]{1,0:T(1,128)}, f32[16,8704]{1,0:T(8,128)}, bf16[2048,8704]{1,0:T(8,128)(2,1)S(1)}) custom-call(s32[12]{0:T(128)} %copy-done.5, f32[8,4096]{1,0:T(8,128)} %objectives.3, f32[8,4096]{1,0:T(8,128)} %copy-done.14, f32[1,4096]{1,0:T(1,128)} %bitcast.17, ...), custom_call_target="tpu_custom_call" | custom-call | flops 285212672 | bytes 17825792 | tf_op jit(solution)/shard_map/adjoint_one_first/pallas_call | solution.py:438
  20.0 9.7 %adjoint_one_rest.1 = (f32[16,4096]{1,0:T(8,128)}, f32[16,4096]{1,0:T(8,128)}, bf16[2048,8704]{1,0:T(8,128)(2,1)S(1)}) custom-call(s32[12]{0:T(128)} %copy-done.5, f32[16,2048]{1,0:T(8,128)} %get-tuple-element.49.start.previous, s32[1,512]{1,0:T(1,128)} %bitcast.19, s32[1,512]{1,0:T(1,128)} %bitcast.24, ...), custom_call_target="tpu_custom_call", output_to_operand_aliasing={{2}: (7, {})} | custom-call | flops 285212672 | bytes 17825792 | tf_op jit(solution)/shard_map/adjoint_one_rest/pallas_call | solution.py:459
  30.2 1.2 %collective-permute-done.5.other = f32[16,4096]{1,0:T(8,128)S(1)} collective-permute-done((f32[16,4096]{1,0:T(8,128)}, f32[16,4096]{1,0:T(8,128)S(1)}, u32[]{:S(2)}, u32[]{:S(2)}) %collective-permute-start.5) | collective-permute-done | bytes 262176 | tf_op jit(solution)/shard_map/ppermute | solution.py:391
  33.0 5.4 %collective-permute-start.8 = (bf16[16,2048]{1,0:T(8,128)(2,1)S(1)}, bf16[16,2048]{1,0:T(8,128)(2,1)S(1)}, u32[]{:S(2)}, u32[]{:S(2)}) collective-permute-start(bf16[16,2048]{1,0:T(8,128)(2,1)S(1)} %get-tuple-element.60), channel_id=1, source_target_pairs={{0,2},{1,6},{2,10},{3,14},{4,3},{5,7},{6,11},{7,15},{8,0},{9,4},{1... | collective-permute-start | bytes 196616 | tf_op jit(solution)/shard_map/ppermute | solution.py:508
  39.0 3.5 %collective-permute-start.9 = (bf16[16,2048]{1,0:T(8,128)(2,1)S(1)}, bf16[16,2048]{1,0:T(8,128)(2,1)S(1)}, u32[]{:S(2)}, u32[]{:S(2)}) collective-permute-start(bf16[16,2048]{1,0:T(8,128)(2,1)S(1)} %get-tuple-element.61), channel_id=1, source_target_pairs={{0,3},{1,7},{2,11},{3,15},{4,2},{5,6},{6,10},{7,14},{8,1},{9,5},{1... | collective-permute-start | bytes 196616 | tf_op jit(solution)/shard_map/ppermute | solution.py:508
  42.6 13.1 %forward_one.1.rest_0_ = f32[16,2048]{1,0:T(8,128)} custom-call(s32[12]{0:T(128)} %copy-done.5, s32[1,512]{1,0:T(1,128)} %bitcast.20, s32[1,512]{1,0:T(1,128)} %bitcast.25, bf16[2048,8704]{1,0:T(8,128)(2,1)S(1)} %get-tuple-element.53.held, f32[16,4096]{1,0:T(8,128)} %copy-done.12, f32[16,4096]{1,0:T(8,128)} %copy-done.13), custom_call_target="tpu_custom_call" | custom-call | flops 570425344 | bytes 35651584 | tf_op jit(solution)/shard_map/forward_one/pallas_call | solution.py:484
  56.5 4.8 %adjoint_two_give.1 = (f32[32,2048]{1,0:T(8,128)}, f32[16,2048]{1,0:T(8,128)}, f32[16,512]{1,0:T(8,128)}, f32[8,2048]{1,0:T(8,128)}, f32[8,2048]{1,0:T(8,128)}) custom-call(s32[12]{0:T(128)} %copy-done.5, f32[16,2048]{1,0:T(8,128)} %get-tuple-element.49.start.previous, f32[16,2048]{1,0:T(8,128)} %get-tuple-element.50.target, ...), custom_call_target="tpu_custom_call" | custom-call | flops 285212672 | bytes 17825792 | tf_op jit(solution)/shard_map/adjoint_two_give/pallas_call | solution.py:512
  63.0 2.4 %collective-permute-start.13 = (bf16[16,2048]{1,0:T(8,128)(2,1)S(1)}, bf16[16,2048]{1,0:T(8,128)(2,1)S(1)}, u32[]{:S(2)}, u32[]{:S(2)}) collective-permute-start(bf16[16,2048]{1,0:T(8,128)(2,1)S(1)} %get-tuple-element.75.ready), channel_id=1, source_target_pairs={{0,8},{1,0},{2,12},{3,4},{4,9},{5,1},{6,13},{7,5},{8,10},{9,2},{10... | collective-permute-start | bytes 196616 | tf_op jit(solution)/shard_map/ppermute | solution.py:546
  66.2 4.3 %adjoint_two_keep.1.keep = f32[32,2048]{1,0:T(8,128)} custom-call(s32[12]{0:T(128)} %copy-done.5, f32[16,2048]{1,0:T(8,128)} %get-tuple-element.73.adjoint, f32[16,512]{1,0:T(8,128)} %get-tuple-element.74.carried, s32[1,512]{1,0:T(1,128)} %bitcast.22, s32[1,512]{1,0:T(1,128)} %bitcast.27, bf16[2048,8704]{1,0:T(8,128)(2,1)S(1)} %get-tuple-element.53.held, ...), custom_call_target="tpu_custom_call" | custom-call | flops 285212672 | bytes 17825792 | tf_op jit(solution)/shard_map/adjoint_two_keep/pallas_call | solution.py:547
  70.6 2.0 %collective-permute-start.14 = (bf16[16,2048]{1,0:T(8,128)(2,1)S(1)}, bf16[16,2048]{1,0:T(8,128)(2,1)S(1)}, u32[]{:S(2)}, u32[]{:S(2)}) collective-permute-start(bf16[16,2048]{1,0:T(8,128)(2,1)S(1)} %collective-permute-done.12.rest_0_), channel_id=1, source_target_pairs={{0,1},{1,0},{2,3},{3,2},{4,5},{5,4},{6,7},{7,6},{8,9},{9,8},{10,11... | collective-permute-start | bytes 196616 | tf_op jit(solution)/shard_map/ppermute | solution.py:391
  74.7 11.4 %forward_two.1.rest_0_.ready = f32[16,2048]{1,0:T(8,128)} custom-call(s32[12]{0:T(128)} %copy-done.5, s32[1,512]{1,0:T(1,128)} %bitcast.23, s32[1,512]{1,0:T(1,128)} %bitcast.28, bf16[2048,8704]{1,0:T(8,128)(2,1)S(1)} %get-tuple-element.53.held, bf16[16,2048]{1,0:T(8,128)(2,1)} %copy-done.20, bf16[16,2048]{1,0:T(8,128)(2,1)} %copy-done.19, ...), custom_call_target="tpu_custom_call" | custom-call | flops 570425344 | bytes 35651584 | tf_op jit(solution)/shard_map/forward_two/pallas_call | solution.py:484
  86.1 3.5 %collective-permute-start.16 = (f32[16,2048]{1,0:T(8,128)}, f32[16,2048]{1,0:T(8,128)S(1)}, u32[]{:S(2)}, u32[]{:S(2)}) collective-permute-start(f32[16,2048]{1,0:T(8,128)} %forward_two.1.rest_0_.ready), channel_id=1, source_target_pairs={{0,2},{2,0},{1,3},{3,1},{4,6},{6,4},{5,7},{7,5},{8,10},{10,8},{9,1... | collective-permute-start | bytes 393224 | tf_op jit(solution)/shard_map/ppermute | solution.py:394
  89.6 4.0 %collective-permute-done.16.rest_1_ = f32[16,2048]{1,0:T(8,128)S(1)} collective-permute-done((f32[16,2048]{1,0:T(8,128)}, f32[16,2048]{1,0:T(8,128)S(1)}, u32[]{:S(2)}, u32[]{:S(2)}) %collective-permute-start.16) | collective-permute-done | bytes 131104 | tf_op jit(solution)/shard_map/ppermute | solution.py:394
  94.5 1.5 %system.1 = (f32[16,128]{1,0:T(8,128)S(1)}, f32[16,128]{1,0:T(8,128)S(1)}) custom-call(s32[12]{0:T(128)S(1)} %copy-done.8, f32[16,2048]{1,0:T(8,128)S(1)} %get-tuple-element.45.right_half.basis, f32[16,2048]{1,0:T(8,128)S(1)} %get-tuple-element.72.image, f32[1,2048]{1,0:T(1,128)S(1)} %copy-done.9, f32[16,2048]{1,0:T(8,128)S(1)} %copy-done, ...), custom_call_target="tpu_custom_call" | custom-call | tf_op jit(solution)/shard_map/system/pallas_call | solution.py:571
  97.2 2.0 %collective-permute-start.20 = (f32[16,128]{1,0:T(8,128)S(1)}, f32[16,128]{1,0:T(8,128)S(1)}, u32[]{:S(2)}, u32[]{:S(2)}) collective-permute-start(f32[16,128]{1,0:T(8,128)S(1)} %add.26.rest_0_), channel_id=1, source_target_pairs={{0,12},{4,8},{8,4},{12,0},{1,13},{5,9},{9,5},{13,1},{2,14},{6,10},... | collective-permute-start | bytes 24584 | tf_op jit(solution)/shard_map/ppermute | solution.py:580
  99.4 2.2 %collective-permute-start.18 = (f32[16,128]{1,0:T(8,128)S(1)}, f32[16,128]{1,0:T(8,128)S(1)}, u32[]{:S(2)}, u32[]{:S(2)}) collective-permute-start(f32[16,128]{1,0:T(8,128)S(1)} %add.26.rest_0_), channel_id=1, source_target_pairs={{0,4},{4,0},{8,12},{12,8},{1,5},{5,1},{9,13},{13,9},{2,6},{6,2},{1... | collective-permute-start | bytes 24584 | tf_op jit(solution)/shard_map/ppermute | solution.py:580
  103.8 1.8 %collective-permute-start.24 = (f32[8,2048]{1,0:T(8,128)S(1)}, f32[8,2048]{1,0:T(8,128)S(1)}, u32[]{:S(2)}, u32[]{:S(2)}) collective-permute-start(f32[8,2048]{1,0:T(8,128)S(1)} %get-tuple-element.85), channel_id=1, source_target_pairs={{0,1},{1,5},{2,9},{3,13},{4,0},{5,4},{6,8},{7,12},{8,3},{9,7},{10,... | collective-permute-start | bytes 196616 | tf_op jit(solution)/shard_map/ppermute | solution.py:590
  105.6 3.4 %collective-permute-start.25 = (f32[8,2048]{1,0:T(8,128)S(1)}, f32[8,2048]{1,0:T(8,128)S(1)}, u32[]{:S(2)}, u32[]{:S(2)}) collective-permute-start(f32[8,2048]{1,0:T(8,128)S(1)} %get-tuple-element.86), channel_id=1, source_target_pairs={{0,2},{1,6},{2,10},{3,14},{4,3},{5,7},{6,11},{7,15},{8,0},{9,4},{1... | collective-permute-start | bytes 196616 | tf_op jit(solution)/shard_map/ppermute | solution.py:590
  109.8 2.8 %solve.1 = f32[8,2048]{1,0:T(8,128)} custom-call(s32[12]{0:T(128)S(1)} %copy-done.8, f32[16,2048]{1,0:T(8,128)S(1)} %get-tuple-element.70.mine, f32[16,2048]{1,0:T(8,128)S(1)} %collective-permute-done.11.received, f32[16,128]{1,0:T(8,128)S(1)} %add.26.rest_0_, f32[16,128]{1,0:T(8,128)S(1)} %collective-permute-done.18.rest_1_, ...), custom_call_target="tpu_custom_call" | custom-call | tf_op jit(solution)/shard_map/solve/pallas_call | solution.py:581
  112.6 7.0 %collective-permute-done.25.rest_2_ = f32[8,2048]{1,0:T(8,128)S(1)} collective-permute-done((f32[8,2048]{1,0:T(8,128)S(1)}, f32[8,2048]{1,0:T(8,128)S(1)}, u32[]{:S(2)}, u32[]{:S(2)}) %collective-permute-start.25) | collective-permute-done | bytes 65568 | tf_op jit(solution)/shard_map/ppermute | solution.py:590
  119.6 1.6 %update.1 = f32[8,2048]{1,0:T(8,128)} custom-call(s32[12]{0:T(128)S(1)} %copy-done.8, f32[8,2048]{1,0:T(8,128)S(1)} %copy-done.11, f32[8,2048]{1,0:T(8,128)S(1)} %collective-permute-done.21.received, f32[1,4096]{1,0:T(1,128)} %bitcast.18, f32[8,4096]{1,0:T(8,128)} %objectives.3, f32[8,2048]{1,0:T(8,128)S(1)} %collective-permute-done.23.rest_0_, ...), custom_call_target="tpu_custom_call" | custom-call | tf_op jit(solution)/shard_map/update/pallas_call | solution.py:591
  (95 shorter events, 16.8 us)
Async XLA Ops:
  0.6 1.5 %collective-permute-start.1 = (s32[1,8]{1,0:T(1,128)}, s32[1,8]{1,0:T(1,128)S(1)}, u32[]{:S(2)}, u32[]{:S(2)}) collective-permute-start(s32[1,8]{1,0:T(1,128)} %bitcast.30), channel_id=1, source_target_pairs={{0,1},{1,0},{2,3},{3,2},{4,5},{5,4},{6,7},{7,6},{8,9},{9,8},{10,11... | collective-permute-start | bytes 104 | tf_op jit(solution)/shard_map/ppermute | solution.py:391
  4.6 15.3 %collective-permute-start.3 = (f32[16,4096]{1,0:T(8,128)S(1)}, f32[16,4096]{1,0:T(8,128)S(1)}, u32[]{:S(2)}, u32[]{:S(2)}) collective-permute-start(f32[16,4096]{1,0:T(8,128)S(1)} %get-tuple-element.47), channel_id=1, source_target_pairs={{0,0},{1,4},{2,8},{3,12},{4,1},{5,5},{6,9},{7,13},{8,2},{9,6},{10,... | collective-permute-start | bytes 786440 | tf_op jit(solution)/shard_map/ppermute | solution.py:436
  5.3 5.3 %collective-permute-start.2 = (f32[8,4096]{1,0:T(8,128)}, f32[8,4096]{1,0:T(8,128)S(1)}, u32[]{:S(2)}, u32[]{:S(2)}) collective-permute-start(f32[8,4096]{1,0:T(8,128)} %objectives.3), channel_id=1, source_target_pairs={{0,1},{1,0},{2,3},{3,2},{4,5},{5,4},{6,7},{7,6},{8,9},{9,8},{10,11... | collective-permute-start | bytes 393224 | tf_op jit(solution)/shard_map/ppermute | solution.py:391
  29.6 1.8 %collective-permute-start.5 = (f32[16,4096]{1,0:T(8,128)}, f32[16,4096]{1,0:T(8,128)S(1)}, u32[]{:S(2)}, u32[]{:S(2)}) collective-permute-start(f32[16,4096]{1,0:T(8,128)} %get-tuple-element.56), channel_id=1, source_target_pairs={{0,1},{1,0},{2,3},{3,2},{4,5},{5,4},{6,7},{7,6},{8,9},{9,8},{10,11... | collective-permute-start | bytes 786440 | tf_op jit(solution)/shard_map/ppermute | solution.py:391
  30.1 2.9 %collective-permute-start.4 = (f32[16,4096]{1,0:T(8,128)S(1)}, f32[16,4096]{1,0:T(8,128)S(1)}, u32[]{:S(2)}, u32[]{:S(2)}) collective-permute-start(f32[16,4096]{1,0:T(8,128)S(1)} %collective-permute-done.3.rest_0_), channel_id=1, source_target_pairs={{0,1},{1,0},{2,3},{3,2},{4,5},{5,4},{6,7},{7,6},{8,9},{9,8},{10,11... | collective-permute-start | bytes 786440 | tf_op jit(solution)/shard_map/ppermute | solution.py:391
  33.0 22.7 %collective-permute-start.8 = (bf16[16,2048]{1,0:T(8,128)(2,1)S(1)}, bf16[16,2048]{1,0:T(8,128)(2,1)S(1)}, u32[]{:S(2)}, u32[]{:S(2)}) collective-permute-start(bf16[16,2048]{1,0:T(8,128)(2,1)S(1)} %get-tuple-element.60), channel_id=1, source_target_pairs={{0,2},{1,6},{2,10},{3,14},{4,3},{5,7},{6,11},{7,15},{8,0},{9,4},{1... | collective-permute-start | bytes 196616 | tf_op jit(solution)/shard_map/ppermute | solution.py:508
  38.4 17.3 %collective-permute-start.6 = (bf16[16,2048]{1,0:T(8,128)(2,1)S(1)}, bf16[16,2048]{1,0:T(8,128)(2,1)S(1)}, u32[]{:S(2)}, u32[]{:S(2)}) collective-permute-start(bf16[16,2048]{1,0:T(8,128)(2,1)S(1)} %get-tuple-element.60), channel_id=1, source_target_pairs={{0,0},{1,4},{2,8},{3,12},{4,1},{5,5},{6,9},{7,13},{8,2},{9,6},{10,... | collective-permute-start | bytes 196616 | tf_op jit(solution)/shard_map/ppermute | solution.py:508
  39.0 16.7 %collective-permute-start.9 = (bf16[16,2048]{1,0:T(8,128)(2,1)S(1)}, bf16[16,2048]{1,0:T(8,128)(2,1)S(1)}, u32[]{:S(2)}, u32[]{:S(2)}) collective-permute-start(bf16[16,2048]{1,0:T(8,128)(2,1)S(1)} %get-tuple-element.61), channel_id=1, source_target_pairs={{0,3},{1,7},{2,11},{3,15},{4,2},{5,6},{6,10},{7,14},{8,1},{9,5},{1... | collective-permute-start | bytes 196616 | tf_op jit(solution)/shard_map/ppermute | solution.py:508
  42.5 13.2 %collective-permute-start.7 = (bf16[16,2048]{1,0:T(8,128)(2,1)S(1)}, bf16[16,2048]{1,0:T(8,128)(2,1)S(1)}, u32[]{:S(2)}, u32[]{:S(2)}) collective-permute-start(bf16[16,2048]{1,0:T(8,128)(2,1)S(1)} %get-tuple-element.61), channel_id=1, source_target_pairs={{0,1},{1,5},{2,9},{3,13},{4,0},{5,4},{6,8},{7,12},{8,3},{9,7},{10,... | collective-permute-start | bytes 196616 | tf_op jit(solution)/shard_map/ppermute | solution.py:508
  55.8 6.6 %collective-permute-start.10 = (f32[16,2048]{1,0:T(8,128)}, f32[16,2048]{1,0:T(8,128)S(1)}, u32[]{:S(2)}, u32[]{:S(2)}) collective-permute-start(f32[16,2048]{1,0:T(8,128)} %forward_one.1.rest_0_), channel_id=1, source_target_pairs={{0,2},{2,0},{1,3},{3,1},{4,6},{6,4},{5,7},{7,5},{8,10},{10,8},{9,1... | collective-permute-start | bytes 393224 | tf_op jit(solution)/shard_map/ppermute | solution.py:394
  63.0 7.6 %collective-permute-start.13 = (bf16[16,2048]{1,0:T(8,128)(2,1)S(1)}, bf16[16,2048]{1,0:T(8,128)(2,1)S(1)}, u32[]{:S(2)}, u32[]{:S(2)}) collective-permute-start(bf16[16,2048]{1,0:T(8,128)(2,1)S(1)} %get-tuple-element.75.ready), channel_id=1, source_target_pairs={{0,8},{1,0},{2,12},{3,4},{4,9},{5,1},{6,13},{7,5},{8,10},{9,2},{10... | collective-permute-start | bytes 196616 | tf_op jit(solution)/shard_map/ppermute | solution.py:546
  65.3 5.2 %collective-permute-start.12 = (bf16[16,2048]{1,0:T(8,128)(2,1)S(1)}, bf16[16,2048]{1,0:T(8,128)(2,1)S(1)}, u32[]{:S(2)}, u32[]{:S(2)}) collective-permute-start(bf16[16,2048]{1,0:T(8,128)(2,1)S(1)} %get-tuple-element.75.ready), channel_id=1, source_target_pairs={{0,0},{1,8},{2,4},{3,12},{4,1},{5,9},{6,5},{7,13},{8,2},{9,10},{10... | collective-permute-start | bytes 196616 | tf_op jit(solution)/shard_map/ppermute | solution.py:546
  70.6 2.9 %collective-permute-start.14 = (bf16[16,2048]{1,0:T(8,128)(2,1)S(1)}, bf16[16,2048]{1,0:T(8,128)(2,1)S(1)}, u32[]{:S(2)}, u32[]{:S(2)}) collective-permute-start(bf16[16,2048]{1,0:T(8,128)(2,1)S(1)} %collective-permute-done.12.rest_0_), channel_id=1, source_target_pairs={{0,1},{1,0},{2,3},{3,2},{4,5},{5,4},{6,7},{7,6},{8,9},{9,8},{10,11... | collective-permute-start | bytes 196616 | tf_op jit(solution)/shard_map/ppermute | solution.py:391
  72.6 29.0 %collective-permute-start.22 = (f32[32,2048]{1,0:T(8,128)S(1)}, f32[32,2048]{1,0:T(8,128)S(1)}, u32[]{:S(2)}, u32[]{:S(2)}) collective-permute-start(f32[32,2048]{1,0:T(8,128)S(1)} %copy-done.23), channel_id=1, source_target_pairs={{0,1},{1,0},{2,3},{3,2},{4,5},{5,4},{6,7},{7,6},{8,9},{9,8},{10,11... | collective-permute-start | bytes 786440 | tf_op jit(solution)/shard_map/ppermute | solution.py:391
  86.1 7.5 %collective-permute-start.16 = (f32[16,2048]{1,0:T(8,128)}, f32[16,2048]{1,0:T(8,128)S(1)}, u32[]{:S(2)}, u32[]{:S(2)}) collective-permute-start(f32[16,2048]{1,0:T(8,128)} %forward_two.1.rest_0_.ready), channel_id=1, source_target_pairs={{0,2},{2,0},{1,3},{3,1},{4,6},{6,4},{5,7},{7,5},{8,10},{10,8},{9,1... | collective-permute-start | bytes 393224 | tf_op jit(solution)/shard_map/ppermute | solution.py:394
  89.6 13.5 %collective-permute-start.11 = (f32[16,2048]{1,0:T(8,128)S(1)}, f32[16,2048]{1,0:T(8,128)S(1)}, u32[]{:S(2)}, u32[]{:S(2)}) collective-permute-start(f32[16,2048]{1,0:T(8,128)S(1)} %get-tuple-element.71), channel_id=1, source_target_pairs={{0,1},{1,0},{2,3},{3,2},{4,5},{5,4},{6,7},{7,6},{8,9},{9,8},{10,11... | collective-permute-start | bytes 393224 | tf_op jit(solution)/shard_map/ppermute | solution.py:391
  97.2 6.6 %collective-permute-start.20 = (f32[16,128]{1,0:T(8,128)S(1)}, f32[16,128]{1,0:T(8,128)S(1)}, u32[]{:S(2)}, u32[]{:S(2)}) collective-permute-start(f32[16,128]{1,0:T(8,128)S(1)} %add.26.rest_0_), channel_id=1, source_target_pairs={{0,12},{4,8},{8,4},{12,0},{1,13},{5,9},{9,5},{13,1},{2,14},{6,10},... | collective-permute-start | bytes 24584 | tf_op jit(solution)/shard_map/ppermute | solution.py:580
  99.2 6.4 %collective-permute-start.19 = (f32[16,128]{1,0:T(8,128)S(1)}, f32[16,128]{1,0:T(8,128)S(1)}, u32[]{:S(2)}, u32[]{:S(2)}) collective-permute-start(f32[16,128]{1,0:T(8,128)S(1)} %add.26.rest_0_), channel_id=1, source_target_pairs={{0,8},{4,12},{8,0},{12,4},{1,9},{5,13},{9,1},{13,5},{2,10},{6,14},... | collective-permute-start | bytes 24584 | tf_op jit(solution)/shard_map/ppermute | solution.py:580
  99.4 9.6 %collective-permute-start.18 = (f32[16,128]{1,0:T(8,128)S(1)}, f32[16,128]{1,0:T(8,128)S(1)}, u32[]{:S(2)}, u32[]{:S(2)}) collective-permute-start(f32[16,128]{1,0:T(8,128)S(1)} %add.26.rest_0_), channel_id=1, source_target_pairs={{0,4},{4,0},{8,12},{12,8},{1,5},{5,1},{9,13},{13,9},{2,6},{6,2},{1... | collective-permute-start | bytes 24584 | tf_op jit(solution)/shard_map/ppermute | solution.py:580
  101.6 11.0 %collective-permute-start.21 = (f32[8,2048]{1,0:T(8,128)S(1)}, f32[8,2048]{1,0:T(8,128)S(1)}, u32[]{:S(2)}, u32[]{:S(2)}) collective-permute-start(f32[8,2048]{1,0:T(8,128)S(1)} %copy-done.24), channel_id=1, source_target_pairs={{0,1},{1,0},{2,3},{3,2},{4,5},{5,4},{6,7},{7,6},{8,9},{9,8},{10,11... | collective-permute-start | bytes 196616 | tf_op jit(solution)/shard_map/ppermute | solution.py:391
  103.1 9.5 %collective-permute-start.23 = (f32[8,2048]{1,0:T(8,128)S(1)}, f32[8,2048]{1,0:T(8,128)S(1)}, u32[]{:S(2)}, u32[]{:S(2)}) collective-permute-start(f32[8,2048]{1,0:T(8,128)S(1)} %get-tuple-element.84), channel_id=1, source_target_pairs={{0,0},{1,4},{2,8},{3,12},{4,1},{5,5},{6,9},{7,13},{8,2},{9,6},{10,... | collective-permute-start | bytes 196616 | tf_op jit(solution)/shard_map/ppermute | solution.py:590
  103.8 8.8 %collective-permute-start.24 = (f32[8,2048]{1,0:T(8,128)S(1)}, f32[8,2048]{1,0:T(8,128)S(1)}, u32[]{:S(2)}, u32[]{:S(2)}) collective-permute-start(f32[8,2048]{1,0:T(8,128)S(1)} %get-tuple-element.85), channel_id=1, source_target_pairs={{0,1},{1,5},{2,9},{3,13},{4,0},{5,4},{6,8},{7,12},{8,3},{9,7},{10,... | collective-permute-start | bytes 196616 | tf_op jit(solution)/shard_map/ppermute | solution.py:590
  105.6 14.0 %collective-permute-start.25 = (f32[8,2048]{1,0:T(8,128)S(1)}, f32[8,2048]{1,0:T(8,128)S(1)}, u32[]{:S(2)}, u32[]{:S(2)}) collective-permute-start(f32[8,2048]{1,0:T(8,128)S(1)} %get-tuple-element.86), channel_id=1, source_target_pairs={{0,2},{1,6},{2,10},{3,14},{4,3},{5,7},{6,11},{7,15},{8,0},{9,4},{1... | collective-permute-start | bytes 196616 | tf_op jit(solution)/shard_map/ppermute | solution.py:590
  109.0 10.6 %collective-permute-start.26 = (f32[8,2048]{1,0:T(8,128)S(1)}, f32[8,2048]{1,0:T(8,128)S(1)}, u32[]{:S(2)}, u32[]{:S(2)}) collective-permute-start(f32[8,2048]{1,0:T(8,128)S(1)} %get-tuple-element.87), channel_id=1, source_target_pairs={{0,3},{1,7},{2,11},{3,15},{4,2},{5,6},{6,10},{7,14},{8,1},{9,5},{1... | collective-permute-start | bytes 196616 | tf_op jit(solution)/shard_map/ppermute | solution.py:590
  (28 other events, 266.6 us)

commit v2 on v1

--- a/solution.py
+++ b/solution.py
@@ -111,13 +111,16 @@
     return upper[...] - start, lower[...] - start
 
 
-def load_first_kernel(
-    chunk, steps, scalars, objectives, objectives_other, self_term, influence, wake,
-    start, target, self_half, whole, held, sems
+def load_adjoint_kernel(
+    chunk, scalars, objectives, objectives_other, self_term, upper, lower, influence, wake,
+    keep, give, start, target, self_half, held, whole, sems
 ):
     half = start.shape[1]
+    piece = keep.shape[1]
+    panels = 2 * piece
     core = scalars[CORE]
     copies = load_copies(influence, wake, held, sems, core * half, chunk)
+    steps = held.shape[0] // chunk
     for i in range(steps):
         for copy in copies(i):
             copy.start()
@@ -134,26 +137,6 @@
             whole[...] = part
         else:
             whole[...] += part
-
-
-def load_rest_kernel(
-    chunk, steps, scalars, start, upper, lower, whole_first, influence, wake, held_first,
-    keep, give, held, whole, sems
-):
-    half = start.shape[1]
-    piece = keep.shape[1]
-    panels = 2 * piece
-    core = scalars[CORE]
-    copies = load_copies(influence, wake, held, sems, core * half, chunk)
-    for i in range(*steps):
-        for copy in copies(i):
-            copy.start()
-    whole[...] = whole_first[...]
-    for i in range(*steps):
-        for copy in copies(i):
-            copy.wait()
-        rows = slice(i * chunk, (i + 1) * chunk)
-        whole[...] += dot(start[:, rows].astype(BF16), held[rows, :], ((1,), (0,)))
     upper_local, lower_local = local_wake(scalars, upper, lower)
     carried = whole[:, panels:]
     whole[:, 0:panels] += put_columns(carried, upper_local, panels) - put_columns(
@@ -296,7 +279,7 @@
     to_output(scalars, (right_half, image), mine, send)
 
 
-def collect_kernel(scalars, keep, other, ready, *outs):
+def collect_kernel(scalars, keep, other, *outs):
     for k, out in enumerate(outs):
         rows = pl.ds(pl.multiple_of(jnp.bitwise_xor(scalars[ROW], k) * BLOCK, BLOCK), BLOCK)
         out[...] = keep[rows, :] + other[rows, :]
@@ -414,8 +397,6 @@
     upper = argument(wake_upper[None, :])
     lower = argument(wake_lower[None, :])
 
-    first_rows = half // 2
-    parts_first, parts_all = first_rows // (half // 8), 8
     chunk = half // 8
     struct = jax.ShapeDtypeStruct
 
@@ -433,50 +414,33 @@
         (swap(modes)),
         argument(blade_of[None, :]), argument(mode_shapes),
     )
+    right, objectives_other = lax.optimization_barrier((right, objectives_other))
     right_near = lax.ppermute(right, GRID, cross(0))
 
-    start, target, self_half, whole, held = pl.pallas_call(
-        functools.partial(load_first_kernel, chunk, parts_first),
-        in_specs=[SMEM] + [VMEM] * 3 + [ANY, ANY],
-        out_specs=[VMEM] * 5,
+    keep, give, start, target, self_half, held = pl.pallas_call(
+        functools.partial(load_adjoint_kernel, chunk),
+        in_specs=[SMEM] + [VMEM] * 5 + [ANY, ANY],
+        out_specs=[VMEM] * 6,
         out_shape=[
+            struct((count, piece), F32),
+            struct((count, piece), F32),
             struct((count, half), F32),
             struct((count, half), F32),
             struct((1, half), F32),
-            struct((count, width), F32),
-            pltpu.VMEM((half, width), BF16),
-        ],
-        scratch_shapes=[pltpu.SemaphoreType.DMA((2, parts_first))],
-        compiler_params=params(),
-        cost_estimate=cost(count * half * width, 2 * first_rows * width),
-        name="adjoint_one_first",
-    )(
-        scalars, objectives, objectives_other, self_row, influence,
-        wake_influence,
-    )
-    right_near, start = lax.optimization_barrier((right_near, start))
-    right_far = swap(right_near)
-    keep, give, held = pl.pallas_call(
-        functools.partial(load_rest_kernel, chunk, (parts_first, parts_all)),
-        in_specs=[SMEM] + [VMEM] * 4 + [ANY, ANY, VMEM],
-        out_specs=[VMEM] * 3,
-        out_shape=[
-            struct((count, piece), F32),
-            struct((count, piece), F32),
             pltpu.VMEM((half, width), BF16),
         ],
         scratch_shapes=[
             pltpu.VMEM((count, width), F32),
-            pltpu.SemaphoreType.DMA((2, parts_all)),
+            pltpu.SemaphoreType.DMA((2, half // chunk)),
         ],
         compiler_params=params(),
-        input_output_aliases={7: 2},
-        cost_estimate=cost(count * half * width, half * width),
-        name="adjoint_one_rest",
+        cost_estimate=cost(2 * count * half * width, 2 * half * width),
+        name="adjoint_one",
     )(
-        scalars, start, upper, lower, whole, influence, wake_influence,
-        keep_in_vmem(held),
-    )
+        scalars, objectives, objectives_other, self_row, upper, lower, influence, wake_influence
+    )
+    right_near, start = lax.optimization_barrier((right_near, start))
+    right_far = swap(right_near)
     held = keep_in_vmem(held)
 
     def forward(places, shards, split, name):
@@ -556,16 +520,20 @@
 
     keep, *shards = lax.optimization_barrier((keep, *shards))
     shards = shards + [swap(value) for value in shards]
-    induced = forward(tuple(CHUNKS + i for i in range(4)), shards, False, "forward_two")
-
     totals = pl.pallas_call(
         collect_kernel,
-        in_specs=[SMEM, VMEM, VMEM, ANY],
+        in_specs=[SMEM, VMEM, VMEM],
         out_specs=[VMEM] * side,
         out_shape=[struct((BLOCK, out_width), F32)] * side,
         compiler_params=params(4),
         name="collect",
-    )(scalars, keep, give, induced)
+    )(scalars, keep, give)
+    *shards, first_total = lax.optimization_barrier((*shards, totals[0]))
+    totals = [first_total, *totals[1:]]
+    induced = forward(tuple(CHUNKS + i for i in range(4)), shards, False, "forward_two")
+
+    induced, *totals = lax.optimization_barrier((induced, *totals))
+    totals = [lax.ppermute(totals[k], GRID, cross(k)) for k in range(side)]
 
     induced = cols_parts(induced)
     system_keep, system_give = pl.pallas_call(
@@ -576,6 +544,7 @@
         compiler_params=params(4),
         name="system",
     )(scalars, right_half, image, self_half, *induced)
+    system_give, *totals = lax.optimization_barrier((system_give, *totals))
     system = system_keep + swap(system_give)
     systems = [system] + [lax.ppermute(system, "rows", flip(k, n_rows)) for k in range(1, n_rows)]
     solution = pl.pallas_call(
@@ -587,7 +556,6 @@
         name="solve",
     )(scalars, bases_mine, swap(bases_send), *systems)
 
-    totals = [lax.ppermute(totals[k], GRID, cross(k)) for k in range(side)]
     adjoint = pl.pallas_call(
         functools.partial(update_kernel, len(totals)),
         in_specs=[SMEM] + [VMEM] * (4 + len(totals)),

time: 122 us -> 110 us (0.902)
  waiting for transfers between devices: 17.7 us -> 7.77 us
  Pallas kernels: 61.5 us -> 57.8 us
  starting transfers between devices: 36.6 us -> 38.4 us
    ppermute x2, waiting for transfers between devices: 5.12 us -> 0.01 us  [cols_parts(): lax.ppermute(value, 'cols', flip(k, n_cols))]
    pallas_call x3 -> x2, Pallas kernels: 18.9 us -> 15.1 us  [the longest x1 14.6 us: per_device(): pl.pallas_call(functools.partial(load_adjoint_kernel, chunk), in_specs=[S...]
    ppermute x4, waiting for transfers between devices: 7 us -> 4.42 us  [per_device(): totals = [lax.ppermute(totals[k], GRID, cross(k)) for k in range(side)]]
    ppermute x11, waiting for transfers between devices: 5.57 us -> 3.06 us  [swap(): return lax.ppermute(value, 'rhs', flip(1, 2))]
    ppermute x2, starting transfers between devices: 3.23 us -> 5.28 us  [per_device(): shards = [lax.ppermute(image_rounded, GRID, fetch(j)) for j in range(2)]]
    unnamed x50 -> x48, local copies, waits for them, and re-layouts: 4.35 us -> 4.05 us
  transfers between devices with their start and end apart: 27 -> 27, of which waited for: 10 -> 6; matrix products, arithmetic and copies ran while one was open for 0% -> 0% of each run, Pallas kernels for 39% -> 40%
where the time goes in v2:
time: 110 us; the launch traced here: 109 us
  Pallas kernels  57.8 us (53%)
  starting transfers between devices  38.4 us (35%)
  waiting for transfers between devices  7.77 us (7%)
  local copies, waits for them, and re-layouts  4.13 us (4%)
    pallas_call x2, Pallas kernels, forward(): pl.pallas_call(functools.partial(forward_kernel, 512, places, split), in_...  24.5 us
    pallas_call x1, Pallas kernels, per_device(): pl.pallas_call(functools.partial(load_adjoint_kernel, chunk), in_specs=[S...  14.6 us
    ppermute x4, starting transfers between devices, per_device(): parts = [lax.ppermute(sends[k % 2], GRID, cross(k)) for k in range(side)]  8.48 us
    ppermute x11, starting transfers between devices, swap(): return lax.ppermute(value, 'rhs', flip(1, 2))  8.41 us
    ppermute x4, starting transfers between devices, per_device(): totals = [lax.ppermute(totals[k], GRID, cross(k)) for k in range(side)]  6.34 us
    ppermute x2, starting transfers between devices, per_device(): shards = [lax.ppermute(image_rounded, GRID, fetch(j)) for j in range(2)]  5.28 us
    ppermute x2, starting transfers between devices, cols_parts(): lax.ppermute(value, 'cols', flip(k, n_cols))  4.79 us
    pallas_call x1, Pallas kernels, per_device(): pl.pallas_call(functools.partial(adjoint_give_kernel, tile, len(parts)),...  4.75 us
  transfers between devices with their start and end apart: 27, of which 6 were waited for; matrix products, arithmetic and copies ran while one was open for 0% of the time, Pallas kernels for 40%

profile of v2, /device:TPU:0, one launch (start us, length us, event | category | flops | bytes accessed | tf_op | source)
XLA Modules:
  0.0 109.1 jit_solution(6711709530353772245)
XLA Ops:
  2.7 2.1 %right.1 = (f32[16,4096]{1,0:T(8,128)S(1)}, f32[16,2048]{1,0:T(8,128)S(1)}) custom-call(s32[12]{0:T(128)S(1)} %stack.55.scalars, f32[5,8]{1,0:T(8,128)} %pitch.1, f32[5,8]{1,0:T(8,128)S(1)} %collective-permute-done.pitch_other, s32[1,8]{1,0:T(1,128)} %bitcast.31, s32[1,8]{1,0:T(1,128)S(1)} %collective-permute-done.1.modes_other, s32[1,4096]{1,0:T(1,128)} %bitcast.29, ...), custom_call_target="tpu_custom_call" | custom-call | tf_op jit(solution)/shard_map/right/pallas_call | solution.py:405
  5.5 14.6 %adjoint_one.1 = (f32[16,4096]{1,0:T(8,128)}, f32[16,4096]{1,0:T(8,128)}, f32[16,2048]{1,0:T(8,128)}, f32[16,2048]{1,0:T(8,128)}, f32[1,2048]{1,0:T(1,128)}, /*index=5*/bf16[2048,8704]{1,0:T(8,128)(2,1)S(1)}) custom-call(s32[12]{0:T(128)} %copy-done.4, f32[8,4096]{1,0:T(8,128)} %objectives.3, f32[8,4096]{1,0:T(8,128)} %copy-done.14, f32[1,4096]{1,0:T(1,128)} %bitcast.17, ...), custom_call_target="tpu_custom_call" | custom-call | flops 570425344 | bytes 35651584 | tf_op jit(solution)/shard_map/adjoint_one/pallas_call | solution.py:420
  20.1 4.3 %collective-permute-start.5 = (f32[16,4096]{1,0:T(8,128)}, f32[16,4096]{1,0:T(8,128)S(1)}, u32[]{:S(2)}, u32[]{:S(2)}) collective-permute-start(f32[16,4096]{1,0:T(8,128)} %get-tuple-element.71), channel_id=1, source_target_pairs={{0,1},{1,0},{2,3},{3,2},{4,5},{5,4},{6,7},{7,6},{8,9},{9,8},{10,11... | collective-permute-start | bytes 786440 | tf_op jit(solution)/shard_map/ppermute | solution.py:374
  24.5 1.3 %collective-permute-done.5.other = f32[16,4096]{1,0:T(8,128)S(1)} collective-permute-done((f32[16,4096]{1,0:T(8,128)}, f32[16,4096]{1,0:T(8,128)S(1)}, u32[]{:S(2)}, u32[]{:S(2)}) %collective-permute-start.5) | collective-permute-done | bytes 262176 | tf_op jit(solution)/shard_map/ppermute | solution.py:374
  25.8 0.9 copy-done.3
  28.5 1.7 %collective-permute-start.7 = (bf16[16,2048]{1,0:T(8,128)(2,1)S(1)}, bf16[16,2048]{1,0:T(8,128)(2,1)S(1)}, u32[]{:S(2)}, u32[]{:S(2)}) collective-permute-start(bf16[16,2048]{1,0:T(8,128)(2,1)S(1)} %get-tuple-element.76), channel_id=1, source_target_pairs={{0,1},{1,5},{2,9},{3,13},{4,0},{5,4},{6,8},{7,12},{8,3},{9,7},{10,... | collective-permute-start | bytes 196616 | tf_op jit(solution)/shard_map/ppermute | solution.py:472
  30.2 5.5 %collective-permute-start.8 = (bf16[16,2048]{1,0:T(8,128)(2,1)S(1)}, bf16[16,2048]{1,0:T(8,128)(2,1)S(1)}, u32[]{:S(2)}, u32[]{:S(2)}) collective-permute-start(bf16[16,2048]{1,0:T(8,128)(2,1)S(1)} %get-tuple-element.75), channel_id=1, source_target_pairs={{0,2},{1,6},{2,10},{3,14},{4,3},{5,7},{6,11},{7,15},{8,0},{9,4},{1... | collective-permute-start | bytes 196616 | tf_op jit(solution)/shard_map/ppermute | solution.py:472
  36.4 13.1 %forward_one.1.rest_0_ = f32[16,2048]{1,0:T(8,128)} custom-call(s32[12]{0:T(128)} %copy-done.4, s32[1,512]{1,0:T(1,128)} %bitcast.20, s32[1,512]{1,0:T(1,128)} %bitcast.25, bf16[2048,8704]{1,0:T(8,128)(2,1)S(1)} %get-tuple-element.68.held, f32[16,4096]{1,0:T(8,128)} %copy-done.12, f32[16,4096]{1,0:T(8,128)} %copy-done.13), custom_call_target="tpu_custom_call" | custom-call | flops 570425344 | bytes 35651584 | tf_op jit(solution)/shard_map/forward_one/pallas_call | solution.py:448
  49.6 2.6 %collective-permute-start.10 = (f32[16,2048]{1,0:T(8,128)}, f32[16,2048]{1,0:T(8,128)S(1)}, u32[]{:S(2)}, u32[]{:S(2)}) collective-permute-start(f32[16,2048]{1,0:T(8,128)} %forward_one.1.rest_0_), channel_id=1, source_target_pairs={{0,2},{2,0},{1,3},{3,1},{4,6},{6,4},{5,7},{7,5},{8,10},{10,8},{9,1... | collective-permute-start | bytes 393224 | tf_op jit(solution)/shard_map/ppermute | solution.py:377
  52.1 4.8 %adjoint_two_give.1 = (f32[32,2048]{1,0:T(8,128)}, f32[16,2048]{1,0:T(8,128)}, f32[16,512]{1,0:T(8,128)}, f32[8,2048]{1,0:T(8,128)}, f32[8,2048]{1,0:T(8,128)}) custom-call(s32[12]{0:T(128)} %copy-done.4, f32[16,2048]{1,0:T(8,128)} %get-tuple-element.66.previous, f32[16,2048]{1,0:T(8,128)} %get-tuple-element.67.target, ...), custom_call_target="tpu_custom_call" | custom-call | flops 285212672 | bytes 17825792 | tf_op jit(solution)/shard_map/adjoint_two_give/pallas_call | solution.py:476
  58.3 4.6 %collective-permute-start.13 = (bf16[16,2048]{1,0:T(8,128)(2,1)S(1)}, bf16[16,2048]{1,0:T(8,128)(2,1)S(1)}, u32[]{:S(2)}, u32[]{:S(2)}) collective-permute-start(bf16[16,2048]{1,0:T(8,128)(2,1)S(1)} %get-tuple-element.90.ready), channel_id=1, source_target_pairs={{0,8},{1,0},{2,12},{3,4},{4,9},{5,1},{6,13},{7,5},{8,10},{9,2},{10... | collective-permute-start | bytes 196616 | tf_op jit(solution)/shard_map/ppermute | solution.py:510
  62.9 4.3 %adjoint_two_keep.1.keep = f32[32,2048]{1,0:T(8,128)} custom-call(s32[12]{0:T(128)} %copy-done.4, f32[16,2048]{1,0:T(8,128)} %get-tuple-element.88.adjoint, f32[16,512]{1,0:T(8,128)} %get-tuple-element.89.carried, s32[1,512]{1,0:T(1,128)} %bitcast.22, s32[1,512]{1,0:T(1,128)} %bitcast.27, bf16[2048,8704]{1,0:T(8,128)(2,1)S(1)} %get-tuple-element.68.held, ...), custom_call_target="tpu_custom_call" | custom-call | flops 285212672 | bytes 17825792 | tf_op jit(solution)/shard_map/adjoint_two_keep/pallas_call | solution.py:511
  67.8 0.9 copy-done
  70.0 11.4 %forward_two.1.rest_0_ = f32[16,2048]{1,0:T(8,128)} custom-call(s32[12]{0:T(128)} %copy-done.4, s32[1,512]{1,0:T(1,128)} %bitcast.23, s32[1,512]{1,0:T(1,128)} %bitcast.28, bf16[2048,8704]{1,0:T(8,128)(2,1)S(1)} %get-tuple-element.68.held, bf16[16,2048]{1,0:T(8,128)(2,1)} %copy-done.16, bf16[16,2048]{1,0:T(8,128)(2,1)} %copy-done.18, ...), custom_call_target="tpu_custom_call" | custom-call | flops 570425344 | bytes 35651584 | tf_op jit(solution)/shard_map/forward_two/pallas_call | solution.py:448
  81.4 2.2 %collective-permute-start.17 = (f32[16,2048]{1,0:T(8,128)}, f32[16,2048]{1,0:T(8,128)S(1)}, u32[]{:S(2)}, u32[]{:S(2)}) collective-permute-start(f32[16,2048]{1,0:T(8,128)} %forward_two.1.rest_0_), channel_id=1, source_target_pairs={{0,2},{2,0},{1,3},{3,1},{4,6},{6,4},{5,7},{7,5},{8,10},{10,8},{9,1... | collective-permute-start | bytes 393224 | tf_op jit(solution)/shard_map/ppermute | solution.py:377
  84.3 1.8 %collective-permute-start.11 = (f32[16,2048]{1,0:T(8,128)S(1)}, f32[16,2048]{1,0:T(8,128)S(1)}, u32[]{:S(2)}, u32[]{:S(2)}) collective-permute-start(f32[16,2048]{1,0:T(8,128)S(1)} %get-tuple-element.86), channel_id=1, source_target_pairs={{0,1},{1,0},{2,3},{3,2},{4,5},{5,4},{6,7},{7,6},{8,9},{9,8},{10,11... | collective-permute-start | bytes 393224 | tf_op jit(solution)/shard_map/ppermute | solution.py:374
  86.2 3.4 %collective-permute-start.20 = (f32[8,2048]{1,0:T(8,128)S(1)}, f32[8,2048]{1,0:T(8,128)S(1)}, u32[]{:S(2)}, u32[]{:S(2)}) collective-permute-start(f32[8,2048]{1,0:T(8,128)S(1)} %get-tuple-element.109), channel_id=1, source_target_pairs={{0,2},{1,6},{2,10},{3,14},{4,3},{5,7},{6,11},{7,15},{8,0},{9,4},{1... | collective-permute-start | bytes 196616 | tf_op jit(solution)/shard_map/ppermute | solution.py:536
  89.6 2.2 %collective-permute-start.21 = (f32[8,2048]{1,0:T(8,128)S(1)}, f32[8,2048]{1,0:T(8,128)S(1)}, u32[]{:S(2)}, u32[]{:S(2)}) collective-permute-start(f32[8,2048]{1,0:T(8,128)S(1)} %get-tuple-element.110), channel_id=1, source_target_pairs={{0,3},{1,7},{2,11},{3,15},{4,2},{5,6},{6,10},{7,14},{8,1},{9,5},{1... | collective-permute-start | bytes 196616 | tf_op jit(solution)/shard_map/ppermute | solution.py:536
  91.8 0.9 copy-done.1
  92.7 1.5 %system.1 = (f32[16,128]{1,0:T(8,128)S(1)}, f32[16,128]{1,0:T(8,128)S(1)}) custom-call(s32[12]{0:T(128)S(1)} %copy-done.8, f32[16,2048]{1,0:T(8,128)S(1)} %get-tuple-element.60.right_half.basis, f32[16,2048]{1,0:T(8,128)S(1)} %get-tuple-element.87.image, f32[1,2048]{1,0:T(1,128)S(1)} %copy-done.9, f32[16,2048]{1,0:T(8,128)S(1)} %copy-done.1, ...), custom_call_target="tpu_custom_call" | custom-call | tf_op jit(solution)/shard_map/system/pallas_call | solution.py:539
  94.2 4.4 %collective-permute-done.20.rest_2_ = f32[8,2048]{1,0:T(8,128)S(1)} collective-permute-done((f32[8,2048]{1,0:T(8,128)S(1)}, f32[8,2048]{1,0:T(8,128)S(1)}, u32[]{:S(2)}, u32[]{:S(2)}) %collective-permute-start.20) | collective-permute-done | bytes 65568 | tf_op jit(solution)/shard_map/ppermute | solution.py:536
  100.8 3.6 %collective-permute-start.25 = (f32[16,128]{1,0:T(8,128)S(1)}, f32[16,128]{1,0:T(8,128)S(1)}, u32[]{:S(2)}, u32[]{:S(2)}) collective-permute-start(f32[16,128]{1,0:T(8,128)S(1)} %add.26.rest_0_), channel_id=1, source_target_pairs={{0,12},{4,8},{8,4},{12,0},{1,13},{5,9},{9,5},{13,1},{2,14},{6,10},... | collective-permute-start | bytes 24584 | tf_op jit(solution)/shard_map/ppermute | solution.py:549
  104.4 1.6 %update.1 = f32[8,2048]{1,0:T(8,128)} custom-call(s32[12]{0:T(128)S(1)} %copy-done.8, f32[8,2048]{1,0:T(8,128)S(1)} %copy-done.11, f32[8,2048]{1,0:T(8,128)S(1)} %collective-permute-done.26.received, f32[1,4096]{1,0:T(1,128)} %bitcast.18, f32[8,4096]{1,0:T(8,128)} %objectives.3, f32[8,2048]{1,0:T(8,128)S(1)} %collective-permute-done.18.rest_0_, ...), custom_call_target="tpu_custom_call" | custom-call | tf_op jit(solution)/shard_map/update/pallas_call | solution.py:559
  106.3 2.8 %solve.1 = f32[8,2048]{1,0:T(8,128)} custom-call(s32[12]{0:T(128)S(1)} %copy-done.8, f32[16,2048]{1,0:T(8,128)S(1)} %get-tuple-element.85.mine, f32[16,2048]{1,0:T(8,128)S(1)} %collective-permute-done.11.received, f32[16,128]{1,0:T(8,128)S(1)} %add.26.rest_0_, f32[16,128]{1,0:T(8,128)S(1)} %collective-permute-done.23.rest_1_, ...), custom_call_target="tpu_custom_call" | custom-call | tf_op jit(solution)/shard_map/solve/pallas_call | solution.py:550
  (92 shorter events, 11.6 us)
Async XLA Ops:
  0.6 4.1 %collective-permute-start.2 = (f32[8,4096]{1,0:T(8,128)}, f32[8,4096]{1,0:T(8,128)S(1)}, u32[]{:S(2)}, u32[]{:S(2)}) collective-permute-start(f32[8,4096]{1,0:T(8,128)} %objectives.3), channel_id=1, source_target_pairs={{0,1},{1,0},{2,3},{3,2},{4,5},{5,4},{6,7},{7,6},{8,9},{9,8},{10,11... | collective-permute-start | bytes 393224 | tf_op jit(solution)/shard_map/ppermute | solution.py:374
  4.8 19.6 %collective-permute-start.3 = (f32[16,4096]{1,0:T(8,128)S(1)}, f32[16,4096]{1,0:T(8,128)S(1)}, u32[]{:S(2)}, u32[]{:S(2)}) collective-permute-start(f32[16,4096]{1,0:T(8,128)S(1)} %get-tuple-element.64), channel_id=1, source_target_pairs={{0,0},{1,4},{2,8},{3,12},{4,1},{5,5},{6,9},{7,13},{8,2},{9,6},{10,... | collective-permute-start | bytes 786440 | tf_op jit(solution)/shard_map/ppermute | solution.py:418
  20.1 5.7 %collective-permute-start.5 = (f32[16,4096]{1,0:T(8,128)}, f32[16,4096]{1,0:T(8,128)S(1)}, u32[]{:S(2)}, u32[]{:S(2)}) collective-permute-start(f32[16,4096]{1,0:T(8,128)} %get-tuple-element.71), channel_id=1, source_target_pairs={{0,1},{1,0},{2,3},{3,2},{4,5},{5,4},{6,7},{7,6},{8,9},{9,8},{10,11... | collective-permute-start | bytes 786440 | tf_op jit(solution)/shard_map/ppermute | solution.py:374
  24.4 3.5 %collective-permute-start.4 = (f32[16,4096]{1,0:T(8,128)S(1)}, f32[16,4096]{1,0:T(8,128)S(1)}, u32[]{:S(2)}, u32[]{:S(2)}) collective-permute-start(f32[16,4096]{1,0:T(8,128)S(1)} %collective-permute-done.3.rest_0_), channel_id=1, source_target_pairs={{0,1},{1,0},{2,3},{3,2},{4,5},{5,4},{6,7},{7,6},{8,9},{9,8},{10,11... | collective-permute-start | bytes 786440 | tf_op jit(solution)/shard_map/ppermute | solution.py:374
  27.9 21.6 %collective-permute-start.6 = (bf16[16,2048]{1,0:T(8,128)(2,1)S(1)}, bf16[16,2048]{1,0:T(8,128)(2,1)S(1)}, u32[]{:S(2)}, u32[]{:S(2)}) collective-permute-start(bf16[16,2048]{1,0:T(8,128)(2,1)S(1)} %get-tuple-element.75), channel_id=1, source_target_pairs={{0,0},{1,4},{2,8},{3,12},{4,1},{5,5},{6,9},{7,13},{8,2},{9,6},{10,... | collective-permute-start | bytes 196616 | tf_op jit(solution)/shard_map/ppermute | solution.py:472
  28.5 21.0 %collective-permute-start.7 = (bf16[16,2048]{1,0:T(8,128)(2,1)S(1)}, bf16[16,2048]{1,0:T(8,128)(2,1)S(1)}, u32[]{:S(2)}, u32[]{:S(2)}) collective-permute-start(bf16[16,2048]{1,0:T(8,128)(2,1)S(1)} %get-tuple-element.76), channel_id=1, source_target_pairs={{0,1},{1,5},{2,9},{3,13},{4,0},{5,4},{6,8},{7,12},{8,3},{9,7},{10,... | collective-permute-start | bytes 196616 | tf_op jit(solution)/shard_map/ppermute | solution.py:472
  30.2 19.3 %collective-permute-start.8 = (bf16[16,2048]{1,0:T(8,128)(2,1)S(1)}, bf16[16,2048]{1,0:T(8,128)(2,1)S(1)}, u32[]{:S(2)}, u32[]{:S(2)}) collective-permute-start(bf16[16,2048]{1,0:T(8,128)(2,1)S(1)} %get-tuple-element.75), channel_id=1, source_target_pairs={{0,2},{1,6},{2,10},{3,14},{4,3},{5,7},{6,11},{7,15},{8,0},{9,4},{1... | collective-permute-start | bytes 196616 | tf_op jit(solution)/shard_map/ppermute | solution.py:472
  35.8 13.8 %collective-permute-start.9 = (bf16[16,2048]{1,0:T(8,128)(2,1)S(1)}, bf16[16,2048]{1,0:T(8,128)(2,1)S(1)}, u32[]{:S(2)}, u32[]{:S(2)}) collective-permute-start(bf16[16,2048]{1,0:T(8,128)(2,1)S(1)} %get-tuple-element.76), channel_id=1, source_target_pairs={{0,3},{1,7},{2,11},{3,15},{4,2},{5,6},{6,10},{7,14},{8,1},{9,5},{1... | collective-permute-start | bytes 196616 | tf_op jit(solution)/shard_map/ppermute | solution.py:472
  49.6 7.3 %collective-permute-start.10 = (f32[16,2048]{1,0:T(8,128)}, f32[16,2048]{1,0:T(8,128)S(1)}, u32[]{:S(2)}, u32[]{:S(2)}) collective-permute-start(f32[16,2048]{1,0:T(8,128)} %forward_one.1.rest_0_), channel_id=1, source_target_pairs={{0,2},{2,0},{1,3},{3,1},{4,6},{6,4},{5,7},{7,5},{8,10},{10,8},{9,1... | collective-permute-start | bytes 393224 | tf_op jit(solution)/shard_map/ppermute | solution.py:377
  56.9 10.9 %collective-permute-start.16 = (f32[32,2048]{1,0:T(8,128)}, f32[32,2048]{1,0:T(8,128)S(1)}, u32[]{:S(2)}, u32[]{:S(2)}) collective-permute-start(f32[32,2048]{1,0:T(8,128)} %get-tuple-element.94), channel_id=1, source_target_pairs={{0,1},{1,0},{2,3},{3,2},{4,5},{5,4},{6,7},{7,6},{8,9},{9,8},{10,11... | collective-permute-start | bytes 786440 | tf_op jit(solution)/shard_map/ppermute | solution.py:374
  57.6 9.6 %collective-permute-start.12 = (bf16[16,2048]{1,0:T(8,128)(2,1)S(1)}, bf16[16,2048]{1,0:T(8,128)(2,1)S(1)}, u32[]{:S(2)}, u32[]{:S(2)}) collective-permute-start(bf16[16,2048]{1,0:T(8,128)(2,1)S(1)} %get-tuple-element.90.ready), channel_id=1, source_target_pairs={{0,0},{1,8},{2,4},{3,12},{4,1},{5,9},{6,5},{7,13},{8,2},{9,10},{10... | collective-permute-start | bytes 196616 | tf_op jit(solution)/shard_map/ppermute | solution.py:510
  58.3 8.9 %collective-permute-start.13 = (bf16[16,2048]{1,0:T(8,128)(2,1)S(1)}, bf16[16,2048]{1,0:T(8,128)(2,1)S(1)}, u32[]{:S(2)}, u32[]{:S(2)}) collective-permute-start(bf16[16,2048]{1,0:T(8,128)(2,1)S(1)} %get-tuple-element.90.ready), channel_id=1, source_target_pairs={{0,8},{1,0},{2,12},{3,4},{4,9},{5,1},{6,13},{7,5},{8,10},{9,2},{10... | collective-permute-start | bytes 196616 | tf_op jit(solution)/shard_map/ppermute | solution.py:510
  67.2 2.1 %collective-permute-start.14 = (bf16[16,2048]{1,0:T(8,128)(2,1)S(1)}, bf16[16,2048]{1,0:T(8,128)(2,1)S(1)}, u32[]{:S(2)}, u32[]{:S(2)}) collective-permute-start(bf16[16,2048]{1,0:T(8,128)(2,1)S(1)} %collective-permute-done.12.rest_0_), channel_id=1, source_target_pairs={{0,1},{1,0},{2,3},{3,2},{4,5},{5,4},{6,7},{7,6},{8,9},{9,8},{10,11... | collective-permute-start | bytes 196616 | tf_op jit(solution)/shard_map/ppermute | solution.py:374
  67.3 2.1 %collective-permute-start.15 = (bf16[16,2048]{1,0:T(8,128)(2,1)S(1)}, bf16[16,2048]{1,0:T(8,128)(2,1)S(1)}, u32[]{:S(2)}, u32[]{:S(2)}) collective-permute-start(bf16[16,2048]{1,0:T(8,128)(2,1)S(1)} %collective-permute-done.13.rest_1_), channel_id=1, source_target_pairs={{0,1},{1,0},{2,3},{3,2},{4,5},{5,4},{6,7},{7,6},{8,9},{9,8},{10,11... | collective-permute-start | bytes 196616 | tf_op jit(solution)/shard_map/ppermute | solution.py:374
  81.4 10.4 %collective-permute-start.17 = (f32[16,2048]{1,0:T(8,128)}, f32[16,2048]{1,0:T(8,128)S(1)}, u32[]{:S(2)}, u32[]{:S(2)}) collective-permute-start(f32[16,2048]{1,0:T(8,128)} %forward_two.1.rest_0_), channel_id=1, source_target_pairs={{0,2},{2,0},{1,3},{3,1},{4,6},{6,4},{5,7},{7,5},{8,10},{10,8},{9,1... | collective-permute-start | bytes 393224 | tf_op jit(solution)/shard_map/ppermute | solution.py:377
  83.7 5.9 %collective-permute-start.18 = (f32[8,2048]{1,0:T(8,128)S(1)}, f32[8,2048]{1,0:T(8,128)S(1)}, u32[]{:S(2)}, u32[]{:S(2)}) collective-permute-start(f32[8,2048]{1,0:T(8,128)S(1)} %get-tuple-element.107), channel_id=1, source_target_pairs={{0,0},{1,4},{2,8},{3,12},{4,1},{5,5},{6,9},{7,13},{8,2},{9,6},{10,... | collective-permute-start | bytes 196616 | tf_op jit(solution)/shard_map/ppermute | solution.py:536
  84.3 21.7 %collective-permute-start.11 = (f32[16,2048]{1,0:T(8,128)S(1)}, f32[16,2048]{1,0:T(8,128)S(1)}, u32[]{:S(2)}, u32[]{:S(2)}) collective-permute-start(f32[16,2048]{1,0:T(8,128)S(1)} %get-tuple-element.86), channel_id=1, source_target_pairs={{0,1},{1,0},{2,3},{3,2},{4,5},{5,4},{6,7},{7,6},{8,9},{9,8},{10,11... | collective-permute-start | bytes 393224 | tf_op jit(solution)/shard_map/ppermute | solution.py:374
  86.1 8.1 %collective-permute-start.19 = (f32[8,2048]{1,0:T(8,128)S(1)}, f32[8,2048]{1,0:T(8,128)S(1)}, u32[]{:S(2)}, u32[]{:S(2)}) collective-permute-start(f32[8,2048]{1,0:T(8,128)S(1)} %get-tuple-element.108), channel_id=1, source_target_pairs={{0,1},{1,5},{2,9},{3,13},{4,0},{5,4},{6,8},{7,12},{8,3},{9,7},{10,... | collective-permute-start | bytes 196616 | tf_op jit(solution)/shard_map/ppermute | solution.py:536
  86.2 12.4 %collective-permute-start.20 = (f32[8,2048]{1,0:T(8,128)S(1)}, f32[8,2048]{1,0:T(8,128)S(1)}, u32[]{:S(2)}, u32[]{:S(2)}) collective-permute-start(f32[8,2048]{1,0:T(8,128)S(1)} %get-tuple-element.109), channel_id=1, source_target_pairs={{0,2},{1,6},{2,10},{3,14},{4,3},{5,7},{6,11},{7,15},{8,0},{9,4},{1... | collective-permute-start | bytes 196616 | tf_op jit(solution)/shard_map/ppermute | solution.py:536
  89.6 9.0 %collective-permute-start.21 = (f32[8,2048]{1,0:T(8,128)S(1)}, f32[8,2048]{1,0:T(8,128)S(1)}, u32[]{:S(2)}, u32[]{:S(2)}) collective-permute-start(f32[8,2048]{1,0:T(8,128)S(1)} %get-tuple-element.110), channel_id=1, source_target_pairs={{0,3},{1,7},{2,11},{3,15},{4,2},{5,6},{6,10},{7,14},{8,1},{9,5},{1... | collective-permute-start | bytes 196616 | tf_op jit(solution)/shard_map/ppermute | solution.py:536
  91.8 12.5 %collective-permute-start.26 = (f32[8,2048]{1,0:T(8,128)S(1)}, f32[8,2048]{1,0:T(8,128)S(1)}, u32[]{:S(2)}, u32[]{:S(2)}) collective-permute-start(f32[8,2048]{1,0:T(8,128)S(1)} %copy-done.23), channel_id=1, source_target_pairs={{0,1},{1,0},{2,3},{3,2},{4,5},{5,4},{6,7},{7,6},{8,9},{9,8},{10,11... | collective-permute-start | bytes 196616 | tf_op jit(solution)/shard_map/ppermute | solution.py:374
  100.0 6.0 %collective-permute-start.23 = (f32[16,128]{1,0:T(8,128)S(1)}, f32[16,128]{1,0:T(8,128)S(1)}, u32[]{:S(2)}, u32[]{:S(2)}) collective-permute-start(f32[16,128]{1,0:T(8,128)S(1)} %add.26.rest_0_), channel_id=1, source_target_pairs={{0,4},{4,0},{8,12},{12,8},{1,5},{5,1},{9,13},{13,9},{2,6},{6,2},{1... | collective-permute-start | bytes 24584 | tf_op jit(solution)/shard_map/ppermute | solution.py:549
  100.0 6.0 %collective-permute-start.24 = (f32[16,128]{1,0:T(8,128)S(1)}, f32[16,128]{1,0:T(8,128)S(1)}, u32[]{:S(2)}, u32[]{:S(2)}) collective-permute-start(f32[16,128]{1,0:T(8,128)S(1)} %add.26.rest_0_), channel_id=1, source_target_pairs={{0,8},{4,12},{8,0},{12,4},{1,9},{5,13},{9,1},{13,5},{2,10},{6,14},... | collective-permute-start | bytes 24584 | tf_op jit(solution)/shard_map/ppermute | solution.py:549
  100.8 5.4 %collective-permute-start.25 = (f32[16,128]{1,0:T(8,128)S(1)}, f32[16,128]{1,0:T(8,128)S(1)}, u32[]{:S(2)}, u32[]{:S(2)}) collective-permute-start(f32[16,128]{1,0:T(8,128)S(1)} %add.26.rest_0_), channel_id=1, source_target_pairs={{0,12},{4,8},{8,4},{12,0},{1,13},{5,9},{9,5},{13,1},{2,14},{6,10},... | collective-permute-start | bytes 24584 | tf_op jit(solution)/shard_map/ppermute | solution.py:549
  (27 other events, 217.4 us)

commit v3 on v2

--- a/solution.py
+++ b/solution.py
@@ -392,6 +392,7 @@
     scalars = jnp.stack(
         [core, col_index * panels, row_index, span % half, holder, span] + places
     ).astype(jnp.int32)
+    scalars = argument(scalars)
     self_row = argument(self_term[None, :])
     objectives = argument(objectives)
     upper = argument(wake_upper[None, :])
@@ -437,7 +438,7 @@
         cost_estimate=cost(2 * count * half * width, 2 * half * width),
         name="adjoint_one",
     )(
-        scalars, objectives, objectives_other, self_row, upper, lower, influence, wake_influence
+        scalars, objectives, argument(objectives_other), self_row, upper, lower, influence, wake_influence
     )
     right_near, start = lax.optimization_barrier((right_near, start))
     right_far = swap(right_near)
@@ -454,7 +455,7 @@
             compiler_params=params(),
             cost_estimate=cost(2 * count * half * width, 2 * half * width),
             name=name,
-        )(scalars, upper, lower, held, *shards)
+        )(scalars, upper, lower, held, *map(keep_in_vmem, shards))
 
     sends = pl.pallas_call(
         combine_kernel,
@@ -463,7 +464,7 @@
         out_shape=[struct((count, half), BF16)] * 2,
         compiler_params=params(4),
         name="combine",
-    )(scalars, keep, swap(give))
+    )(scalars, argument(keep), swap(give))
 
     right_far, *sends = lax.optimization_barrier((right_far, *sends))
     induced = forward(
@@ -489,7 +490,7 @@
         name="adjoint_two_give",
     )(
         scalars, start, target, self_half, upper, lower, held,
-        *parts,
+        *map(keep_in_vmem, parts),
     )
     induced = cols_parts(induced)
     give, *induced = lax.optimization_barrier((give, *induced))
@@ -516,7 +517,7 @@
         compiler_params=params(),
         cost_estimate=cost(count * half * width, half * width),
         name="adjoint_two_keep",
-    )(scalars, adjoint, carried, upper, lower, held, image_rounded)
+    )(scalars, adjoint, carried, upper, lower, held, keep_in_vmem(image_rounded))
 
     keep, *shards = lax.optimization_barrier((keep, *shards))
     shards = shards + [swap(value) for value in shards]
@@ -527,7 +528,7 @@
         out_shape=[struct((BLOCK, out_width), F32)] * side,
         compiler_params=params(4),
         name="collect",
-    )(scalars, keep, give)
+    )(scalars, argument(keep), give)
     *shards, first_total = lax.optimization_barrier((*shards, totals[0]))
     totals = [first_total, *totals[1:]]
     induced = forward(tuple(CHUNKS + i for i in range(4)), shards, False, "forward_two")

time: 110 us -> 107 us (0.973)
  local copies, waits for them, and re-layouts: 4.13 us -> 1.53 us
    unnamed x48 -> x12, local copies, waits for them, and re-layouts: 4.05 us -> 0.92 us
  transfers between devices with their start and end apart: 27 -> 27, of which waited for: 6 -> 6; matrix products, arithmetic and copies ran while one was open for 0% -> 1% of each run, Pallas kernels for 40% -> 42%
where the time goes in v3:
time: 107 us; the launch traced here: 106 us
  Pallas kernels  58.3 us (54%)
  starting transfers between devices  38.4 us (36%)
  waiting for transfers between devices  7.28 us (7%)
  local copies, waits for them, and re-layouts  1.53 us (1%)
    pallas_call x2, Pallas kernels, forward(): pl.pallas_call(functools.partial(forward_kernel, 512, places, split), in_...  24 us
    pallas_call x1, Pallas kernels, per_device(): pl.pallas_call(functools.partial(load_adjoint_kernel, chunk), in_specs=[S...  14.6 us
    ppermute x4, starting transfers between devices, per_device(): parts = [lax.ppermute(sends[k % 2], GRID, cross(k)) for k in range(side)]  8.48 us
    ppermute x11, starting transfers between devices, swap(): return lax.ppermute(value, 'rhs', flip(1, 2))  8.46 us
    ppermute x4, starting transfers between devices, per_device(): totals = [lax.ppermute(totals[k], GRID, cross(k)) for k in range(side)]  6.33 us
    ppermute x2, starting transfers between devices, per_device(): shards = [lax.ppermute(image_rounded, GRID, fetch(j)) for j in range(2)]  5.3 us
    ppermute x2, starting transfers between devices, cols_parts(): lax.ppermute(value, 'cols', flip(k, n_cols))  4.74 us
    pallas_call x1, Pallas kernels, per_device(): pl.pallas_call(functools.partial(adjoint_give_kernel, tile, len(parts)),...  4.62 us
  transfers between devices with their start and end apart: 27, of which 6 were waited for; matrix products, arithmetic and copies ran while one was open for 1% of the time, Pallas kernels for 42%

profile of v3, /device:TPU:0, one launch (start us, length us, event | category | flops | bytes accessed | tf_op | source)
XLA Modules:
  0.0 106.3 jit_solution(15732592170479739052)
XLA Ops:
  2.7 2.1 %right.1 = (f32[16,4096]{1,0:T(8,128)S(1)}, f32[16,2048]{1,0:T(8,128)S(1)}) custom-call(s32[12]{0:T(128)} %stack.55.scalars, f32[5,8]{1,0:T(8,128)} %pitch.1, f32[5,8]{1,0:T(8,128)S(1)} %collective-permute-done.pitch_other, s32[1,8]{1,0:T(1,128)} %bitcast.31, s32[1,8]{1,0:T(1,128)S(1)} %collective-permute-done.1.modes_other, s32[1,4096]{1,0:T(1,128)} %bitcast.29, ...), custom_call_target="tpu_custom_call" | custom-call | tf_op jit(solution)/shard_map/right/pallas_call | solution.py:406
  5.5 14.6 %adjoint_one.1 = (f32[16,4096]{1,0:T(8,128)}, f32[16,4096]{1,0:T(8,128)}, f32[16,2048]{1,0:T(8,128)}, f32[16,2048]{1,0:T(8,128)}, f32[1,2048]{1,0:T(1,128)}, /*index=5*/bf16[2048,8704]{1,0:T(8,128)(2,1)S(1)}) custom-call(s32[12]{0:T(128)} %stack.55.scalars, f32[8,4096]{1,0:T(8,128)} %objectives.3, f32[8,4096]{1,0:T(8,128)} %copy-done.4, f32[1,4096]{1,0:T(1,128)} %bitcast.17, ...), custom_call_target="tpu_custom_call" | custom-call | flops 570425344 | bytes 35651584 | tf_op jit(solution)/shard_map/adjoint_one/pallas_call | solution.py:421
  20.0 4.3 %collective-permute-start.5 = (f32[16,4096]{1,0:T(8,128)}, f32[16,4096]{1,0:T(8,128)S(1)}, u32[]{:S(2)}, u32[]{:S(2)}) collective-permute-start(f32[16,4096]{1,0:T(8,128)} %get-tuple-element.71), channel_id=1, source_target_pairs={{0,1},{1,0},{2,3},{3,2},{4,5},{5,4},{6,7},{7,6},{8,9},{9,8},{10,11... | collective-permute-start | bytes 786440 | tf_op jit(solution)/shard_map/ppermute | solution.py:374
  24.5 1.3 %collective-permute-done.5.other = f32[16,4096]{1,0:T(8,128)S(1)} collective-permute-done((f32[16,4096]{1,0:T(8,128)}, f32[16,4096]{1,0:T(8,128)S(1)}, u32[]{:S(2)}, u32[]{:S(2)}) %collective-permute-start.5) | collective-permute-done | bytes 262176 | tf_op jit(solution)/shard_map/ppermute | solution.py:374
  25.7 1.0 combine.1
  27.4 1.7 %collective-permute-start.7 = (bf16[16,2048]{1,0:T(8,128)(2,1)S(1)}, bf16[16,2048]{1,0:T(8,128)(2,1)S(1)}, u32[]{:S(2)}, u32[]{:S(2)}) collective-permute-start(bf16[16,2048]{1,0:T(8,128)(2,1)S(1)} %get-tuple-element.76), channel_id=1, source_target_pairs={{0,1},{1,5},{2,9},{3,13},{4,0},{5,4},{6,8},{7,12},{8,3},{9,7},{10,... | collective-permute-start | bytes 196616 | tf_op jit(solution)/shard_map/ppermute | solution.py:473
  29.1 5.5 %collective-permute-start.8 = (bf16[16,2048]{1,0:T(8,128)(2,1)S(1)}, bf16[16,2048]{1,0:T(8,128)(2,1)S(1)}, u32[]{:S(2)}, u32[]{:S(2)}) collective-permute-start(bf16[16,2048]{1,0:T(8,128)(2,1)S(1)} %get-tuple-element.75), channel_id=1, source_target_pairs={{0,2},{1,6},{2,10},{3,14},{4,3},{5,7},{6,11},{7,15},{8,0},{9,4},{1... | collective-permute-start | bytes 196616 | tf_op jit(solution)/shard_map/ppermute | solution.py:473
  35.2 12.8 %forward_one.1.rest_0_ = f32[16,2048]{1,0:T(8,128)} custom-call(s32[12]{0:T(128)} %stack.55.scalars, s32[1,512]{1,0:T(1,128)} %bitcast.20, s32[1,512]{1,0:T(1,128)} %bitcast.25, bf16[2048,8704]{1,0:T(8,128)(2,1)S(1)} %get-tuple-element.68.held, f32[16,4096]{1,0:T(8,128)S(1)} %collective-permute-done.3.rest_0_, f32[16,4096]{1,0:T(8,128)S(1)} %collective-permute-done.4.rest_1_), custom_call_target="tpu_custom_call" | custom-call | flops 570425344 | bytes 35651584 | tf_op jit(solution)/shard_map/forward_one/pallas_call | solution.py:449
  48.1 2.6 %collective-permute-start.10 = (f32[16,2048]{1,0:T(8,128)}, f32[16,2048]{1,0:T(8,128)S(1)}, u32[]{:S(2)}, u32[]{:S(2)}) collective-permute-start(f32[16,2048]{1,0:T(8,128)} %forward_one.1.rest_0_), channel_id=1, source_target_pairs={{0,2},{2,0},{1,3},{3,1},{4,6},{6,4},{5,7},{7,5},{8,10},{10,8},{9,1... | collective-permute-start | bytes 393224 | tf_op jit(solution)/shard_map/ppermute | solution.py:377
  50.6 4.6 %adjoint_two_give.1 = (f32[32,2048]{1,0:T(8,128)}, f32[16,2048]{1,0:T(8,128)}, f32[16,512]{1,0:T(8,128)}, f32[8,2048]{1,0:T(8,128)}, f32[8,2048]{1,0:T(8,128)}) custom-call(s32[12]{0:T(128)} %stack.55.scalars, f32[16,2048]{1,0:T(8,128)} %get-tuple-element.66.previous, f32[16,2048]{1,0:T(8,128)} %get-tuple-element.67.target, ...), custom_call_target="tpu_custom_call" | custom-call | flops 285212672 | bytes 17825792 | tf_op jit(solution)/shard_map/adjoint_two_give/pallas_call | solution.py:477
  56.8 4.6 %collective-permute-start.13 = (bf16[16,2048]{1,0:T(8,128)(2,1)S(1)}, bf16[16,2048]{1,0:T(8,128)(2,1)S(1)}, u32[]{:S(2)}, u32[]{:S(2)}) collective-permute-start(bf16[16,2048]{1,0:T(8,128)(2,1)S(1)} %get-tuple-element.90.ready), channel_id=1, source_target_pairs={{0,8},{1,0},{2,12},{3,4},{4,9},{5,1},{6,13},{7,5},{8,10},{9,2},{10... | collective-permute-start | bytes 196616 | tf_op jit(solution)/shard_map/ppermute | solution.py:511
  61.4 4.3 %adjoint_two_keep.1.keep = f32[32,2048]{1,0:T(8,128)} custom-call(s32[12]{0:T(128)} %stack.55.scalars, f32[16,2048]{1,0:T(8,128)} %get-tuple-element.88.adjoint, f32[16,512]{1,0:T(8,128)} %get-tuple-element.89.carried, s32[1,512]{1,0:T(1,128)} %bitcast.22, s32[1,512]{1,0:T(1,128)} %bitcast.27, bf16[2048,8704]{1,0:T(8,128)(2,1)S(1)} %get-tuple-element.68.held, ...), custom_call_target="tpu_custom_call" | custom-call | flops 285212672 | bytes 17825792 | tf_op jit(solution)/shard_map/adjoint_two_keep/pallas_call | solution.py:512
  66.3 1.0 collect.1
  67.3 11.2 %forward_two.1.rest_0_ = f32[16,2048]{1,0:T(8,128)} custom-call(s32[12]{0:T(128)} %stack.55.scalars, s32[1,512]{1,0:T(1,128)} %bitcast.23, s32[1,512]{1,0:T(1,128)} %bitcast.28, bf16[2048,8704]{1,0:T(8,128)(2,1)S(1)} %get-tuple-element.68.held, bf16[16,2048]{1,0:T(8,128)(2,1)S(1)} %collective-permute-done.12.rest_0_, ...), custom_call_target="tpu_custom_call" | custom-call | flops 570425344 | bytes 35651584 | tf_op jit(solution)/shard_map/forward_two/pallas_call | solution.py:449
  78.5 2.2 %collective-permute-start.17 = (f32[16,2048]{1,0:T(8,128)}, f32[16,2048]{1,0:T(8,128)S(1)}, u32[]{:S(2)}, u32[]{:S(2)}) collective-permute-start(f32[16,2048]{1,0:T(8,128)} %forward_two.1.rest_0_), channel_id=1, source_target_pairs={{0,2},{2,0},{1,3},{3,1},{4,6},{6,4},{5,7},{7,5},{8,10},{10,8},{9,1... | collective-permute-start | bytes 393224 | tf_op jit(solution)/shard_map/ppermute | solution.py:377
  81.3 1.9 %collective-permute-start.11 = (f32[16,2048]{1,0:T(8,128)S(1)}, f32[16,2048]{1,0:T(8,128)S(1)}, u32[]{:S(2)}, u32[]{:S(2)}) collective-permute-start(f32[16,2048]{1,0:T(8,128)S(1)} %get-tuple-element.86), channel_id=1, source_target_pairs={{0,1},{1,0},{2,3},{3,2},{4,5},{5,4},{6,7},{7,6},{8,9},{9,8},{10,11... | collective-permute-start | bytes 393224 | tf_op jit(solution)/shard_map/ppermute | solution.py:374
  83.2 3.3 %collective-permute-start.20 = (f32[8,2048]{1,0:T(8,128)S(1)}, f32[8,2048]{1,0:T(8,128)S(1)}, u32[]{:S(2)}, u32[]{:S(2)}) collective-permute-start(f32[8,2048]{1,0:T(8,128)S(1)} %get-tuple-element.109), channel_id=1, source_target_pairs={{0,2},{1,6},{2,10},{3,14},{4,3},{5,7},{6,11},{7,15},{8,0},{9,4},{1... | collective-permute-start | bytes 196616 | tf_op jit(solution)/shard_map/ppermute | solution.py:537
  86.6 2.3 %collective-permute-start.21 = (f32[8,2048]{1,0:T(8,128)S(1)}, f32[8,2048]{1,0:T(8,128)S(1)}, u32[]{:S(2)}, u32[]{:S(2)}) collective-permute-start(f32[8,2048]{1,0:T(8,128)S(1)} %get-tuple-element.110), channel_id=1, source_target_pairs={{0,3},{1,7},{2,11},{3,15},{4,2},{5,6},{6,10},{7,14},{8,1},{9,5},{1... | collective-permute-start | bytes 196616 | tf_op jit(solution)/shard_map/ppermute | solution.py:537
  89.7 1.6 %system.1 = (f32[16,128]{1,0:T(8,128)S(1)}, f32[16,128]{1,0:T(8,128)S(1)}) custom-call(s32[12]{0:T(128)} %stack.55.scalars, f32[16,2048]{1,0:T(8,128)S(1)} %get-tuple-element.60.right_half.basis, f32[16,2048]{1,0:T(8,128)S(1)} %get-tuple-element.87.image, f32[1,2048]{1,0:T(1,128)S(1)} %copy-done.2, f32[16,2048]{1,0:T(8,128)S(1)} %copy-done, ...), custom_call_target="tpu_custom_call" | custom-call | tf_op jit(solution)/shard_map/system/pallas_call | solution.py:540
  91.3 4.3 %collective-permute-done.20.rest_2_ = f32[8,2048]{1,0:T(8,128)S(1)} collective-permute-done((f32[8,2048]{1,0:T(8,128)S(1)}, f32[8,2048]{1,0:T(8,128)S(1)}, u32[]{:S(2)}, u32[]{:S(2)}) %collective-permute-start.20) | collective-permute-done | bytes 65568 | tf_op jit(solution)/shard_map/ppermute | solution.py:537
  97.0 1.0 collective-permute-start.24
  97.9 3.4 %collective-permute-start.25 = (f32[16,128]{1,0:T(8,128)S(1)}, f32[16,128]{1,0:T(8,128)S(1)}, u32[]{:S(2)}, u32[]{:S(2)}) collective-permute-start(f32[16,128]{1,0:T(8,128)S(1)} %add.26.rest_0_), channel_id=1, source_target_pairs={{0,12},{4,8},{8,4},{12,0},{1,13},{5,9},{9,5},{13,1},{2,14},{6,10},... | collective-permute-start | bytes 24584 | tf_op jit(solution)/shard_map/ppermute | solution.py:550
  101.4 1.6 %update.1 = f32[8,2048]{1,0:T(8,128)} custom-call(s32[12]{0:T(128)} %stack.55.scalars, f32[8,2048]{1,0:T(8,128)S(1)} %copy-done.3, f32[8,2048]{1,0:T(8,128)S(1)} %collective-permute-done.26.received, f32[1,4096]{1,0:T(1,128)} %bitcast.18, f32[8,4096]{1,0:T(8,128)} %objectives.3, f32[8,2048]{1,0:T(8,128)S(1)} %collective-permute-done.18.rest_0_, ...), custom_call_target="tpu_custom_call" | custom-call | tf_op jit(solution)/shard_map/update/pallas_call | solution.py:560
  103.4 2.9 %solve.1 = f32[8,2048]{1,0:T(8,128)} custom-call(s32[12]{0:T(128)} %stack.55.scalars, f32[16,2048]{1,0:T(8,128)S(1)} %get-tuple-element.85.mine, f32[16,2048]{1,0:T(8,128)S(1)} %collective-permute-done.11.received, f32[16,128]{1,0:T(8,128)S(1)} %add.26.rest_0_, f32[16,128]{1,0:T(8,128)S(1)} %collective-permute-done.23.rest_1_, ...), custom_call_target="tpu_custom_call" | custom-call | tf_op jit(solution)/shard_map/solve/pallas_call | solution.py:551
  (56 shorter events, 9.6 us)
Async XLA Ops:
  0.6 4.1 %collective-permute-start.2 = (f32[8,4096]{1,0:T(8,128)}, f32[8,4096]{1,0:T(8,128)S(1)}, u32[]{:S(2)}, u32[]{:S(2)}) collective-permute-start(f32[8,4096]{1,0:T(8,128)} %objectives.3), channel_id=1, source_target_pairs={{0,1},{1,0},{2,3},{3,2},{4,5},{5,4},{6,7},{7,6},{8,9},{9,8},{10,11... | collective-permute-start | bytes 393224 | tf_op jit(solution)/shard_map/ppermute | solution.py:374
  4.8 19.6 %collective-permute-start.3 = (f32[16,4096]{1,0:T(8,128)S(1)}, f32[16,4096]{1,0:T(8,128)S(1)}, u32[]{:S(2)}, u32[]{:S(2)}) collective-permute-start(f32[16,4096]{1,0:T(8,128)S(1)} %get-tuple-element.64), channel_id=1, source_target_pairs={{0,0},{1,4},{2,8},{3,12},{4,1},{5,5},{6,9},{7,13},{8,2},{9,6},{10,... | collective-permute-start | bytes 786440 | tf_op jit(solution)/shard_map/ppermute | solution.py:419
  20.0 5.7 %collective-permute-start.5 = (f32[16,4096]{1,0:T(8,128)}, f32[16,4096]{1,0:T(8,128)S(1)}, u32[]{:S(2)}, u32[]{:S(2)}) collective-permute-start(f32[16,4096]{1,0:T(8,128)} %get-tuple-element.71), channel_id=1, source_target_pairs={{0,1},{1,0},{2,3},{3,2},{4,5},{5,4},{6,7},{7,6},{8,9},{9,8},{10,11... | collective-permute-start | bytes 786440 | tf_op jit(solution)/shard_map/ppermute | solution.py:374
  24.4 2.4 %collective-permute-start.4 = (f32[16,4096]{1,0:T(8,128)S(1)}, f32[16,4096]{1,0:T(8,128)S(1)}, u32[]{:S(2)}, u32[]{:S(2)}) collective-permute-start(f32[16,4096]{1,0:T(8,128)S(1)} %collective-permute-done.3.rest_0_), channel_id=1, source_target_pairs={{0,1},{1,0},{2,3},{3,2},{4,5},{5,4},{6,7},{7,6},{8,9},{9,8},{10,11... | collective-permute-start | bytes 786440 | tf_op jit(solution)/shard_map/ppermute | solution.py:374
  26.8 21.3 %collective-permute-start.6 = (bf16[16,2048]{1,0:T(8,128)(2,1)S(1)}, bf16[16,2048]{1,0:T(8,128)(2,1)S(1)}, u32[]{:S(2)}, u32[]{:S(2)}) collective-permute-start(bf16[16,2048]{1,0:T(8,128)(2,1)S(1)} %get-tuple-element.75), channel_id=1, source_target_pairs={{0,0},{1,4},{2,8},{3,12},{4,1},{5,5},{6,9},{7,13},{8,2},{9,6},{10,... | collective-permute-start | bytes 196616 | tf_op jit(solution)/shard_map/ppermute | solution.py:473
  27.4 20.6 %collective-permute-start.7 = (bf16[16,2048]{1,0:T(8,128)(2,1)S(1)}, bf16[16,2048]{1,0:T(8,128)(2,1)S(1)}, u32[]{:S(2)}, u32[]{:S(2)}) collective-permute-start(bf16[16,2048]{1,0:T(8,128)(2,1)S(1)} %get-tuple-element.76), channel_id=1, source_target_pairs={{0,1},{1,5},{2,9},{3,13},{4,0},{5,4},{6,8},{7,12},{8,3},{9,7},{10,... | collective-permute-start | bytes 196616 | tf_op jit(solution)/shard_map/ppermute | solution.py:473
  29.1 18.9 %collective-permute-start.8 = (bf16[16,2048]{1,0:T(8,128)(2,1)S(1)}, bf16[16,2048]{1,0:T(8,128)(2,1)S(1)}, u32[]{:S(2)}, u32[]{:S(2)}) collective-permute-start(bf16[16,2048]{1,0:T(8,128)(2,1)S(1)} %get-tuple-element.75), channel_id=1, source_target_pairs={{0,2},{1,6},{2,10},{3,14},{4,3},{5,7},{6,11},{7,15},{8,0},{9,4},{1... | collective-permute-start | bytes 196616 | tf_op jit(solution)/shard_map/ppermute | solution.py:473
  34.6 13.4 %collective-permute-start.9 = (bf16[16,2048]{1,0:T(8,128)(2,1)S(1)}, bf16[16,2048]{1,0:T(8,128)(2,1)S(1)}, u32[]{:S(2)}, u32[]{:S(2)}) collective-permute-start(bf16[16,2048]{1,0:T(8,128)(2,1)S(1)} %get-tuple-element.76), channel_id=1, source_target_pairs={{0,3},{1,7},{2,11},{3,15},{4,2},{5,6},{6,10},{7,14},{8,1},{9,5},{1... | collective-permute-start | bytes 196616 | tf_op jit(solution)/shard_map/ppermute | solution.py:473
  48.1 7.2 %collective-permute-start.10 = (f32[16,2048]{1,0:T(8,128)}, f32[16,2048]{1,0:T(8,128)S(1)}, u32[]{:S(2)}, u32[]{:S(2)}) collective-permute-start(f32[16,2048]{1,0:T(8,128)} %forward_one.1.rest_0_), channel_id=1, source_target_pairs={{0,2},{2,0},{1,3},{3,1},{4,6},{6,4},{5,7},{7,5},{8,10},{10,8},{9,1... | collective-permute-start | bytes 393224 | tf_op jit(solution)/shard_map/ppermute | solution.py:377
  55.3 11.0 %collective-permute-start.16 = (f32[32,2048]{1,0:T(8,128)}, f32[32,2048]{1,0:T(8,128)S(1)}, u32[]{:S(2)}, u32[]{:S(2)}) collective-permute-start(f32[32,2048]{1,0:T(8,128)} %get-tuple-element.94), channel_id=1, source_target_pairs={{0,1},{1,0},{2,3},{3,2},{4,5},{5,4},{6,7},{7,6},{8,9},{9,8},{10,11... | collective-permute-start | bytes 786440 | tf_op jit(solution)/shard_map/ppermute | solution.py:374
  56.1 9.6 %collective-permute-start.12 = (bf16[16,2048]{1,0:T(8,128)(2,1)S(1)}, bf16[16,2048]{1,0:T(8,128)(2,1)S(1)}, u32[]{:S(2)}, u32[]{:S(2)}) collective-permute-start(bf16[16,2048]{1,0:T(8,128)(2,1)S(1)} %get-tuple-element.90.ready), channel_id=1, source_target_pairs={{0,0},{1,8},{2,4},{3,12},{4,1},{5,9},{6,5},{7,13},{8,2},{9,10},{10... | collective-permute-start | bytes 196616 | tf_op jit(solution)/shard_map/ppermute | solution.py:511
  56.8 8.9 %collective-permute-start.13 = (bf16[16,2048]{1,0:T(8,128)(2,1)S(1)}, bf16[16,2048]{1,0:T(8,128)(2,1)S(1)}, u32[]{:S(2)}, u32[]{:S(2)}) collective-permute-start(bf16[16,2048]{1,0:T(8,128)(2,1)S(1)} %get-tuple-element.90.ready), channel_id=1, source_target_pairs={{0,8},{1,0},{2,12},{3,4},{4,9},{5,1},{6,13},{7,5},{8,10},{9,2},{10... | collective-permute-start | bytes 196616 | tf_op jit(solution)/shard_map/ppermute | solution.py:511
  65.7 1.6 %collective-permute-start.14 = (bf16[16,2048]{1,0:T(8,128)(2,1)S(1)}, bf16[16,2048]{1,0:T(8,128)(2,1)S(1)}, u32[]{:S(2)}, u32[]{:S(2)}) collective-permute-start(bf16[16,2048]{1,0:T(8,128)(2,1)S(1)} %collective-permute-done.12.rest_0_), channel_id=1, source_target_pairs={{0,1},{1,0},{2,3},{3,2},{4,5},{5,4},{6,7},{7,6},{8,9},{9,8},{10,11... | collective-permute-start | bytes 196616 | tf_op jit(solution)/shard_map/ppermute | solution.py:374
  65.8 1.5 %collective-permute-start.15 = (bf16[16,2048]{1,0:T(8,128)(2,1)S(1)}, bf16[16,2048]{1,0:T(8,128)(2,1)S(1)}, u32[]{:S(2)}, u32[]{:S(2)}) collective-permute-start(bf16[16,2048]{1,0:T(8,128)(2,1)S(1)} %collective-permute-done.13.rest_1_), channel_id=1, source_target_pairs={{0,1},{1,0},{2,3},{3,2},{4,5},{5,4},{6,7},{7,6},{8,9},{9,8},{10,11... | collective-permute-start | bytes 196616 | tf_op jit(solution)/shard_map/ppermute | solution.py:374
  78.5 10.4 %collective-permute-start.17 = (f32[16,2048]{1,0:T(8,128)}, f32[16,2048]{1,0:T(8,128)S(1)}, u32[]{:S(2)}, u32[]{:S(2)}) collective-permute-start(f32[16,2048]{1,0:T(8,128)} %forward_two.1.rest_0_), channel_id=1, source_target_pairs={{0,2},{2,0},{1,3},{3,1},{4,6},{6,4},{5,7},{7,5},{8,10},{10,8},{9,1... | collective-permute-start | bytes 393224 | tf_op jit(solution)/shard_map/ppermute | solution.py:377
  80.6 5.9 %collective-permute-start.18 = (f32[8,2048]{1,0:T(8,128)S(1)}, f32[8,2048]{1,0:T(8,128)S(1)}, u32[]{:S(2)}, u32[]{:S(2)}) collective-permute-start(f32[8,2048]{1,0:T(8,128)S(1)} %get-tuple-element.107), channel_id=1, source_target_pairs={{0,0},{1,4},{2,8},{3,12},{4,1},{5,5},{6,9},{7,13},{8,2},{9,6},{10,... | collective-permute-start | bytes 196616 | tf_op jit(solution)/shard_map/ppermute | solution.py:537
  81.3 21.7 %collective-permute-start.11 = (f32[16,2048]{1,0:T(8,128)S(1)}, f32[16,2048]{1,0:T(8,128)S(1)}, u32[]{:S(2)}, u32[]{:S(2)}) collective-permute-start(f32[16,2048]{1,0:T(8,128)S(1)} %get-tuple-element.86), channel_id=1, source_target_pairs={{0,1},{1,0},{2,3},{3,2},{4,5},{5,4},{6,7},{7,6},{8,9},{9,8},{10,11... | collective-permute-start | bytes 393224 | tf_op jit(solution)/shard_map/ppermute | solution.py:374
  83.1 8.2 %collective-permute-start.19 = (f32[8,2048]{1,0:T(8,128)S(1)}, f32[8,2048]{1,0:T(8,128)S(1)}, u32[]{:S(2)}, u32[]{:S(2)}) collective-permute-start(f32[8,2048]{1,0:T(8,128)S(1)} %get-tuple-element.108), channel_id=1, source_target_pairs={{0,1},{1,5},{2,9},{3,13},{4,0},{5,4},{6,8},{7,12},{8,3},{9,7},{10,... | collective-permute-start | bytes 196616 | tf_op jit(solution)/shard_map/ppermute | solution.py:537
  83.2 12.4 %collective-permute-start.20 = (f32[8,2048]{1,0:T(8,128)S(1)}, f32[8,2048]{1,0:T(8,128)S(1)}, u32[]{:S(2)}, u32[]{:S(2)}) collective-permute-start(f32[8,2048]{1,0:T(8,128)S(1)} %get-tuple-element.109), channel_id=1, source_target_pairs={{0,2},{1,6},{2,10},{3,14},{4,3},{5,7},{6,11},{7,15},{8,0},{9,4},{1... | collective-permute-start | bytes 196616 | tf_op jit(solution)/shard_map/ppermute | solution.py:537
  86.6 9.1 %collective-permute-start.21 = (f32[8,2048]{1,0:T(8,128)S(1)}, f32[8,2048]{1,0:T(8,128)S(1)}, u32[]{:S(2)}, u32[]{:S(2)}) collective-permute-start(f32[8,2048]{1,0:T(8,128)S(1)} %get-tuple-element.110), channel_id=1, source_target_pairs={{0,3},{1,7},{2,11},{3,15},{4,2},{5,6},{6,10},{7,14},{8,1},{9,5},{1... | collective-permute-start | bytes 196616 | tf_op jit(solution)/shard_map/ppermute | solution.py:537
  88.8 12.5 %collective-permute-start.26 = (f32[8,2048]{1,0:T(8,128)S(1)}, f32[8,2048]{1,0:T(8,128)S(1)}, u32[]{:S(2)}, u32[]{:S(2)}) collective-permute-start(f32[8,2048]{1,0:T(8,128)S(1)} %copy-done.5), channel_id=1, source_target_pairs={{0,1},{1,0},{2,3},{3,2},{4,5},{5,4},{6,7},{7,6},{8,9},{9,8},{10,11... | collective-permute-start | bytes 196616 | tf_op jit(solution)/shard_map/ppermute | solution.py:374
  97.0 6.0 %collective-permute-start.23 = (f32[16,128]{1,0:T(8,128)S(1)}, f32[16,128]{1,0:T(8,128)S(1)}, u32[]{:S(2)}, u32[]{:S(2)}) collective-permute-start(f32[16,128]{1,0:T(8,128)S(1)} %add.26.rest_0_), channel_id=1, source_target_pairs={{0,4},{4,0},{8,12},{12,8},{1,5},{5,1},{9,13},{13,9},{2,6},{6,2},{1... | collective-permute-start | bytes 24584 | tf_op jit(solution)/shard_map/ppermute | solution.py:550
  97.0 6.0 %collective-permute-start.24 = (f32[16,128]{1,0:T(8,128)S(1)}, f32[16,128]{1,0:T(8,128)S(1)}, u32[]{:S(2)}, u32[]{:S(2)}) collective-permute-start(f32[16,128]{1,0:T(8,128)S(1)} %add.26.rest_0_), channel_id=1, source_target_pairs={{0,8},{4,12},{8,0},{12,4},{1,9},{5,13},{9,1},{13,5},{2,10},{6,14},... | collective-permute-start | bytes 24584 | tf_op jit(solution)/shard_map/ppermute | solution.py:550
  97.9 5.4 %collective-permute-start.25 = (f32[16,128]{1,0:T(8,128)S(1)}, f32[16,128]{1,0:T(8,128)S(1)}, u32[]{:S(2)}, u32[]{:S(2)}) collective-permute-start(f32[16,128]{1,0:T(8,128)S(1)} %add.26.rest_0_), channel_id=1, source_target_pairs={{0,12},{4,8},{8,4},{12,0},{1,13},{5,9},{9,5},{13,1},{2,14},{6,10},... | collective-permute-start | bytes 24584 | tf_op jit(solution)/shard_map/ppermute | solution.py:550
  (9 other events, 100.5 us)

commit v4 on v3

--- a/solution.py
+++ b/solution.py
@@ -66,23 +66,6 @@
     first = jnp.where(core == 0, own, other)
     second = jnp.where(core == 0, other, own)
     return jnp.concatenate([first, second], axis=0)
-
-
-def load_copies(influence, wake, held, sems, first, chunk):
-    def copies(i):
-        source = pl.ds(pl.multiple_of(first + i * chunk, 16), chunk)
-        target = pl.ds(i * chunk, chunk)
-        panels = influence.shape[1]
-        return (
-            pltpu.make_async_copy(
-                influence.at[source], held.at[target, pl.ds(0, panels)], sems.at[0, i]
-            ),
-            pltpu.make_async_copy(
-                wake.at[source], held.at[target, pl.ds(panels, wake.shape[1])], sems.at[1, i]
-            ),
-        )
-
-    return copies
 
 
 def right_kernel(
@@ -112,36 +95,46 @@
 
 
 def load_adjoint_kernel(
-    chunk, scalars, objectives, objectives_other, self_term, upper, lower, influence, wake,
+    cuts, scalars, objectives, objectives_other, self_term, upper, lower, influence, wake,
     keep, give, start, target, self_half, held, whole, sems
 ):
     half = start.shape[1]
     piece = keep.shape[1]
     panels = 2 * piece
     core = scalars[CORE]
-    copies = load_copies(influence, wake, held, sems, core * half, chunk)
-    steps = held.shape[0] // chunk
-    for i in range(steps):
-        for copy in copies(i):
-            copy.start()
-    span = pl.ds(pl.multiple_of(core * half, LANES), half)
+    first = core * half
+
+    wake_copy = pltpu.make_async_copy(
+        wake.at[pl.ds(pl.multiple_of(first, 16), half)],
+        held.at[:, pl.ds(panels, wake.shape[1])],
+        sems.at[len(cuts) - 1],
+    )
+
+    def panel_copy(i):
+        begin, stop = cuts[i], cuts[i + 1]
+        return pltpu.make_async_copy(
+            influence.at[pl.ds(pl.multiple_of(first + begin, 16), stop - begin)],
+            held.at[pl.ds(begin, stop - begin), pl.ds(0, panels)],
+            sems.at[i],
+        )
+
+    wake_copy.start()
+    for i in range(len(cuts) - 1):
+        panel_copy(i).start()
+    span = pl.ds(pl.multiple_of(first, LANES), half)
     target[...] = both_cores(core, objectives[:, span], objectives_other[:, span])
     self_half[...] = self_term[:, span]
     start[...] = target[...] / self_half[...]
-    for i in range(steps):
-        for copy in copies(i):
-            copy.wait()
-        rows = slice(i * chunk, (i + 1) * chunk)
-        part = dot(start[:, rows].astype(BF16), held[rows, :], ((1,), (0,)))
-        if i == 0:
-            whole[...] = part
-        else:
-            whole[...] += part
+    wake_copy.wait()
+    carried = dot(start[...].astype(BF16), held[:, panels:], ((1,), (0,)))
     upper_local, lower_local = local_wake(scalars, upper, lower)
-    carried = whole[:, panels:]
-    whole[:, 0:panels] += put_columns(carried, upper_local, panels) - put_columns(
+    whole[...] = put_columns(carried, upper_local, panels) - put_columns(
         carried, lower_local, panels
     )
+    for i in range(len(cuts) - 1):
+        panel_copy(i).wait()
+        rows = slice(cuts[i], cuts[i + 1])
+        whole[...] += dot(start[:, rows].astype(BF16), held[rows, 0:panels], ((1,), (0,)))
     keep[...] = whole[:, pl.ds(pl.multiple_of(core * piece, LANES), piece)]
     give[...] = whole[:, pl.ds(pl.multiple_of((1 - core) * piece, LANES), piece)]
 
@@ -398,7 +391,7 @@
     upper = argument(wake_upper[None, :])
     lower = argument(wake_lower[None, :])
 
-    chunk = half // 8
+    cuts = [half * i // 8 for i in range(8)] + [half * 15 // 16, half]
     struct = jax.ShapeDtypeStruct
 
     modes = design_map[None, :]
@@ -419,7 +412,7 @@
     right_near = lax.ppermute(right, GRID, cross(0))
 
     keep, give, start, target, self_half, held = pl.pallas_call(
-        functools.partial(load_adjoint_kernel, chunk),
+        functools.partial(load_adjoint_kernel, cuts),
         in_specs=[SMEM] + [VMEM] * 5 + [ANY, ANY],
         out_specs=[VMEM] * 6,
         out_shape=[
@@ -431,8 +424,8 @@
             pltpu.VMEM((half, width), BF16),
         ],
         scratch_shapes=[
-            pltpu.VMEM((count, width), F32),
-            pltpu.SemaphoreType.DMA((2, half // chunk)),
+            pltpu.VMEM((count, panels), F32),
+            pltpu.SemaphoreType.DMA((len(cuts),)),
         ],
         compiler_params=params(),
         cost_estimate=cost(2 * count * half * width, 2 * half * width),
@@ -529,7 +522,10 @@
         compiler_params=params(4),
         name="collect",
     )(scalars, argument(keep), give)
-    *shards, first_total = lax.optimization_barrier((*shards, totals[0]))
+    bases_other, adjoint_other = swap(bases_send), swap(adjoint_send)
+    *shards, first_total, bases_other, adjoint_other = lax.optimization_barrier(
+        (*shards, totals[0], bases_other, adjoint_other)
+    )
     totals = [first_total, *totals[1:]]
     induced = forward(tuple(CHUNKS + i for i in range(4)), shards, False, "forward_two")
 
@@ -545,8 +541,8 @@
         compiler_params=params(4),
         name="system",
     )(scalars, right_half, image, self_half, *induced)
-    system_give, *totals = lax.optimization_barrier((system_give, *totals))
-    system = system_keep + swap(system_give)
+    system_other, *totals = lax.optimization_barrier((swap(system_give), *totals))
+    system = system_keep + system_other
     systems = [system] + [lax.ppermute(system, "rows", flip(k, n_rows)) for k in range(1, n_rows)]
     solution = pl.pallas_call(
         functools.partial(solve_kernel, len(systems)),
@@ -555,7 +551,7 @@
         out_shape=struct((BLOCK, out_width), F32),
         compiler_params=params(4),
         name="solve",
-    )(scalars, bases_mine, swap(bases_send), *systems)
+    )(scalars, bases_mine, bases_other, *systems)
 
     adjoint = pl.pallas_call(
         functools.partial(update_kernel, len(totals)),
@@ -564,7 +560,7 @@
         out_shape=struct((BLOCK, out_width), F32),
         compiler_params=params(4),
         name="update",
-    )(scalars, adjoint_mine, swap(adjoint_send), self_row, objectives, *totals)
+    )(scalars, adjoint_mine, adjoint_other, self_row, objectives, *totals)
     return (solution, adjoint)
 
 

time: 107 us -> 105 us (0.981)
  starting transfers between devices: 38.4 us -> 36.6 us
    ppermute x4, waiting for transfers between devices: 4.3 us -> 5.67 us  [per_device(): totals = [lax.ppermute(totals[k], GRID, cross(k)) for k in range(side)]]
    ppermute x4, starting transfers between devices: 6.33 us -> 5.08 us  [per_device(): totals = [lax.ppermute(totals[k], GRID, cross(k)) for k in range(side)]]
  transfers between devices with their start and end apart: 27 -> 27, of which waited for: 6 -> 5; matrix products, arithmetic and copies ran while one was open for 1% -> 1% of each run, Pallas kernels for 42% -> 41%
where the time goes in v4:
time: 105 us; the launch traced here: 104 us
  Pallas kernels  57.3 us (55%)
  starting transfers between devices  36.6 us (35%)
  waiting for transfers between devices  8.13 us (8%)
  local copies, waits for them, and re-layouts  1.52 us (1%)
    pallas_call x2, Pallas kernels, forward(): pl.pallas_call(functools.partial(forward_kernel, 512, places, split), in_...  24 us
    pallas_call x1, Pallas kernels, per_device(): pl.pallas_call(functools.partial(load_adjoint_kernel, cuts), in_specs=[SM...  13.6 us
    ppermute x4, starting transfers between devices, per_device(): parts = [lax.ppermute(sends[k % 2], GRID, cross(k)) for k in range(side)]  8.48 us
    ppermute x11, starting transfers between devices, swap(): return lax.ppermute(value, 'rhs', flip(1, 2))  7.86 us
    ppermute x4, waiting for transfers between devices, per_device(): totals = [lax.ppermute(totals[k], GRID, cross(k)) for k in range(side)]  5.67 us
    ppermute x2, starting transfers between devices, per_device(): shards = [lax.ppermute(image_rounded, GRID, fetch(j)) for j in range(2)]  5.29 us
    ppermute x4, starting transfers between devices, per_device(): totals = [lax.ppermute(totals[k], GRID, cross(k)) for k in range(side)]  5.08 us
    ppermute x2, starting transfers between devices, cols_parts(): lax.ppermute(value, 'cols', flip(k, n_cols))  4.74 us
  transfers between devices with their start and end apart: 27, of which 5 were waited for; matrix products, arithmetic and copies ran while one was open for 1% of the time, Pallas kernels for 41%

profile of v4, /device:TPU:0, one launch (start us, length us, event | category | flops | bytes accessed | tf_op | source)
XLA Modules:
  0.0 104.4 jit_solution(4246411198020348972)
XLA Ops:
  2.7 2.1 %right.1 = (f32[16,4096]{1,0:T(8,128)S(1)}, f32[16,2048]{1,0:T(8,128)S(1)}) custom-call(s32[12]{0:T(128)} %stack.55.scalars, f32[5,8]{1,0:T(8,128)} %pitch.1, f32[5,8]{1,0:T(8,128)S(1)} %collective-permute-done.pitch_other, s32[1,8]{1,0:T(1,128)} %bitcast.31, s32[1,8]{1,0:T(1,128)S(1)} %collective-permute-done.1.modes_other, s32[1,4096]{1,0:T(1,128)} %bitcast.29, ...), custom_call_target="tpu_custom_call" | custom-call | tf_op jit(solution)/shard_map/right/pallas_call | solution.py:399
  5.5 13.6 %adjoint_one.1 = (f32[16,4096]{1,0:T(8,128)}, f32[16,4096]{1,0:T(8,128)}, f32[16,2048]{1,0:T(8,128)}, f32[16,2048]{1,0:T(8,128)}, f32[1,2048]{1,0:T(1,128)}, /*index=5*/bf16[2048,8704]{1,0:T(8,128)(2,1)S(1)}) custom-call(s32[12]{0:T(128)} %stack.55.scalars, f32[8,4096]{1,0:T(8,128)} %objectives.3, f32[8,4096]{1,0:T(8,128)} %copy-done.4, f32[1,4096]{1,0:T(1,128)} %bitcast.17, ...), custom_call_target="tpu_custom_call" | custom-call | flops 570425344 | bytes 35651584 | tf_op jit(solution)/shard_map/adjoint_one/pallas_call | solution.py:414
  19.0 4.3 %collective-permute-start.5 = (f32[16,4096]{1,0:T(8,128)}, f32[16,4096]{1,0:T(8,128)S(1)}, u32[]{:S(2)}, u32[]{:S(2)}) collective-permute-start(f32[16,4096]{1,0:T(8,128)} %get-tuple-element.73), channel_id=1, source_target_pairs={{0,1},{1,0},{2,3},{3,2},{4,5},{5,4},{6,7},{7,6},{8,9},{9,8},{10,11... | collective-permute-start | bytes 786440 | tf_op jit(solution)/shard_map/ppermute | solution.py:367
  23.5 1.3 %collective-permute-done.5.other = f32[16,4096]{1,0:T(8,128)S(1)} collective-permute-done((f32[16,4096]{1,0:T(8,128)}, f32[16,4096]{1,0:T(8,128)S(1)}, u32[]{:S(2)}, u32[]{:S(2)}) %collective-permute-start.5) | collective-permute-done | bytes 262176 | tf_op jit(solution)/shard_map/ppermute | solution.py:367
  24.7 1.0 combine.1
  26.4 1.7 %collective-permute-start.7 = (bf16[16,2048]{1,0:T(8,128)(2,1)S(1)}, bf16[16,2048]{1,0:T(8,128)(2,1)S(1)}, u32[]{:S(2)}, u32[]{:S(2)}) collective-permute-start(bf16[16,2048]{1,0:T(8,128)(2,1)S(1)} %get-tuple-element.78), channel_id=1, source_target_pairs={{0,1},{1,5},{2,9},{3,13},{4,0},{5,4},{6,8},{7,12},{8,3},{9,7},{10,... | collective-permute-start | bytes 196616 | tf_op jit(solution)/shard_map/ppermute | solution.py:466
  28.1 5.5 %collective-permute-start.8 = (bf16[16,2048]{1,0:T(8,128)(2,1)S(1)}, bf16[16,2048]{1,0:T(8,128)(2,1)S(1)}, u32[]{:S(2)}, u32[]{:S(2)}) collective-permute-start(bf16[16,2048]{1,0:T(8,128)(2,1)S(1)} %get-tuple-element.77), channel_id=1, source_target_pairs={{0,2},{1,6},{2,10},{3,14},{4,3},{5,7},{6,11},{7,15},{8,0},{9,4},{1... | collective-permute-start | bytes 196616 | tf_op jit(solution)/shard_map/ppermute | solution.py:466
  34.2 12.8 %forward_one.1.rest_0_ = f32[16,2048]{1,0:T(8,128)} custom-call(s32[12]{0:T(128)} %stack.55.scalars, s32[1,512]{1,0:T(1,128)} %bitcast.20, s32[1,512]{1,0:T(1,128)} %bitcast.25, bf16[2048,8704]{1,0:T(8,128)(2,1)S(1)} %get-tuple-element.70.held, f32[16,4096]{1,0:T(8,128)S(1)} %collective-permute-done.3.rest_0_, f32[16,4096]{1,0:T(8,128)S(1)} %collective-permute-done.4.rest_1_), custom_call_target="tpu_custom_call" | custom-call | flops 570425344 | bytes 35651584 | tf_op jit(solution)/shard_map/forward_one/pallas_call | solution.py:442
  47.1 2.6 %collective-permute-start.10 = (f32[16,2048]{1,0:T(8,128)}, f32[16,2048]{1,0:T(8,128)S(1)}, u32[]{:S(2)}, u32[]{:S(2)}) collective-permute-start(f32[16,2048]{1,0:T(8,128)} %forward_one.1.rest_0_), channel_id=1, source_target_pairs={{0,2},{2,0},{1,3},{3,1},{4,6},{6,4},{5,7},{7,5},{8,10},{10,8},{9,1... | collective-permute-start | bytes 393224 | tf_op jit(solution)/shard_map/ppermute | solution.py:370
  49.7 4.6 %adjoint_two_give.1 = (f32[32,2048]{1,0:T(8,128)}, f32[16,2048]{1,0:T(8,128)}, f32[16,512]{1,0:T(8,128)}, f32[8,2048]{1,0:T(8,128)}, f32[8,2048]{1,0:T(8,128)}) custom-call(s32[12]{0:T(128)} %stack.55.scalars, f32[16,2048]{1,0:T(8,128)} %get-tuple-element.68.previous, f32[16,2048]{1,0:T(8,128)} %get-tuple-element.69.target, ...), custom_call_target="tpu_custom_call" | custom-call | flops 285212672 | bytes 17825792 | tf_op jit(solution)/shard_map/adjoint_two_give/pallas_call | solution.py:470
  55.8 4.6 %collective-permute-start.12 = (bf16[16,2048]{1,0:T(8,128)(2,1)S(1)}, bf16[16,2048]{1,0:T(8,128)(2,1)S(1)}, u32[]{:S(2)}, u32[]{:S(2)}) collective-permute-start(bf16[16,2048]{1,0:T(8,128)(2,1)S(1)} %get-tuple-element.90.ready), channel_id=1, source_target_pairs={{0,8},{1,0},{2,12},{3,4},{4,9},{5,1},{6,13},{7,5},{8,10},{9,2},{10... | collective-permute-start | bytes 196616 | tf_op jit(solution)/shard_map/ppermute | solution.py:504
  60.9 4.3 %adjoint_two_keep.1.keep = f32[32,2048]{1,0:T(8,128)} custom-call(s32[12]{0:T(128)} %stack.55.scalars, f32[16,2048]{1,0:T(8,128)} %get-tuple-element.88.adjoint, f32[16,512]{1,0:T(8,128)} %get-tuple-element.89.carried, s32[1,512]{1,0:T(1,128)} %bitcast.22, s32[1,512]{1,0:T(1,128)} %bitcast.27, bf16[2048,8704]{1,0:T(8,128)(2,1)S(1)} %get-tuple-element.70.held, ...), custom_call_target="tpu_custom_call" | custom-call | flops 285212672 | bytes 17825792 | tf_op jit(solution)/shard_map/adjoint_two_keep/pallas_call | solution.py:505
  65.8 1.0 collect.1
  66.8 11.2 %forward_two.1.rest_0_ = f32[16,2048]{1,0:T(8,128)} custom-call(s32[12]{0:T(128)} %stack.55.scalars, s32[1,512]{1,0:T(1,128)} %bitcast.23, s32[1,512]{1,0:T(1,128)} %bitcast.28, bf16[2048,8704]{1,0:T(8,128)(2,1)S(1)} %get-tuple-element.70.held, bf16[16,2048]{1,0:T(8,128)(2,1)S(1)} %collective-permute-done.11.rest_0_, ...), custom_call_target="tpu_custom_call" | custom-call | flops 570425344 | bytes 35651584 | tf_op jit(solution)/shard_map/forward_two/pallas_call | solution.py:442
  78.0 2.2 %collective-permute-start.18 = (f32[16,2048]{1,0:T(8,128)}, f32[16,2048]{1,0:T(8,128)S(1)}, u32[]{:S(2)}, u32[]{:S(2)}) collective-permute-start(f32[16,2048]{1,0:T(8,128)} %forward_two.1.rest_0_), channel_id=1, source_target_pairs={{0,2},{2,0},{1,3},{3,1},{4,6},{6,4},{5,7},{7,5},{8,10},{10,8},{9,1... | collective-permute-start | bytes 393224 | tf_op jit(solution)/shard_map/ppermute | solution.py:370
  80.8 1.9 %collective-permute-start.21 = (f32[8,2048]{1,0:T(8,128)S(1)}, f32[8,2048]{1,0:T(8,128)S(1)}, u32[]{:S(2)}, u32[]{:S(2)}) collective-permute-start(f32[8,2048]{1,0:T(8,128)S(1)} %get-tuple-element.112), channel_id=1, source_target_pairs={{0,1},{1,5},{2,9},{3,13},{4,0},{5,4},{6,8},{7,12},{8,3},{9,7},{10,... | collective-permute-start | bytes 196616 | tf_op jit(solution)/shard_map/ppermute | solution.py:533
  82.7 2.0 %collective-permute-start.22 = (f32[8,2048]{1,0:T(8,128)S(1)}, f32[8,2048]{1,0:T(8,128)S(1)}, u32[]{:S(2)}, u32[]{:S(2)}) collective-permute-start(f32[8,2048]{1,0:T(8,128)S(1)} %get-tuple-element.113), channel_id=1, source_target_pairs={{0,2},{1,6},{2,10},{3,14},{4,3},{5,7},{6,11},{7,15},{8,0},{9,4},{1... | collective-permute-start | bytes 196616 | tf_op jit(solution)/shard_map/ppermute | solution.py:533
  86.2 1.6 %system.1 = (f32[16,128]{1,0:T(8,128)S(1)}, f32[16,128]{1,0:T(8,128)S(1)}) custom-call(s32[12]{0:T(128)} %stack.55.scalars, f32[16,2048]{1,0:T(8,128)S(1)} %get-tuple-element.62.right_half.basis, f32[16,2048]{1,0:T(8,128)S(1)} %get-tuple-element.99.image, f32[1,2048]{1,0:T(1,128)S(1)} %copy-done.2, f32[16,2048]{1,0:T(8,128)S(1)} %copy-done, ...), custom_call_target="tpu_custom_call" | custom-call | tf_op jit(solution)/shard_map/system/pallas_call | solution.py:536
  87.7 1.3 %collective-permute-start.19 = (f32[16,128]{1,0:T(8,128)S(1)}, f32[16,128]{1,0:T(8,128)S(1)}, u32[]{:S(2)}, u32[]{:S(2)}) collective-permute-start(f32[16,128]{1,0:T(8,128)S(1)} %get-tuple-element.110), channel_id=1, source_target_pairs={{0,1},{1,0},{2,3},{3,2},{4,5},{5,4},{6,7},{7,6},{8,9},{9,8},{10,11... | collective-permute-start | bytes 24584 | tf_op jit(solution)/shard_map/ppermute | solution.py:367
  89.0 5.7 %collective-permute-done.22.rest_2_ = f32[8,2048]{1,0:T(8,128)S(1)} collective-permute-done((f32[8,2048]{1,0:T(8,128)S(1)}, f32[8,2048]{1,0:T(8,128)S(1)}, u32[]{:S(2)}, u32[]{:S(2)}) %collective-permute-start.22) | collective-permute-done | bytes 65568 | tf_op jit(solution)/shard_map/ppermute | solution.py:533
  94.8 1.2 %collective-permute-start.25 = (f32[16,128]{1,0:T(8,128)S(1)}, f32[16,128]{1,0:T(8,128)S(1)}, u32[]{:S(2)}, u32[]{:S(2)}) collective-permute-start(f32[16,128]{1,0:T(8,128)S(1)} %add.26.rest_0_), channel_id=1, source_target_pairs={{0,8},{4,12},{8,0},{12,4},{1,9},{5,13},{9,1},{13,5},{2,10},{6,14},... | collective-permute-start | bytes 24584 | tf_op jit(solution)/shard_map/ppermute | solution.py:546
  96.0 3.1 %collective-permute-start.26 = (f32[16,128]{1,0:T(8,128)S(1)}, f32[16,128]{1,0:T(8,128)S(1)}, u32[]{:S(2)}, u32[]{:S(2)}) collective-permute-start(f32[16,128]{1,0:T(8,128)S(1)} %add.26.rest_0_), channel_id=1, source_target_pairs={{0,12},{4,8},{8,4},{12,0},{1,13},{5,9},{9,5},{13,1},{2,14},{6,10},... | collective-permute-start | bytes 24584 | tf_op jit(solution)/shard_map/ppermute | solution.py:546
  99.2 1.6 %update.1 = f32[8,2048]{1,0:T(8,128)} custom-call(s32[12]{0:T(128)} %stack.55.scalars, f32[8,2048]{1,0:T(8,128)S(1)} %copy-done.3, f32[8,2048]{1,0:T(8,128)S(1)} %collective-permute-done.17.received, f32[1,4096]{1,0:T(1,128)} %bitcast.18, f32[8,4096]{1,0:T(8,128)} %objectives.3, f32[8,2048]{1,0:T(8,128)S(1)} %collective-permute-done.20.rest_0_, ...), custom_call_target="tpu_custom_call" | custom-call | tf_op jit(solution)/shard_map/update/pallas_call | solution.py:556
  101.5 2.9 %solve.1 = f32[8,2048]{1,0:T(8,128)} custom-call(s32[12]{0:T(128)} %stack.55.scalars, f32[16,2048]{1,0:T(8,128)S(1)} %get-tuple-element.87.mine, f32[16,2048]{1,0:T(8,128)S(1)} %collective-permute-done.16.received, f32[16,128]{1,0:T(8,128)S(1)} %add.26.rest_0_, f32[16,128]{1,0:T(8,128)S(1)} %collective-permute-done.24.rest_1_, ...), custom_call_target="tpu_custom_call" | custom-call | tf_op jit(solution)/shard_map/solve/pallas_call | solution.py:547
  (54 shorter events, 9.6 us)
Async XLA Ops:
  0.6 4.1 %collective-permute-start.2 = (f32[8,4096]{1,0:T(8,128)}, f32[8,4096]{1,0:T(8,128)S(1)}, u32[]{:S(2)}, u32[]{:S(2)}) collective-permute-start(f32[8,4096]{1,0:T(8,128)} %objectives.3), channel_id=1, source_target_pairs={{0,1},{1,0},{2,3},{3,2},{4,5},{5,4},{6,7},{7,6},{8,9},{9,8},{10,11... | collective-permute-start | bytes 393224 | tf_op jit(solution)/shard_map/ppermute | solution.py:367
  4.8 18.6 %collective-permute-start.3 = (f32[16,4096]{1,0:T(8,128)S(1)}, f32[16,4096]{1,0:T(8,128)S(1)}, u32[]{:S(2)}, u32[]{:S(2)}) collective-permute-start(f32[16,4096]{1,0:T(8,128)S(1)} %get-tuple-element.66), channel_id=1, source_target_pairs={{0,0},{1,4},{2,8},{3,12},{4,1},{5,5},{6,9},{7,13},{8,2},{9,6},{10,... | collective-permute-start | bytes 786440 | tf_op jit(solution)/shard_map/ppermute | solution.py:412
  19.0 5.7 %collective-permute-start.5 = (f32[16,4096]{1,0:T(8,128)}, f32[16,4096]{1,0:T(8,128)S(1)}, u32[]{:S(2)}, u32[]{:S(2)}) collective-permute-start(f32[16,4096]{1,0:T(8,128)} %get-tuple-element.73), channel_id=1, source_target_pairs={{0,1},{1,0},{2,3},{3,2},{4,5},{5,4},{6,7},{7,6},{8,9},{9,8},{10,11... | collective-permute-start | bytes 786440 | tf_op jit(solution)/shard_map/ppermute | solution.py:367
  23.4 2.4 %collective-permute-start.4 = (f32[16,4096]{1,0:T(8,128)S(1)}, f32[16,4096]{1,0:T(8,128)S(1)}, u32[]{:S(2)}, u32[]{:S(2)}) collective-permute-start(f32[16,4096]{1,0:T(8,128)S(1)} %collective-permute-done.3.rest_0_), channel_id=1, source_target_pairs={{0,1},{1,0},{2,3},{3,2},{4,5},{5,4},{6,7},{7,6},{8,9},{9,8},{10,11... | collective-permute-start | bytes 786440 | tf_op jit(solution)/shard_map/ppermute | solution.py:367
  25.8 21.3 %collective-permute-start.6 = (bf16[16,2048]{1,0:T(8,128)(2,1)S(1)}, bf16[16,2048]{1,0:T(8,128)(2,1)S(1)}, u32[]{:S(2)}, u32[]{:S(2)}) collective-permute-start(bf16[16,2048]{1,0:T(8,128)(2,1)S(1)} %get-tuple-element.77), channel_id=1, source_target_pairs={{0,0},{1,4},{2,8},{3,12},{4,1},{5,5},{6,9},{7,13},{8,2},{9,6},{10,... | collective-permute-start | bytes 196616 | tf_op jit(solution)/shard_map/ppermute | solution.py:466
  26.4 20.7 %collective-permute-start.7 = (bf16[16,2048]{1,0:T(8,128)(2,1)S(1)}, bf16[16,2048]{1,0:T(8,128)(2,1)S(1)}, u32[]{:S(2)}, u32[]{:S(2)}) collective-permute-start(bf16[16,2048]{1,0:T(8,128)(2,1)S(1)} %get-tuple-element.78), channel_id=1, source_target_pairs={{0,1},{1,5},{2,9},{3,13},{4,0},{5,4},{6,8},{7,12},{8,3},{9,7},{10,... | collective-permute-start | bytes 196616 | tf_op jit(solution)/shard_map/ppermute | solution.py:466
  28.1 19.0 %collective-permute-start.8 = (bf16[16,2048]{1,0:T(8,128)(2,1)S(1)}, bf16[16,2048]{1,0:T(8,128)(2,1)S(1)}, u32[]{:S(2)}, u32[]{:S(2)}) collective-permute-start(bf16[16,2048]{1,0:T(8,128)(2,1)S(1)} %get-tuple-element.77), channel_id=1, source_target_pairs={{0,2},{1,6},{2,10},{3,14},{4,3},{5,7},{6,11},{7,15},{8,0},{9,4},{1... | collective-permute-start | bytes 196616 | tf_op jit(solution)/shard_map/ppermute | solution.py:466
  33.6 13.5 %collective-permute-start.9 = (bf16[16,2048]{1,0:T(8,128)(2,1)S(1)}, bf16[16,2048]{1,0:T(8,128)(2,1)S(1)}, u32[]{:S(2)}, u32[]{:S(2)}) collective-permute-start(bf16[16,2048]{1,0:T(8,128)(2,1)S(1)} %get-tuple-element.78), channel_id=1, source_target_pairs={{0,3},{1,7},{2,11},{3,15},{4,2},{5,6},{6,10},{7,14},{8,1},{9,5},{1... | collective-permute-start | bytes 196616 | tf_op jit(solution)/shard_map/ppermute | solution.py:466
  47.1 7.2 %collective-permute-start.10 = (f32[16,2048]{1,0:T(8,128)}, f32[16,2048]{1,0:T(8,128)S(1)}, u32[]{:S(2)}, u32[]{:S(2)}) collective-permute-start(f32[16,2048]{1,0:T(8,128)} %forward_one.1.rest_0_), channel_id=1, source_target_pairs={{0,2},{2,0},{1,3},{3,1},{4,6},{6,4},{5,7},{7,5},{8,10},{10,8},{9,1... | collective-permute-start | bytes 393224 | tf_op jit(solution)/shard_map/ppermute | solution.py:370
  54.3 11.5 %collective-permute-start.15 = (f32[32,2048]{1,0:T(8,128)}, f32[32,2048]{1,0:T(8,128)S(1)}, u32[]{:S(2)}, u32[]{:S(2)}) collective-permute-start(f32[32,2048]{1,0:T(8,128)} %get-tuple-element.94), channel_id=1, source_target_pairs={{0,1},{1,0},{2,3},{3,2},{4,5},{5,4},{6,7},{7,6},{8,9},{9,8},{10,11... | collective-permute-start | bytes 786440 | tf_op jit(solution)/shard_map/ppermute | solution.py:367
  55.1 10.1 %collective-permute-start.11 = (bf16[16,2048]{1,0:T(8,128)(2,1)S(1)}, bf16[16,2048]{1,0:T(8,128)(2,1)S(1)}, u32[]{:S(2)}, u32[]{:S(2)}) collective-permute-start(bf16[16,2048]{1,0:T(8,128)(2,1)S(1)} %get-tuple-element.90.ready), channel_id=1, source_target_pairs={{0,0},{1,8},{2,4},{3,12},{4,1},{5,9},{6,5},{7,13},{8,2},{9,10},{10... | collective-permute-start | bytes 196616 | tf_op jit(solution)/shard_map/ppermute | solution.py:504
  55.8 9.4 %collective-permute-start.12 = (bf16[16,2048]{1,0:T(8,128)(2,1)S(1)}, bf16[16,2048]{1,0:T(8,128)(2,1)S(1)}, u32[]{:S(2)}, u32[]{:S(2)}) collective-permute-start(bf16[16,2048]{1,0:T(8,128)(2,1)S(1)} %get-tuple-element.90.ready), channel_id=1, source_target_pairs={{0,8},{1,0},{2,12},{3,4},{4,9},{5,1},{6,13},{7,5},{8,10},{9,2},{10... | collective-permute-start | bytes 196616 | tf_op jit(solution)/shard_map/ppermute | solution.py:504
  60.4 6.4 %collective-permute-start.16 = (f32[16,2048]{1,0:T(8,128)S(1)}, f32[16,2048]{1,0:T(8,128)S(1)}, u32[]{:S(2)}, u32[]{:S(2)}) collective-permute-start(f32[16,2048]{1,0:T(8,128)S(1)} %get-tuple-element.96), channel_id=1, source_target_pairs={{0,1},{1,0},{2,3},{3,2},{4,5},{5,4},{6,7},{7,6},{8,9},{9,8},{10,11... | collective-permute-start | bytes 393224 | tf_op jit(solution)/shard_map/ppermute | solution.py:367
  60.4 6.4 %collective-permute-start.17 = (f32[8,2048]{1,0:T(8,128)}, f32[8,2048]{1,0:T(8,128)S(1)}, u32[]{:S(2)}, u32[]{:S(2)}) collective-permute-start(f32[8,2048]{1,0:T(8,128)} %get-tuple-element.97), channel_id=1, source_target_pairs={{0,1},{1,0},{2,3},{3,2},{4,5},{5,4},{6,7},{7,6},{8,9},{9,8},{10,11... | collective-permute-start | bytes 196616 | tf_op jit(solution)/shard_map/ppermute | solution.py:367
  65.2 1.6 %collective-permute-start.13 = (bf16[16,2048]{1,0:T(8,128)(2,1)S(1)}, bf16[16,2048]{1,0:T(8,128)(2,1)S(1)}, u32[]{:S(2)}, u32[]{:S(2)}) collective-permute-start(bf16[16,2048]{1,0:T(8,128)(2,1)S(1)} %collective-permute-done.11.rest_0_), channel_id=1, source_target_pairs={{0,1},{1,0},{2,3},{3,2},{4,5},{5,4},{6,7},{7,6},{8,9},{9,8},{10,11... | collective-permute-start | bytes 196616 | tf_op jit(solution)/shard_map/ppermute | solution.py:367
  78.0 7.3 %collective-permute-start.18 = (f32[16,2048]{1,0:T(8,128)}, f32[16,2048]{1,0:T(8,128)S(1)}, u32[]{:S(2)}, u32[]{:S(2)}) collective-permute-start(f32[16,2048]{1,0:T(8,128)} %forward_two.1.rest_0_), channel_id=1, source_target_pairs={{0,2},{2,0},{1,3},{3,1},{4,6},{6,4},{5,7},{7,5},{8,10},{10,8},{9,1... | collective-permute-start | bytes 393224 | tf_op jit(solution)/shard_map/ppermute | solution.py:370
  80.2 8.9 %collective-permute-start.20 = (f32[8,2048]{1,0:T(8,128)S(1)}, f32[8,2048]{1,0:T(8,128)S(1)}, u32[]{:S(2)}, u32[]{:S(2)}) collective-permute-start(f32[8,2048]{1,0:T(8,128)S(1)} %get-tuple-element.111), channel_id=1, source_target_pairs={{0,0},{1,4},{2,8},{3,12},{4,1},{5,5},{6,9},{7,13},{8,2},{9,6},{10,... | collective-permute-start | bytes 196616 | tf_op jit(solution)/shard_map/ppermute | solution.py:533
  80.8 8.2 %collective-permute-start.21 = (f32[8,2048]{1,0:T(8,128)S(1)}, f32[8,2048]{1,0:T(8,128)S(1)}, u32[]{:S(2)}, u32[]{:S(2)}) collective-permute-start(f32[8,2048]{1,0:T(8,128)S(1)} %get-tuple-element.112), channel_id=1, source_target_pairs={{0,1},{1,5},{2,9},{3,13},{4,0},{5,4},{6,8},{7,12},{8,3},{9,7},{10,... | collective-permute-start | bytes 196616 | tf_op jit(solution)/shard_map/ppermute | solution.py:533
  82.7 12.0 %collective-permute-start.22 = (f32[8,2048]{1,0:T(8,128)S(1)}, f32[8,2048]{1,0:T(8,128)S(1)}, u32[]{:S(2)}, u32[]{:S(2)}) collective-permute-start(f32[8,2048]{1,0:T(8,128)S(1)} %get-tuple-element.113), channel_id=1, source_target_pairs={{0,2},{1,6},{2,10},{3,14},{4,3},{5,7},{6,11},{7,15},{8,0},{9,4},{1... | collective-permute-start | bytes 196616 | tf_op jit(solution)/shard_map/ppermute | solution.py:533
  84.6 10.0 %collective-permute-start.23 = (f32[8,2048]{1,0:T(8,128)S(1)}, f32[8,2048]{1,0:T(8,128)S(1)}, u32[]{:S(2)}, u32[]{:S(2)}) collective-permute-start(f32[8,2048]{1,0:T(8,128)S(1)} %get-tuple-element.114), channel_id=1, source_target_pairs={{0,3},{1,7},{2,11},{3,15},{4,2},{5,6},{6,10},{7,14},{8,1},{9,5},{1... | collective-permute-start | bytes 196616 | tf_op jit(solution)/shard_map/ppermute | solution.py:533
  87.7 6.9 %collective-permute-start.19 = (f32[16,128]{1,0:T(8,128)S(1)}, f32[16,128]{1,0:T(8,128)S(1)}, u32[]{:S(2)}, u32[]{:S(2)}) collective-permute-start(f32[16,128]{1,0:T(8,128)S(1)} %get-tuple-element.110), channel_id=1, source_target_pairs={{0,1},{1,0},{2,3},{3,2},{4,5},{5,4},{6,7},{7,6},{8,9},{9,8},{10,11... | collective-permute-start | bytes 24584 | tf_op jit(solution)/shard_map/ppermute | solution.py:367
  94.7 6.1 %collective-permute-start.24 = (f32[16,128]{1,0:T(8,128)S(1)}, f32[16,128]{1,0:T(8,128)S(1)}, u32[]{:S(2)}, u32[]{:S(2)}) collective-permute-start(f32[16,128]{1,0:T(8,128)S(1)} %add.26.rest_0_), channel_id=1, source_target_pairs={{0,4},{4,0},{8,12},{12,8},{1,5},{5,1},{9,13},{13,9},{2,6},{6,2},{1... | collective-permute-start | bytes 24584 | tf_op jit(solution)/shard_map/ppermute | solution.py:546
  94.8 6.0 %collective-permute-start.25 = (f32[16,128]{1,0:T(8,128)S(1)}, f32[16,128]{1,0:T(8,128)S(1)}, u32[]{:S(2)}, u32[]{:S(2)}) collective-permute-start(f32[16,128]{1,0:T(8,128)S(1)} %add.26.rest_0_), channel_id=1, source_target_pairs={{0,8},{4,12},{8,0},{12,4},{1,9},{5,13},{9,1},{13,5},{2,10},{6,14},... | collective-permute-start | bytes 24584 | tf_op jit(solution)/shard_map/ppermute | solution.py:546
  96.0 5.4 %collective-permute-start.26 = (f32[16,128]{1,0:T(8,128)S(1)}, f32[16,128]{1,0:T(8,128)S(1)}, u32[]{:S(2)}, u32[]{:S(2)}) collective-permute-start(f32[16,128]{1,0:T(8,128)S(1)} %add.26.rest_0_), channel_id=1, source_target_pairs={{0,12},{4,8},{8,4},{12,0},{1,13},{5,9},{9,5},{13,1},{2,14},{6,10},... | collective-permute-start | bytes 24584 | tf_op jit(solution)/shard_map/ppermute | solution.py:546
  (8 other events, 71.6 us)

commit v5 on v4

--- a/solution.py
+++ b/solution.py
@@ -275,7 +275,7 @@
 def collect_kernel(scalars, keep, other, *outs):
     for k, out in enumerate(outs):
         rows = pl.ds(pl.multiple_of(jnp.bitwise_xor(scalars[ROW], k) * BLOCK, BLOCK), BLOCK)
-        out[...] = keep[rows, :] + other[rows, :]
+        out[...] = (keep[rows, :] + other[rows, :]).astype(BF16)
 
 
 def update_kernel(n_parts, scalars, mine, received, self_term, objectives, *rest):
@@ -285,7 +285,7 @@
     scale = self_term[:, span]
     image = scale * previous
     for part in parts:
-        image = image + part[...]
+        image = image + part[...].astype(F32)
     out[...] = previous + (objectives[:, span] - image) / scale
 
 
@@ -298,7 +298,7 @@
     size = basis.shape[0]
     row = lax.broadcasted_iota(jnp.int32, (size, 1), 0)
     for j in range(size):
-        pivot_row = system[j : j + 1, :] / system[j : j + 1, j : j + 1]
+        pivot_row = system[j : j + 1, :] * (1.0 / system[j : j + 1, j : j + 1])
         factor = jnp.where(row == j, 0.0, system[:, j : j + 1])
         system = jnp.where(row == j, pivot_row, system - factor * pivot_row)
     weights = system[:, size : size + BLOCK]
@@ -440,10 +440,10 @@
     def forward(places, shards, split, name):
         rows = 2 * count if split else count
         return pl.pallas_call(
-            functools.partial(forward_kernel, 512, places, split),
+            functools.partial(forward_kernel, 256, places, split),
             in_specs=[SMEM] + [VMEM] * (3 + len(shards)),
             out_specs=VMEM,
-            out_shape=struct((count, half), F32),
+            out_shape=pltpu.VMEM((count, half), F32),
             scratch_shapes=[pltpu.VMEM((rows, width), BF16)],
             compiler_params=params(),
             cost_estimate=cost(2 * count * half * width, 2 * half * width),
@@ -472,7 +472,7 @@
         in_specs=[SMEM] + [VMEM] * (6 + len(parts)),
         out_specs=[VMEM] * 5,
         out_shape=[
-            struct((side * BLOCK, out_width), F32),
+            pltpu.VMEM((side * BLOCK, out_width), F32),
             struct((count, half), F32),
             struct((count, wake), F32),
             struct((BLOCK, out_width), F32),
@@ -506,7 +506,7 @@
         functools.partial(adjoint_keep_kernel, tile),
         in_specs=[SMEM] + [VMEM] * 5 + [ANY],
         out_specs=VMEM,
-        out_shape=struct((side * BLOCK, out_width), F32),
+        out_shape=pltpu.VMEM((side * BLOCK, out_width), F32),
         compiler_params=params(),
         cost_estimate=cost(count * half * width, half * width),
         name="adjoint_two_keep",
@@ -518,10 +518,10 @@
         collect_kernel,
         in_specs=[SMEM, VMEM, VMEM],
         out_specs=[VMEM] * side,
-        out_shape=[struct((BLOCK, out_width), F32)] * side,
+        out_shape=[struct((BLOCK, out_width), BF16)] * side,
         compiler_params=params(4),
         name="collect",
-    )(scalars, argument(keep), give)
+    )(scalars, keep, give)
     bases_other, adjoint_other = swap(bases_send), swap(adjoint_send)
     *shards, first_total, bases_other, adjoint_other = lax.optimization_barrier(
         (*shards, totals[0], bases_other, adjoint_other)

time: 105 us -> 99.1 us (0.944)
  Pallas kernels: 57.3 us -> 54.8 us
  waiting for transfers between devices: 8.13 us -> 5.78 us
    ppermute x4, waiting for transfers between devices: 5.67 us -> 2.46 us  [per_device(): totals = [lax.ppermute(totals[k], GRID, cross(k)) for k in range(side)]]
    pallas_call x2, Pallas kernels: 24 us -> 22.6 us  [forward(): pl.pallas_call(functools.partial(forward_kernel, 256, places, split), in_...]
  transfers between devices with their start and end apart: 27 -> 27, of which waited for: 5 -> 7; matrix products, arithmetic and copies ran while one was open for 1% -> 1% of each run, Pallas kernels for 41% -> 42%
where the time goes in v5:
time: 99.1 us; the launch traced here: 98.7 us
  Pallas kernels  54.8 us (55%)
  starting transfers between devices  36.6 us (37%)
  waiting for transfers between devices  5.78 us (6%)
    pallas_call x2, Pallas kernels, forward(): pl.pallas_call(functools.partial(forward_kernel, 256, places, split), in_...  22.6 us
    pallas_call x1, Pallas kernels, per_device(): pl.pallas_call(functools.partial(load_adjoint_kernel, cuts), in_specs=[SM...  13.6 us
    ppermute x4, starting transfers between devices, per_device(): parts = [lax.ppermute(sends[k % 2], GRID, cross(k)) for k in range(side)]  8.48 us
    ppermute x11, starting transfers between devices, swap(): return lax.ppermute(value, 'rhs', flip(1, 2))  7.8 us
    ppermute x2, starting transfers between devices, per_device(): shards = [lax.ppermute(image_rounded, GRID, fetch(j)) for j in range(2)]  5.29 us
    ppermute x4, starting transfers between devices, per_device(): totals = [lax.ppermute(totals[k], GRID, cross(k)) for k in range(side)]  5.1 us
    ppermute x2, starting transfers between devices, cols_parts(): lax.ppermute(value, 'cols', flip(k, n_cols))  4.91 us
    pallas_call x1, Pallas kernels, per_device(): pl.pallas_call(functools.partial(adjoint_give_kernel, tile, len(parts)),...  4.47 us
  transfers between devices with their start and end apart: 27, of which 7 were waited for; matrix products, arithmetic and copies ran while one was open for 1% of the time, Pallas kernels for 42%

profile of v5, /device:TPU:0, one launch (start us, length us, event | category | flops | bytes accessed | tf_op | source)
XLA Modules:
  0.0 98.7 jit_solution(17960412796806541134)
XLA Ops:
  2.7 2.1 %right.1 = (f32[16,4096]{1,0:T(8,128)S(1)}, f32[16,2048]{1,0:T(8,128)S(1)}) custom-call(s32[12]{0:T(128)} %stack.55.scalars, f32[5,8]{1,0:T(8,128)} %pitch.1, f32[5,8]{1,0:T(8,128)S(1)} %collective-permute-done.pitch_other, s32[1,8]{1,0:T(1,128)} %bitcast.31, s32[1,8]{1,0:T(1,128)S(1)} %collective-permute-done.1.modes_other, s32[1,4096]{1,0:T(1,128)} %bitcast.29, ...), custom_call_target="tpu_custom_call" | custom-call | tf_op jit(solution)/shard_map/right/pallas_call | solution.py:399
  5.5 13.6 %adjoint_one.1 = (f32[16,4096]{1,0:T(8,128)}, f32[16,4096]{1,0:T(8,128)}, f32[16,2048]{1,0:T(8,128)}, f32[16,2048]{1,0:T(8,128)}, f32[1,2048]{1,0:T(1,128)}, /*index=5*/bf16[2048,8704]{1,0:T(8,128)(2,1)S(1)}) custom-call(s32[12]{0:T(128)} %stack.55.scalars, f32[8,4096]{1,0:T(8,128)} %objectives.3, f32[8,4096]{1,0:T(8,128)} %copy-done.2, f32[1,4096]{1,0:T(1,128)} %bitcast.17, ...), custom_call_target="tpu_custom_call" | custom-call | flops 570425344 | bytes 35651584 | tf_op jit(solution)/shard_map/adjoint_one/pallas_call | solution.py:414
  19.0 4.3 %collective-permute-start.5 = (f32[16,4096]{1,0:T(8,128)}, f32[16,4096]{1,0:T(8,128)S(1)}, u32[]{:S(2)}, u32[]{:S(2)}) collective-permute-start(f32[16,4096]{1,0:T(8,128)} %get-tuple-element.73), channel_id=1, source_target_pairs={{0,1},{1,0},{2,3},{3,2},{4,5},{5,4},{6,7},{7,6},{8,9},{9,8},{10,11... | collective-permute-start | bytes 786440 | tf_op jit(solution)/shard_map/ppermute | solution.py:367
  23.5 1.3 %collective-permute-done.5.other = f32[16,4096]{1,0:T(8,128)S(1)} collective-permute-done((f32[16,4096]{1,0:T(8,128)}, f32[16,4096]{1,0:T(8,128)S(1)}, u32[]{:S(2)}, u32[]{:S(2)}) %collective-permute-start.5) | collective-permute-done | bytes 262176 | tf_op jit(solution)/shard_map/ppermute | solution.py:367
  24.7 1.0 %combine.1 = (bf16[16,2048]{1,0:T(8,128)(2,1)S(1)}, bf16[16,2048]{1,0:T(8,128)(2,1)S(1)}) custom-call(s32[12]{0:T(128)} %stack.55.scalars, f32[16,4096]{1,0:T(8,128)} %get-tuple-element.72.keep, f32[16,4096]{1,0:T(8,128)S(1)} %collective-permute-done.5.other), custom_call_target="tpu_custom_call" | custom-call | tf_op jit(solution)/shard_map/combine/pallas_call | solution.py:453
  26.4 1.7 %collective-permute-start.7 = (bf16[16,2048]{1,0:T(8,128)(2,1)S(1)}, bf16[16,2048]{1,0:T(8,128)(2,1)S(1)}, u32[]{:S(2)}, u32[]{:S(2)}) collective-permute-start(bf16[16,2048]{1,0:T(8,128)(2,1)S(1)} %get-tuple-element.78), channel_id=1, source_target_pairs={{0,1},{1,5},{2,9},{3,13},{4,0},{5,4},{6,8},{7,12},{8,3},{9,7},{10,... | collective-permute-start | bytes 196616 | tf_op jit(solution)/shard_map/ppermute | solution.py:466
  28.1 5.5 %collective-permute-start.8 = (bf16[16,2048]{1,0:T(8,128)(2,1)S(1)}, bf16[16,2048]{1,0:T(8,128)(2,1)S(1)}, u32[]{:S(2)}, u32[]{:S(2)}) collective-permute-start(bf16[16,2048]{1,0:T(8,128)(2,1)S(1)} %get-tuple-element.77), channel_id=1, source_target_pairs={{0,2},{1,6},{2,10},{3,14},{4,3},{5,7},{6,11},{7,15},{8,0},{9,4},{1... | collective-permute-start | bytes 196616 | tf_op jit(solution)/shard_map/ppermute | solution.py:466
  34.2 12.1 %forward_one.1.rest_0_ = f32[16,2048]{1,0:T(8,128)S(1)} custom-call(s32[12]{0:T(128)} %stack.55.scalars, s32[1,512]{1,0:T(1,128)} %bitcast.20, s32[1,512]{1,0:T(1,128)} %bitcast.25, bf16[2048,8704]{1,0:T(8,128)(2,1)S(1)} %get-tuple-element.70.held, f32[16,4096]{1,0:T(8,128)S(1)} %collective-permute-done.3.rest_0_, f32[16,4096]{1,0:T(8,128)S(1)} %collective-permute-done.4.rest_1_), custom_call_target="tpu_custom_call" | custom-call | flops 570425344 | bytes 35651584 | tf_op jit(solution)/shard_map/forward_one/pallas_call | solution.py:442
  46.4 2.6 %collective-permute-start.10 = (f32[16,2048]{1,0:T(8,128)S(1)}, f32[16,2048]{1,0:T(8,128)S(1)}, u32[]{:S(2)}, u32[]{:S(2)}) collective-permute-start(f32[16,2048]{1,0:T(8,128)S(1)} %forward_one.1.rest_0_), channel_id=1, source_target_pairs={{0,2},{2,0},{1,3},{3,1},{4,6},{6,4},{5,7},{7,5},{8,10},{10,8},{9,1... | collective-permute-start | bytes 393224 | tf_op jit(solution)/shard_map/ppermute | solution.py:370
  49.0 4.5 %adjoint_two_give.1 = (f32[32,2048]{1,0:T(8,128)S(1)}, f32[16,2048]{1,0:T(8,128)}, f32[16,512]{1,0:T(8,128)}, f32[8,2048]{1,0:T(8,128)}, f32[8,2048]{1,0:T(8,128)}) custom-call(s32[12]{0:T(128)} %stack.55.scalars, f32[16,2048]{1,0:T(8,128)} %get-tuple-element.68.previous, f32[16,2048]{1,0:T(8,128)} %get-tuple-element.69.target, ...), custom_call_target="tpu_custom_call" | custom-call | flops 285212672 | bytes 17825792 | tf_op jit(solution)/shard_map/adjoint_two_give/pallas_call | solution.py:470
  54.9 4.6 %collective-permute-start.12 = (bf16[16,2048]{1,0:T(8,128)(2,1)S(1)}, bf16[16,2048]{1,0:T(8,128)(2,1)S(1)}, u32[]{:S(2)}, u32[]{:S(2)}) collective-permute-start(bf16[16,2048]{1,0:T(8,128)(2,1)S(1)} %get-tuple-element.90.ready), channel_id=1, source_target_pairs={{0,8},{1,0},{2,12},{3,4},{4,9},{5,1},{6,13},{7,5},{8,10},{9,2},{10... | collective-permute-start | bytes 196616 | tf_op jit(solution)/shard_map/ppermute | solution.py:504
  60.0 3.6 %adjoint_two_keep.1.keep = f32[32,2048]{1,0:T(8,128)S(1)} custom-call(s32[12]{0:T(128)} %stack.55.scalars, f32[16,2048]{1,0:T(8,128)} %get-tuple-element.88.adjoint, f32[16,512]{1,0:T(8,128)} %get-tuple-element.89.carried, s32[1,512]{1,0:T(1,128)} %bitcast.22, s32[1,512]{1,0:T(1,128)} %bitcast.27, bf16[2048,8704]{1,0:T(8,128)(2,1)S(1)} %get-tuple-element.70.held, ...), custom_call_target="tpu_custom_call" | custom-call | flops 285212672 | bytes 17825792 | tf_op jit(solution)/shard_map/adjoint_two_keep/pallas_call | solution.py:505
  65.1 10.5 %forward_two.1.rest_0_ = f32[16,2048]{1,0:T(8,128)S(1)} custom-call(s32[12]{0:T(128)} %stack.55.scalars, s32[1,512]{1,0:T(1,128)} %bitcast.23, s32[1,512]{1,0:T(1,128)} %bitcast.28, bf16[2048,8704]{1,0:T(8,128)(2,1)S(1)} %get-tuple-element.70.held, bf16[16,2048]{1,0:T(8,128)(2,1)S(1)} %collective-permute-done.11.rest_0_, ...), custom_call_target="tpu_custom_call" | custom-call | flops 570425344 | bytes 35651584 | tf_op jit(solution)/shard_map/forward_two/pallas_call | solution.py:442
  75.6 2.3 %collective-permute-start.18 = (f32[16,2048]{1,0:T(8,128)S(1)}, f32[16,2048]{1,0:T(8,128)S(1)}, u32[]{:S(2)}, u32[]{:S(2)}) collective-permute-start(f32[16,2048]{1,0:T(8,128)S(1)} %forward_two.1.rest_0_), channel_id=1, source_target_pairs={{0,2},{2,0},{1,3},{3,1},{4,6},{6,4},{5,7},{7,5},{8,10},{10,8},{9,1... | collective-permute-start | bytes 393224 | tf_op jit(solution)/shard_map/ppermute | solution.py:370
  78.6 1.7 %collective-permute-start.21 = (bf16[8,2048]{1,0:T(8,128)(2,1)S(1)}, bf16[8,2048]{1,0:T(8,128)(2,1)S(1)}, u32[]{:S(2)}, u32[]{:S(2)}) collective-permute-start(bf16[8,2048]{1,0:T(8,128)(2,1)S(1)} %get-tuple-element.112), channel_id=1, source_target_pairs={{0,1},{1,5},{2,9},{3,13},{4,0},{5,4},{6,8},{7,12},{8,3},{9,7},{10,... | collective-permute-start | bytes 98312 | tf_op jit(solution)/shard_map/ppermute | solution.py:533
  80.3 2.0 %collective-permute-start.22 = (bf16[8,2048]{1,0:T(8,128)(2,1)S(1)}, bf16[8,2048]{1,0:T(8,128)(2,1)S(1)}, u32[]{:S(2)}, u32[]{:S(2)}) collective-permute-start(bf16[8,2048]{1,0:T(8,128)(2,1)S(1)} %get-tuple-element.113), channel_id=1, source_target_pairs={{0,2},{1,6},{2,10},{3,14},{4,3},{5,7},{6,11},{7,15},{8,0},{9,4},{1... | collective-permute-start | bytes 98312 | tf_op jit(solution)/shard_map/ppermute | solution.py:533
  83.0 1.6 %system.1 = (f32[16,128]{1,0:T(8,128)S(1)}, f32[16,128]{1,0:T(8,128)S(1)}) custom-call(s32[12]{0:T(128)} %stack.55.scalars, f32[16,2048]{1,0:T(8,128)S(1)} %get-tuple-element.62.right_half.basis, f32[16,2048]{1,0:T(8,128)S(1)} %get-tuple-element.99.image, f32[1,2048]{1,0:T(1,128)S(1)} %copy-done, f32[16,2048]{1,0:T(8,128)S(1)} %forward_two.1.rest_0_, ...), custom_call_target="tpu_custom_call" | custom-call | tf_op jit(solution)/shard_map/system/pallas_call | solution.py:536
  84.6 1.3 %collective-permute-start.19 = (f32[16,128]{1,0:T(8,128)S(1)}, f32[16,128]{1,0:T(8,128)S(1)}, u32[]{:S(2)}, u32[]{:S(2)}) collective-permute-start(f32[16,128]{1,0:T(8,128)S(1)} %get-tuple-element.110), channel_id=1, source_target_pairs={{0,1},{1,0},{2,3},{3,2},{4,5},{5,4},{6,7},{7,6},{8,9},{9,8},{10,11... | collective-permute-start | bytes 24584 | tf_op jit(solution)/shard_map/ppermute | solution.py:367
  85.9 1.7 %collective-permute-done.22.rest_2_ = bf16[8,2048]{1,0:T(8,128)(2,1)S(1)} collective-permute-done((bf16[8,2048]{1,0:T(8,128)(2,1)S(1)}, bf16[8,2048]{1,0:T(8,128)(2,1)S(1)}, u32[]{:S(2)}, u32[]{:S(2)}) %collective-permute-start.22) | collective-permute-done | bytes 32800 | tf_op jit(solution)/shard_map/ppermute | solution.py:533
  88.9 1.4 %collective-permute-start.25 = (f32[16,128]{1,0:T(8,128)S(1)}, f32[16,128]{1,0:T(8,128)S(1)}, u32[]{:S(2)}, u32[]{:S(2)}) collective-permute-start(f32[16,128]{1,0:T(8,128)S(1)} %add.26.rest_0_), channel_id=1, source_target_pairs={{0,8},{4,12},{8,0},{12,4},{1,9},{5,13},{9,1},{13,5},{2,10},{6,14},... | collective-permute-start | bytes 24584 | tf_op jit(solution)/shard_map/ppermute | solution.py:546
  90.3 2.5 %collective-permute-start.26 = (f32[16,128]{1,0:T(8,128)S(1)}, f32[16,128]{1,0:T(8,128)S(1)}, u32[]{:S(2)}, u32[]{:S(2)}) collective-permute-start(f32[16,128]{1,0:T(8,128)S(1)} %add.26.rest_0_), channel_id=1, source_target_pairs={{0,12},{4,8},{8,4},{12,0},{1,13},{5,9},{9,5},{13,1},{2,14},{6,10},... | collective-permute-start | bytes 24584 | tf_op jit(solution)/shard_map/ppermute | solution.py:546
  92.8 1.6 %update.1 = f32[8,2048]{1,0:T(8,128)} custom-call(s32[12]{0:T(128)} %stack.55.scalars, f32[8,2048]{1,0:T(8,128)S(1)} %copy-done.1, f32[8,2048]{1,0:T(8,128)S(1)} %collective-permute-done.17.received, f32[1,4096]{1,0:T(1,128)} %bitcast.18, f32[8,4096]{1,0:T(8,128)} %objectives.3, bf16[8,2048]{1,0:T(8,128)(2,1)S(1)} %collective-permute-done.20.rest_0_, ...), custom_call_target="tpu_custom_call" | custom-call | tf_op jit(solution)/shard_map/update/pallas_call | solution.py:556
  94.4 1.4 %collective-permute-done.26.rest_3_ = f32[16,128]{1,0:T(8,128)S(1)} collective-permute-done((f32[16,128]{1,0:T(8,128)S(1)}, f32[16,128]{1,0:T(8,128)S(1)}, u32[]{:S(2)}, u32[]{:S(2)}) %collective-permute-start.26) | collective-permute-done | bytes 8224 | tf_op jit(solution)/shard_map/ppermute | solution.py:546
  95.7 3.0 %solve.1 = f32[8,2048]{1,0:T(8,128)} custom-call(s32[12]{0:T(128)} %stack.55.scalars, f32[16,2048]{1,0:T(8,128)S(1)} %get-tuple-element.87.mine, f32[16,2048]{1,0:T(8,128)S(1)} %collective-permute-done.16.received, f32[16,128]{1,0:T(8,128)S(1)} %add.26.rest_0_, f32[16,128]{1,0:T(8,128)S(1)} %collective-permute-done.24.rest_1_, ...), custom_call_target="tpu_custom_call" | custom-call | tf_op jit(solution)/shard_map/solve/pallas_call | solution.py:547
  (50 shorter events, 10.2 us)
Async XLA Ops:
  0.6 4.1 %collective-permute-start.2 = (f32[8,4096]{1,0:T(8,128)}, f32[8,4096]{1,0:T(8,128)S(1)}, u32[]{:S(2)}, u32[]{:S(2)}) collective-permute-start(f32[8,4096]{1,0:T(8,128)} %objectives.3), channel_id=1, source_target_pairs={{0,1},{1,0},{2,3},{3,2},{4,5},{5,4},{6,7},{7,6},{8,9},{9,8},{10,11... | collective-permute-start | bytes 393224 | tf_op jit(solution)/shard_map/ppermute | solution.py:367
  1.2 1.5 %collective-permute-start = (f32[5,8]{1,0:T(8,128)}, f32[5,8]{1,0:T(8,128)S(1)}, u32[]{:S(2)}, u32[]{:S(2)}) collective-permute-start(f32[5,8]{1,0:T(8,128)} %pitch.1), channel_id=1, source_target_pairs={{0,1},{1,0},{2,3},{3,2},{4,5},{5,4},{6,7},{7,6},{8,9},{9,8},{10,11... | collective-permute-start | bytes 488 | tf_op jit(solution)/shard_map/ppermute | solution.py:367
  4.8 18.6 %collective-permute-start.3 = (f32[16,4096]{1,0:T(8,128)S(1)}, f32[16,4096]{1,0:T(8,128)S(1)}, u32[]{:S(2)}, u32[]{:S(2)}) collective-permute-start(f32[16,4096]{1,0:T(8,128)S(1)} %get-tuple-element.66), channel_id=1, source_target_pairs={{0,0},{1,4},{2,8},{3,12},{4,1},{5,5},{6,9},{7,13},{8,2},{9,6},{10,... | collective-permute-start | bytes 786440 | tf_op jit(solution)/shard_map/ppermute | solution.py:412
  19.0 5.7 %collective-permute-start.5 = (f32[16,4096]{1,0:T(8,128)}, f32[16,4096]{1,0:T(8,128)S(1)}, u32[]{:S(2)}, u32[]{:S(2)}) collective-permute-start(f32[16,4096]{1,0:T(8,128)} %get-tuple-element.73), channel_id=1, source_target_pairs={{0,1},{1,0},{2,3},{3,2},{4,5},{5,4},{6,7},{7,6},{8,9},{9,8},{10,11... | collective-permute-start | bytes 786440 | tf_op jit(solution)/shard_map/ppermute | solution.py:367
  23.4 2.4 %collective-permute-start.4 = (f32[16,4096]{1,0:T(8,128)S(1)}, f32[16,4096]{1,0:T(8,128)S(1)}, u32[]{:S(2)}, u32[]{:S(2)}) collective-permute-start(f32[16,4096]{1,0:T(8,128)S(1)} %collective-permute-done.3.rest_0_), channel_id=1, source_target_pairs={{0,1},{1,0},{2,3},{3,2},{4,5},{5,4},{6,7},{7,6},{8,9},{9,8},{10,11... | collective-permute-start | bytes 786440 | tf_op jit(solution)/shard_map/ppermute | solution.py:367
  25.7 20.6 %collective-permute-start.6 = (bf16[16,2048]{1,0:T(8,128)(2,1)S(1)}, bf16[16,2048]{1,0:T(8,128)(2,1)S(1)}, u32[]{:S(2)}, u32[]{:S(2)}) collective-permute-start(bf16[16,2048]{1,0:T(8,128)(2,1)S(1)} %get-tuple-element.77), channel_id=1, source_target_pairs={{0,0},{1,4},{2,8},{3,12},{4,1},{5,5},{6,9},{7,13},{8,2},{9,6},{10,... | collective-permute-start | bytes 196616 | tf_op jit(solution)/shard_map/ppermute | solution.py:466
  26.4 20.0 %collective-permute-start.7 = (bf16[16,2048]{1,0:T(8,128)(2,1)S(1)}, bf16[16,2048]{1,0:T(8,128)(2,1)S(1)}, u32[]{:S(2)}, u32[]{:S(2)}) collective-permute-start(bf16[16,2048]{1,0:T(8,128)(2,1)S(1)} %get-tuple-element.78), channel_id=1, source_target_pairs={{0,1},{1,5},{2,9},{3,13},{4,0},{5,4},{6,8},{7,12},{8,3},{9,7},{10,... | collective-permute-start | bytes 196616 | tf_op jit(solution)/shard_map/ppermute | solution.py:466
  28.1 18.3 %collective-permute-start.8 = (bf16[16,2048]{1,0:T(8,128)(2,1)S(1)}, bf16[16,2048]{1,0:T(8,128)(2,1)S(1)}, u32[]{:S(2)}, u32[]{:S(2)}) collective-permute-start(bf16[16,2048]{1,0:T(8,128)(2,1)S(1)} %get-tuple-element.77), channel_id=1, source_target_pairs={{0,2},{1,6},{2,10},{3,14},{4,3},{5,7},{6,11},{7,15},{8,0},{9,4},{1... | collective-permute-start | bytes 196616 | tf_op jit(solution)/shard_map/ppermute | solution.py:466
  33.6 12.8 %collective-permute-start.9 = (bf16[16,2048]{1,0:T(8,128)(2,1)S(1)}, bf16[16,2048]{1,0:T(8,128)(2,1)S(1)}, u32[]{:S(2)}, u32[]{:S(2)}) collective-permute-start(bf16[16,2048]{1,0:T(8,128)(2,1)S(1)} %get-tuple-element.78), channel_id=1, source_target_pairs={{0,3},{1,7},{2,11},{3,15},{4,2},{5,6},{6,10},{7,14},{8,1},{9,5},{1... | collective-permute-start | bytes 196616 | tf_op jit(solution)/shard_map/ppermute | solution.py:466
  46.4 7.0 %collective-permute-start.10 = (f32[16,2048]{1,0:T(8,128)S(1)}, f32[16,2048]{1,0:T(8,128)S(1)}, u32[]{:S(2)}, u32[]{:S(2)}) collective-permute-start(f32[16,2048]{1,0:T(8,128)S(1)} %forward_one.1.rest_0_), channel_id=1, source_target_pairs={{0,2},{2,0},{1,3},{3,1},{4,6},{6,4},{5,7},{7,5},{8,10},{10,8},{9,1... | collective-permute-start | bytes 393224 | tf_op jit(solution)/shard_map/ppermute | solution.py:370
  53.5 10.7 %collective-permute-start.15 = (f32[32,2048]{1,0:T(8,128)S(1)}, f32[32,2048]{1,0:T(8,128)S(1)}, u32[]{:S(2)}, u32[]{:S(2)}) collective-permute-start(f32[32,2048]{1,0:T(8,128)S(1)} %get-tuple-element.94), channel_id=1, source_target_pairs={{0,1},{1,0},{2,3},{3,2},{4,5},{5,4},{6,7},{7,6},{8,9},{9,8},{10,11... | collective-permute-start | bytes 786440 | tf_op jit(solution)/shard_map/ppermute | solution.py:367
  54.2 9.4 %collective-permute-start.11 = (bf16[16,2048]{1,0:T(8,128)(2,1)S(1)}, bf16[16,2048]{1,0:T(8,128)(2,1)S(1)}, u32[]{:S(2)}, u32[]{:S(2)}) collective-permute-start(bf16[16,2048]{1,0:T(8,128)(2,1)S(1)} %get-tuple-element.90.ready), channel_id=1, source_target_pairs={{0,0},{1,8},{2,4},{3,12},{4,1},{5,9},{6,5},{7,13},{8,2},{9,10},{10... | collective-permute-start | bytes 196616 | tf_op jit(solution)/shard_map/ppermute | solution.py:504
  54.9 8.7 %collective-permute-start.12 = (bf16[16,2048]{1,0:T(8,128)(2,1)S(1)}, bf16[16,2048]{1,0:T(8,128)(2,1)S(1)}, u32[]{:S(2)}, u32[]{:S(2)}) collective-permute-start(bf16[16,2048]{1,0:T(8,128)(2,1)S(1)} %get-tuple-element.90.ready), channel_id=1, source_target_pairs={{0,8},{1,0},{2,12},{3,4},{4,9},{5,1},{6,13},{7,5},{8,10},{9,2},{10... | collective-permute-start | bytes 196616 | tf_op jit(solution)/shard_map/ppermute | solution.py:504
  59.5 5.4 %collective-permute-start.16 = (f32[16,2048]{1,0:T(8,128)S(1)}, f32[16,2048]{1,0:T(8,128)S(1)}, u32[]{:S(2)}, u32[]{:S(2)}) collective-permute-start(f32[16,2048]{1,0:T(8,128)S(1)} %get-tuple-element.96), channel_id=1, source_target_pairs={{0,1},{1,0},{2,3},{3,2},{4,5},{5,4},{6,7},{7,6},{8,9},{9,8},{10,11... | collective-permute-start | bytes 393224 | tf_op jit(solution)/shard_map/ppermute | solution.py:367
  59.5 5.4 %collective-permute-start.17 = (f32[8,2048]{1,0:T(8,128)}, f32[8,2048]{1,0:T(8,128)S(1)}, u32[]{:S(2)}, u32[]{:S(2)}) collective-permute-start(f32[8,2048]{1,0:T(8,128)} %get-tuple-element.97), channel_id=1, source_target_pairs={{0,1},{1,0},{2,3},{3,2},{4,5},{5,4},{6,7},{7,6},{8,9},{9,8},{10,11... | collective-permute-start | bytes 196616 | tf_op jit(solution)/shard_map/ppermute | solution.py:367
  75.6 7.5 %collective-permute-start.18 = (f32[16,2048]{1,0:T(8,128)S(1)}, f32[16,2048]{1,0:T(8,128)S(1)}, u32[]{:S(2)}, u32[]{:S(2)}) collective-permute-start(f32[16,2048]{1,0:T(8,128)S(1)} %forward_two.1.rest_0_), channel_id=1, source_target_pairs={{0,2},{2,0},{1,3},{3,1},{4,6},{6,4},{5,7},{7,5},{8,10},{10,8},{9,1... | collective-permute-start | bytes 393224 | tf_op jit(solution)/shard_map/ppermute | solution.py:370
  77.9 8.0 %collective-permute-start.20 = (bf16[8,2048]{1,0:T(8,128)(2,1)S(1)}, bf16[8,2048]{1,0:T(8,128)(2,1)S(1)}, u32[]{:S(2)}, u32[]{:S(2)}) collective-permute-start(bf16[8,2048]{1,0:T(8,128)(2,1)S(1)} %get-tuple-element.111), channel_id=1, source_target_pairs={{0,0},{1,4},{2,8},{3,12},{4,1},{5,5},{6,9},{7,13},{8,2},{9,6},{10,... | collective-permute-start | bytes 98312 | tf_op jit(solution)/shard_map/ppermute | solution.py:533
  78.6 7.3 %collective-permute-start.21 = (bf16[8,2048]{1,0:T(8,128)(2,1)S(1)}, bf16[8,2048]{1,0:T(8,128)(2,1)S(1)}, u32[]{:S(2)}, u32[]{:S(2)}) collective-permute-start(bf16[8,2048]{1,0:T(8,128)(2,1)S(1)} %get-tuple-element.112), channel_id=1, source_target_pairs={{0,1},{1,5},{2,9},{3,13},{4,0},{5,4},{6,8},{7,12},{8,3},{9,7},{10,... | collective-permute-start | bytes 98312 | tf_op jit(solution)/shard_map/ppermute | solution.py:533
  80.3 7.3 %collective-permute-start.22 = (bf16[8,2048]{1,0:T(8,128)(2,1)S(1)}, bf16[8,2048]{1,0:T(8,128)(2,1)S(1)}, u32[]{:S(2)}, u32[]{:S(2)}) collective-permute-start(bf16[8,2048]{1,0:T(8,128)(2,1)S(1)} %get-tuple-element.113), channel_id=1, source_target_pairs={{0,2},{1,6},{2,10},{3,14},{4,3},{5,7},{6,11},{7,15},{8,0},{9,4},{1... | collective-permute-start | bytes 98312 | tf_op jit(solution)/shard_map/ppermute | solution.py:533
  82.2 6.1 %collective-permute-start.23 = (bf16[8,2048]{1,0:T(8,128)(2,1)S(1)}, bf16[8,2048]{1,0:T(8,128)(2,1)S(1)}, u32[]{:S(2)}, u32[]{:S(2)}) collective-permute-start(bf16[8,2048]{1,0:T(8,128)(2,1)S(1)} %get-tuple-element.114), channel_id=1, source_target_pairs={{0,3},{1,7},{2,11},{3,15},{4,2},{5,6},{6,10},{7,14},{8,1},{9,5},{1... | collective-permute-start | bytes 98312 | tf_op jit(solution)/shard_map/ppermute | solution.py:533
  84.6 3.7 %collective-permute-start.19 = (f32[16,128]{1,0:T(8,128)S(1)}, f32[16,128]{1,0:T(8,128)S(1)}, u32[]{:S(2)}, u32[]{:S(2)}) collective-permute-start(f32[16,128]{1,0:T(8,128)S(1)} %get-tuple-element.110), channel_id=1, source_target_pairs={{0,1},{1,0},{2,3},{3,2},{4,5},{5,4},{6,7},{7,6},{8,9},{9,8},{10,11... | collective-permute-start | bytes 24584 | tf_op jit(solution)/shard_map/ppermute | solution.py:367
  88.4 6.0 %collective-permute-start.24 = (f32[16,128]{1,0:T(8,128)S(1)}, f32[16,128]{1,0:T(8,128)S(1)}, u32[]{:S(2)}, u32[]{:S(2)}) collective-permute-start(f32[16,128]{1,0:T(8,128)S(1)} %add.26.rest_0_), channel_id=1, source_target_pairs={{0,4},{4,0},{8,12},{12,8},{1,5},{5,1},{9,13},{13,9},{2,6},{6,2},{1... | collective-permute-start | bytes 24584 | tf_op jit(solution)/shard_map/ppermute | solution.py:546
  88.9 5.4 %collective-permute-start.25 = (f32[16,128]{1,0:T(8,128)S(1)}, f32[16,128]{1,0:T(8,128)S(1)}, u32[]{:S(2)}, u32[]{:S(2)}) collective-permute-start(f32[16,128]{1,0:T(8,128)S(1)} %add.26.rest_0_), channel_id=1, source_target_pairs={{0,8},{4,12},{8,0},{12,4},{1,9},{5,13},{9,1},{13,5},{2,10},{6,14},... | collective-permute-start | bytes 24584 | tf_op jit(solution)/shard_map/ppermute | solution.py:546
  90.3 5.4 %collective-permute-start.26 = (f32[16,128]{1,0:T(8,128)S(1)}, f32[16,128]{1,0:T(8,128)S(1)}, u32[]{:S(2)}, u32[]{:S(2)}) collective-permute-start(f32[16,128]{1,0:T(8,128)S(1)} %add.26.rest_0_), channel_id=1, source_target_pairs={{0,12},{4,8},{8,4},{12,0},{1,13},{5,9},{9,5},{13,1},{2,14},{6,10},... | collective-permute-start | bytes 24584 | tf_op jit(solution)/shard_map/ppermute | solution.py:546
  (6 other events, 56.7 us)

commit v6 on v5

--- a/solution.py
+++ b/solution.py
@@ -522,10 +522,7 @@
         compiler_params=params(4),
         name="collect",
     )(scalars, keep, give)
-    bases_other, adjoint_other = swap(bases_send), swap(adjoint_send)
-    *shards, first_total, bases_other, adjoint_other = lax.optimization_barrier(
-        (*shards, totals[0], bases_other, adjoint_other)
-    )
+    *shards, first_total = lax.optimization_barrier((*shards, totals[0]))
     totals = [first_total, *totals[1:]]
     induced = forward(tuple(CHUNKS + i for i in range(4)), shards, False, "forward_two")
 
@@ -541,7 +538,9 @@
         compiler_params=params(4),
         name="system",
     )(scalars, right_half, image, self_half, *induced)
-    system_other, *totals = lax.optimization_barrier((swap(system_give), *totals))
+    system_other, bases_send, adjoint_send, *totals = lax.optimization_barrier(
+        (swap(system_give), bases_send, adjoint_send, *totals)
+    )
     system = system_keep + system_other
     systems = [system] + [lax.ppermute(system, "rows", flip(k, n_rows)) for k in range(1, n_rows)]
     solution = pl.pallas_call(
@@ -551,7 +550,7 @@
         out_shape=struct((BLOCK, out_width), F32),
         compiler_params=params(4),
         name="solve",
-    )(scalars, bases_mine, bases_other, *systems)
+    )(scalars, bases_mine, swap(bases_send), *systems)
 
     adjoint = pl.pallas_call(
         functools.partial(update_kernel, len(totals)),
@@ -560,7 +559,7 @@
         out_shape=struct((BLOCK, out_width), F32),
         compiler_params=params(4),
         name="update",
-    )(scalars, adjoint_mine, adjoint_other, self_row, objectives, *totals)
+    )(scalars, adjoint_mine, swap(adjoint_send), self_row, objectives, *totals)
     return (solution, adjoint)
 
 

time: 99.1 us -> 99.3 us (level)
  transfers between devices with their start and end apart: 27 -> 27, of which waited for: 7 -> 6; matrix products, arithmetic and copies ran while one was open for 1% -> 1% of each run, Pallas kernels for 42% -> 42%
where the time goes in v6:
time: 99.3 us; the launch traced here: 98.9 us
  Pallas kernels  54.8 us (55%)
  starting transfers between devices  37 us (37%)
  waiting for transfers between devices  5.67 us (6%)
    pallas_call x2, Pallas kernels, forward(): pl.pallas_call(functools.partial(forward_kernel, 256, places, split), in_...  22.6 us
    pallas_call x1, Pallas kernels, per_device(): pl.pallas_call(functools.partial(load_adjoint_kernel, cuts), in_specs=[SM...  13.6 us
    ppermute x4, starting transfers between devices, per_device(): parts = [lax.ppermute(sends[k % 2], GRID, cross(k)) for k in range(side)]  8.48 us
    ppermute x11, starting transfers between devices, swap(): return lax.ppermute(value, 'rhs', flip(1, 2))  7.83 us
    ppermute x2, starting transfers between devices, cols_parts(): lax.ppermute(value, 'cols', flip(k, n_cols))  5.36 us
    ppermute x2, starting transfers between devices, per_device(): shards = [lax.ppermute(image_rounded, GRID, fetch(j)) for j in range(2)]  5.3 us
    ppermute x4, starting transfers between devices, per_device(): totals = [lax.ppermute(totals[k], GRID, cross(k)) for k in range(side)]  5 us
    pallas_call x1, Pallas kernels, per_device(): pl.pallas_call(functools.partial(adjoint_give_kernel, tile, len(parts)),...  4.47 us
  transfers between devices with their start and end apart: 27, of which 6 were waited for; matrix products, arithmetic and copies ran while one was open for 1% of the time, Pallas kernels for 42%

profile of v6, /device:TPU:0, one launch (start us, length us, event | category | flops | bytes accessed | tf_op | source)
XLA Modules:
  0.0 98.9 jit_solution(12747287370026631714)
XLA Ops:
  2.7 2.1 %right.1 = (f32[16,4096]{1,0:T(8,128)S(1)}, f32[16,2048]{1,0:T(8,128)S(1)}) custom-call(s32[12]{0:T(128)} %stack.55.scalars, f32[5,8]{1,0:T(8,128)} %pitch.1, f32[5,8]{1,0:T(8,128)S(1)} %collective-permute-done.pitch_other, s32[1,8]{1,0:T(1,128)} %bitcast.31, s32[1,8]{1,0:T(1,128)S(1)} %collective-permute-done.1.modes_other, s32[1,4096]{1,0:T(1,128)} %bitcast.29, ...), custom_call_target="tpu_custom_call" | custom-call | tf_op jit(solution)/shard_map/right/pallas_call | solution.py:399
  5.5 13.6 %adjoint_one.1 = (f32[16,4096]{1,0:T(8,128)}, f32[16,4096]{1,0:T(8,128)}, f32[16,2048]{1,0:T(8,128)}, f32[16,2048]{1,0:T(8,128)}, f32[1,2048]{1,0:T(1,128)}, /*index=5*/bf16[2048,8704]{1,0:T(8,128)(2,1)S(1)}) custom-call(s32[12]{0:T(128)} %stack.55.scalars, f32[8,4096]{1,0:T(8,128)} %objectives.3, f32[8,4096]{1,0:T(8,128)} %copy-done.2, f32[1,4096]{1,0:T(1,128)} %bitcast.17, ...), custom_call_target="tpu_custom_call" | custom-call | flops 570425344 | bytes 35651584 | tf_op jit(solution)/shard_map/adjoint_one/pallas_call | solution.py:414
  19.0 4.3 %collective-permute-start.5 = (f32[16,4096]{1,0:T(8,128)}, f32[16,4096]{1,0:T(8,128)S(1)}, u32[]{:S(2)}, u32[]{:S(2)}) collective-permute-start(f32[16,4096]{1,0:T(8,128)} %get-tuple-element.73), channel_id=1, source_target_pairs={{0,1},{1,0},{2,3},{3,2},{4,5},{5,4},{6,7},{7,6},{8,9},{9,8},{10,11... | collective-permute-start | bytes 786440 | tf_op jit(solution)/shard_map/ppermute | solution.py:367
  23.4 1.3 %collective-permute-done.5.other = f32[16,4096]{1,0:T(8,128)S(1)} collective-permute-done((f32[16,4096]{1,0:T(8,128)}, f32[16,4096]{1,0:T(8,128)S(1)}, u32[]{:S(2)}, u32[]{:S(2)}) %collective-permute-start.5) | collective-permute-done | bytes 262176 | tf_op jit(solution)/shard_map/ppermute | solution.py:367
  26.4 1.7 %collective-permute-start.7 = (bf16[16,2048]{1,0:T(8,128)(2,1)S(1)}, bf16[16,2048]{1,0:T(8,128)(2,1)S(1)}, u32[]{:S(2)}, u32[]{:S(2)}) collective-permute-start(bf16[16,2048]{1,0:T(8,128)(2,1)S(1)} %get-tuple-element.78), channel_id=1, source_target_pairs={{0,1},{1,5},{2,9},{3,13},{4,0},{5,4},{6,8},{7,12},{8,3},{9,7},{10,... | collective-permute-start | bytes 196616 | tf_op jit(solution)/shard_map/ppermute | solution.py:466
  28.1 5.5 %collective-permute-start.8 = (bf16[16,2048]{1,0:T(8,128)(2,1)S(1)}, bf16[16,2048]{1,0:T(8,128)(2,1)S(1)}, u32[]{:S(2)}, u32[]{:S(2)}) collective-permute-start(bf16[16,2048]{1,0:T(8,128)(2,1)S(1)} %get-tuple-element.77), channel_id=1, source_target_pairs={{0,2},{1,6},{2,10},{3,14},{4,3},{5,7},{6,11},{7,15},{8,0},{9,4},{1... | collective-permute-start | bytes 196616 | tf_op jit(solution)/shard_map/ppermute | solution.py:466
  34.2 12.1 %forward_one.1.rest_0_ = f32[16,2048]{1,0:T(8,128)S(1)} custom-call(s32[12]{0:T(128)} %stack.55.scalars, s32[1,512]{1,0:T(1,128)} %bitcast.20, s32[1,512]{1,0:T(1,128)} %bitcast.25, bf16[2048,8704]{1,0:T(8,128)(2,1)S(1)} %get-tuple-element.70.held, f32[16,4096]{1,0:T(8,128)S(1)} %collective-permute-done.3.rest_0_, f32[16,4096]{1,0:T(8,128)S(1)} %collective-permute-done.4.rest_1_), custom_call_target="tpu_custom_call" | custom-call | flops 570425344 | bytes 35651584 | tf_op jit(solution)/shard_map/forward_one/pallas_call | solution.py:442
  46.4 2.6 %collective-permute-start.10 = (f32[16,2048]{1,0:T(8,128)S(1)}, f32[16,2048]{1,0:T(8,128)S(1)}, u32[]{:S(2)}, u32[]{:S(2)}) collective-permute-start(f32[16,2048]{1,0:T(8,128)S(1)} %forward_one.1.rest_0_), channel_id=1, source_target_pairs={{0,2},{2,0},{1,3},{3,1},{4,6},{6,4},{5,7},{7,5},{8,10},{10,8},{9,1... | collective-permute-start | bytes 393224 | tf_op jit(solution)/shard_map/ppermute | solution.py:370
  49.0 4.5 %adjoint_two_give.1 = (f32[32,2048]{1,0:T(8,128)S(1)}, f32[16,2048]{1,0:T(8,128)}, f32[16,512]{1,0:T(8,128)}, f32[8,2048]{1,0:T(8,128)}, f32[8,2048]{1,0:T(8,128)}) custom-call(s32[12]{0:T(128)} %stack.55.scalars, f32[16,2048]{1,0:T(8,128)} %get-tuple-element.68.previous, f32[16,2048]{1,0:T(8,128)} %get-tuple-element.69.target, ...), custom_call_target="tpu_custom_call" | custom-call | flops 285212672 | bytes 17825792 | tf_op jit(solution)/shard_map/adjoint_two_give/pallas_call | solution.py:470
  54.9 4.6 %collective-permute-start.12 = (bf16[16,2048]{1,0:T(8,128)(2,1)S(1)}, bf16[16,2048]{1,0:T(8,128)(2,1)S(1)}, u32[]{:S(2)}, u32[]{:S(2)}) collective-permute-start(bf16[16,2048]{1,0:T(8,128)(2,1)S(1)} %get-tuple-element.91.ready), channel_id=1, source_target_pairs={{0,8},{1,0},{2,12},{3,4},{4,9},{5,1},{6,13},{7,5},{8,10},{9,2},{10... | collective-permute-start | bytes 196616 | tf_op jit(solution)/shard_map/ppermute | solution.py:504
  59.5 3.6 %adjoint_two_keep.1.keep = f32[32,2048]{1,0:T(8,128)S(1)} custom-call(s32[12]{0:T(128)} %stack.55.scalars, f32[16,2048]{1,0:T(8,128)} %get-tuple-element.89.adjoint, f32[16,512]{1,0:T(8,128)} %get-tuple-element.90.carried, s32[1,512]{1,0:T(1,128)} %bitcast.22, s32[1,512]{1,0:T(1,128)} %bitcast.27, bf16[2048,8704]{1,0:T(8,128)(2,1)S(1)} %get-tuple-element.70.held, ...), custom_call_target="tpu_custom_call" | custom-call | flops 285212672 | bytes 17825792 | tf_op jit(solution)/shard_map/adjoint_two_keep/pallas_call | solution.py:505
  64.6 10.5 %forward_two.1.rest_0_ = f32[16,2048]{1,0:T(8,128)S(1)} custom-call(s32[12]{0:T(128)} %stack.55.scalars, s32[1,512]{1,0:T(1,128)} %bitcast.23, s32[1,512]{1,0:T(1,128)} %bitcast.28, bf16[2048,8704]{1,0:T(8,128)(2,1)S(1)} %get-tuple-element.70.held, bf16[16,2048]{1,0:T(8,128)(2,1)S(1)} %collective-permute-done.11.rest_0_, ...), custom_call_target="tpu_custom_call" | custom-call | flops 570425344 | bytes 35651584 | tf_op jit(solution)/shard_map/forward_two/pallas_call | solution.py:442
  75.1 2.8 %collective-permute-start.16 = (f32[16,2048]{1,0:T(8,128)S(1)}, f32[16,2048]{1,0:T(8,128)S(1)}, u32[]{:S(2)}, u32[]{:S(2)}) collective-permute-start(f32[16,2048]{1,0:T(8,128)S(1)} %forward_two.1.rest_0_), channel_id=1, source_target_pairs={{0,2},{2,0},{1,3},{3,1},{4,6},{6,4},{5,7},{7,5},{8,10},{10,8},{9,1... | collective-permute-start | bytes 393224 | tf_op jit(solution)/shard_map/ppermute | solution.py:370
  78.6 1.2 %collective-permute-start.19 = (bf16[8,2048]{1,0:T(8,128)(2,1)S(1)}, bf16[8,2048]{1,0:T(8,128)(2,1)S(1)}, u32[]{:S(2)}, u32[]{:S(2)}) collective-permute-start(bf16[8,2048]{1,0:T(8,128)(2,1)S(1)} %get-tuple-element.110), channel_id=1, source_target_pairs={{0,1},{1,5},{2,9},{3,13},{4,0},{5,4},{6,8},{7,12},{8,3},{9,7},{10,... | collective-permute-start | bytes 98312 | tf_op jit(solution)/shard_map/ppermute | solution.py:530
  79.8 2.0 %collective-permute-start.20 = (bf16[8,2048]{1,0:T(8,128)(2,1)S(1)}, bf16[8,2048]{1,0:T(8,128)(2,1)S(1)}, u32[]{:S(2)}, u32[]{:S(2)}) collective-permute-start(bf16[8,2048]{1,0:T(8,128)(2,1)S(1)} %get-tuple-element.111), channel_id=1, source_target_pairs={{0,2},{1,6},{2,10},{3,14},{4,3},{5,7},{6,11},{7,15},{8,0},{9,4},{1... | collective-permute-start | bytes 98312 | tf_op jit(solution)/shard_map/ppermute | solution.py:530
  81.7 1.2 %collective-permute-start.21 = (bf16[8,2048]{1,0:T(8,128)(2,1)S(1)}, bf16[8,2048]{1,0:T(8,128)(2,1)S(1)}, u32[]{:S(2)}, u32[]{:S(2)}) collective-permute-start(bf16[8,2048]{1,0:T(8,128)(2,1)S(1)} %get-tuple-element.112), channel_id=1, source_target_pairs={{0,3},{1,7},{2,11},{3,15},{4,2},{5,6},{6,10},{7,14},{8,1},{9,5},{1... | collective-permute-start | bytes 98312 | tf_op jit(solution)/shard_map/ppermute | solution.py:530
  82.9 1.6 %system.1 = (f32[16,128]{1,0:T(8,128)S(1)}, f32[16,128]{1,0:T(8,128)S(1)}) custom-call(s32[12]{0:T(128)} %stack.55.scalars, f32[16,2048]{1,0:T(8,128)S(1)} %get-tuple-element.62.right_half.basis, f32[16,2048]{1,0:T(8,128)S(1)} %get-tuple-element.88.image, f32[1,2048]{1,0:T(1,128)S(1)} %copy-done, f32[16,2048]{1,0:T(8,128)S(1)} %forward_two.1.rest_0_, ...), custom_call_target="tpu_custom_call" | custom-call | tf_op jit(solution)/shard_map/system/pallas_call | solution.py:533
  84.5 1.3 %collective-permute-start.17 = (f32[16,128]{1,0:T(8,128)S(1)}, f32[16,128]{1,0:T(8,128)S(1)}, u32[]{:S(2)}, u32[]{:S(2)}) collective-permute-start(f32[16,128]{1,0:T(8,128)S(1)} %get-tuple-element.106), channel_id=1, source_target_pairs={{0,1},{1,0},{2,3},{3,2},{4,5},{5,4},{6,7},{7,6},{8,9},{9,8},{10,11... | collective-permute-start | bytes 24584 | tf_op jit(solution)/shard_map/ppermute | solution.py:367
  85.8 2.4 %collective-permute-done.20.rest_2_ = bf16[8,2048]{1,0:T(8,128)(2,1)S(1)} collective-permute-done((bf16[8,2048]{1,0:T(8,128)(2,1)S(1)}, bf16[8,2048]{1,0:T(8,128)(2,1)S(1)}, u32[]{:S(2)}, u32[]{:S(2)}) %collective-permute-start.20) | collective-permute-done | bytes 32800 | tf_op jit(solution)/shard_map/ppermute | solution.py:530
  89.0 1.5 %collective-permute-start.24 = (f32[16,128]{1,0:T(8,128)S(1)}, f32[16,128]{1,0:T(8,128)S(1)}, u32[]{:S(2)}, u32[]{:S(2)}) collective-permute-start(f32[16,128]{1,0:T(8,128)S(1)} %add.26.rest_0_), channel_id=1, source_target_pairs={{0,8},{4,12},{8,0},{12,4},{1,9},{5,13},{9,1},{13,5},{2,10},{6,14},... | collective-permute-start | bytes 24584 | tf_op jit(solution)/shard_map/ppermute | solution.py:545
  90.5 2.6 %collective-permute-start.25 = (f32[16,128]{1,0:T(8,128)S(1)}, f32[16,128]{1,0:T(8,128)S(1)}, u32[]{:S(2)}, u32[]{:S(2)}) collective-permute-start(f32[16,128]{1,0:T(8,128)S(1)} %add.26.rest_0_), channel_id=1, source_target_pairs={{0,12},{4,8},{8,4},{12,0},{1,13},{5,9},{9,5},{13,1},{2,14},{6,10},... | collective-permute-start | bytes 24584 | tf_op jit(solution)/shard_map/ppermute | solution.py:545
  93.1 1.6 %update.1 = f32[8,2048]{1,0:T(8,128)} custom-call(s32[12]{0:T(128)} %stack.55.scalars, f32[8,2048]{1,0:T(8,128)S(1)} %copy-done.1, f32[8,2048]{1,0:T(8,128)S(1)} %collective-permute-done.26.received, f32[1,4096]{1,0:T(1,128)} %bitcast.18, f32[8,4096]{1,0:T(8,128)} %objectives.3, bf16[8,2048]{1,0:T(8,128)(2,1)S(1)} %collective-permute-done.18.rest_0_, ...), custom_call_target="tpu_custom_call" | custom-call | tf_op jit(solution)/shard_map/update/pallas_call | solution.py:555
  94.7 1.2 %collective-permute-done.25.rest_3_ = f32[16,128]{1,0:T(8,128)S(1)} collective-permute-done((f32[16,128]{1,0:T(8,128)S(1)}, f32[16,128]{1,0:T(8,128)S(1)}, u32[]{:S(2)}, u32[]{:S(2)}) %collective-permute-start.25) | collective-permute-done | bytes 8224 | tf_op jit(solution)/shard_map/ppermute | solution.py:545
  96.0 3.0 %solve.1 = f32[8,2048]{1,0:T(8,128)} custom-call(s32[12]{0:T(128)} %stack.55.scalars, f32[16,2048]{1,0:T(8,128)S(1)} %get-tuple-element.87.mine, f32[16,2048]{1,0:T(8,128)S(1)} %collective-permute-done.22.received, f32[16,128]{1,0:T(8,128)S(1)} %add.26.rest_0_, f32[16,128]{1,0:T(8,128)S(1)} %collective-permute-done.23.rest_1_, ...), custom_call_target="tpu_custom_call" | custom-call | tf_op jit(solution)/shard_map/solve/pallas_call | solution.py:546
  (52 shorter events, 9.5 us)
Async XLA Ops:
  0.6 4.1 %collective-permute-start.2 = (f32[8,4096]{1,0:T(8,128)}, f32[8,4096]{1,0:T(8,128)S(1)}, u32[]{:S(2)}, u32[]{:S(2)}) collective-permute-start(f32[8,4096]{1,0:T(8,128)} %objectives.3), channel_id=1, source_target_pairs={{0,1},{1,0},{2,3},{3,2},{4,5},{5,4},{6,7},{7,6},{8,9},{9,8},{10,11... | collective-permute-start | bytes 393224 | tf_op jit(solution)/shard_map/ppermute | solution.py:367
  1.2 1.5 %collective-permute-start = (f32[5,8]{1,0:T(8,128)}, f32[5,8]{1,0:T(8,128)S(1)}, u32[]{:S(2)}, u32[]{:S(2)}) collective-permute-start(f32[5,8]{1,0:T(8,128)} %pitch.1), channel_id=1, source_target_pairs={{0,1},{1,0},{2,3},{3,2},{4,5},{5,4},{6,7},{7,6},{8,9},{9,8},{10,11... | collective-permute-start | bytes 488 | tf_op jit(solution)/shard_map/ppermute | solution.py:367
  4.8 18.6 %collective-permute-start.3 = (f32[16,4096]{1,0:T(8,128)S(1)}, f32[16,4096]{1,0:T(8,128)S(1)}, u32[]{:S(2)}, u32[]{:S(2)}) collective-permute-start(f32[16,4096]{1,0:T(8,128)S(1)} %get-tuple-element.66), channel_id=1, source_target_pairs={{0,0},{1,4},{2,8},{3,12},{4,1},{5,5},{6,9},{7,13},{8,2},{9,6},{10,... | collective-permute-start | bytes 786440 | tf_op jit(solution)/shard_map/ppermute | solution.py:412
  19.0 5.7 %collective-permute-start.5 = (f32[16,4096]{1,0:T(8,128)}, f32[16,4096]{1,0:T(8,128)S(1)}, u32[]{:S(2)}, u32[]{:S(2)}) collective-permute-start(f32[16,4096]{1,0:T(8,128)} %get-tuple-element.73), channel_id=1, source_target_pairs={{0,1},{1,0},{2,3},{3,2},{4,5},{5,4},{6,7},{7,6},{8,9},{9,8},{10,11... | collective-permute-start | bytes 786440 | tf_op jit(solution)/shard_map/ppermute | solution.py:367
  23.4 2.4 %collective-permute-start.4 = (f32[16,4096]{1,0:T(8,128)S(1)}, f32[16,4096]{1,0:T(8,128)S(1)}, u32[]{:S(2)}, u32[]{:S(2)}) collective-permute-start(f32[16,4096]{1,0:T(8,128)S(1)} %collective-permute-done.3.rest_0_), channel_id=1, source_target_pairs={{0,1},{1,0},{2,3},{3,2},{4,5},{5,4},{6,7},{7,6},{8,9},{9,8},{10,11... | collective-permute-start | bytes 786440 | tf_op jit(solution)/shard_map/ppermute | solution.py:367
  25.7 20.6 %collective-permute-start.6 = (bf16[16,2048]{1,0:T(8,128)(2,1)S(1)}, bf16[16,2048]{1,0:T(8,128)(2,1)S(1)}, u32[]{:S(2)}, u32[]{:S(2)}) collective-permute-start(bf16[16,2048]{1,0:T(8,128)(2,1)S(1)} %get-tuple-element.77), channel_id=1, source_target_pairs={{0,0},{1,4},{2,8},{3,12},{4,1},{5,5},{6,9},{7,13},{8,2},{9,6},{10,... | collective-permute-start | bytes 196616 | tf_op jit(solution)/shard_map/ppermute | solution.py:466
  26.4 20.0 %collective-permute-start.7 = (bf16[16,2048]{1,0:T(8,128)(2,1)S(1)}, bf16[16,2048]{1,0:T(8,128)(2,1)S(1)}, u32[]{:S(2)}, u32[]{:S(2)}) collective-permute-start(bf16[16,2048]{1,0:T(8,128)(2,1)S(1)} %get-tuple-element.78), channel_id=1, source_target_pairs={{0,1},{1,5},{2,9},{3,13},{4,0},{5,4},{6,8},{7,12},{8,3},{9,7},{10,... | collective-permute-start | bytes 196616 | tf_op jit(solution)/shard_map/ppermute | solution.py:466
  28.1 18.3 %collective-permute-start.8 = (bf16[16,2048]{1,0:T(8,128)(2,1)S(1)}, bf16[16,2048]{1,0:T(8,128)(2,1)S(1)}, u32[]{:S(2)}, u32[]{:S(2)}) collective-permute-start(bf16[16,2048]{1,0:T(8,128)(2,1)S(1)} %get-tuple-element.77), channel_id=1, source_target_pairs={{0,2},{1,6},{2,10},{3,14},{4,3},{5,7},{6,11},{7,15},{8,0},{9,4},{1... | collective-permute-start | bytes 196616 | tf_op jit(solution)/shard_map/ppermute | solution.py:466
  33.6 12.8 %collective-permute-start.9 = (bf16[16,2048]{1,0:T(8,128)(2,1)S(1)}, bf16[16,2048]{1,0:T(8,128)(2,1)S(1)}, u32[]{:S(2)}, u32[]{:S(2)}) collective-permute-start(bf16[16,2048]{1,0:T(8,128)(2,1)S(1)} %get-tuple-element.78), channel_id=1, source_target_pairs={{0,3},{1,7},{2,11},{3,15},{4,2},{5,6},{6,10},{7,14},{8,1},{9,5},{1... | collective-permute-start | bytes 196616 | tf_op jit(solution)/shard_map/ppermute | solution.py:466
  46.4 7.0 %collective-permute-start.10 = (f32[16,2048]{1,0:T(8,128)S(1)}, f32[16,2048]{1,0:T(8,128)S(1)}, u32[]{:S(2)}, u32[]{:S(2)}) collective-permute-start(f32[16,2048]{1,0:T(8,128)S(1)} %forward_one.1.rest_0_), channel_id=1, source_target_pairs={{0,2},{2,0},{1,3},{3,1},{4,6},{6,4},{5,7},{7,5},{8,10},{10,8},{9,1... | collective-permute-start | bytes 393224 | tf_op jit(solution)/shard_map/ppermute | solution.py:370
  53.5 10.2 %collective-permute-start.15 = (f32[32,2048]{1,0:T(8,128)S(1)}, f32[32,2048]{1,0:T(8,128)S(1)}, u32[]{:S(2)}, u32[]{:S(2)}) collective-permute-start(f32[32,2048]{1,0:T(8,128)S(1)} %get-tuple-element.95), channel_id=1, source_target_pairs={{0,1},{1,0},{2,3},{3,2},{4,5},{5,4},{6,7},{7,6},{8,9},{9,8},{10,11... | collective-permute-start | bytes 786440 | tf_op jit(solution)/shard_map/ppermute | solution.py:367
  54.2 8.9 %collective-permute-start.11 = (bf16[16,2048]{1,0:T(8,128)(2,1)S(1)}, bf16[16,2048]{1,0:T(8,128)(2,1)S(1)}, u32[]{:S(2)}, u32[]{:S(2)}) collective-permute-start(bf16[16,2048]{1,0:T(8,128)(2,1)S(1)} %get-tuple-element.91.ready), channel_id=1, source_target_pairs={{0,0},{1,8},{2,4},{3,12},{4,1},{5,9},{6,5},{7,13},{8,2},{9,10},{10... | collective-permute-start | bytes 196616 | tf_op jit(solution)/shard_map/ppermute | solution.py:504
  54.9 8.2 %collective-permute-start.12 = (bf16[16,2048]{1,0:T(8,128)(2,1)S(1)}, bf16[16,2048]{1,0:T(8,128)(2,1)S(1)}, u32[]{:S(2)}, u32[]{:S(2)}) collective-permute-start(bf16[16,2048]{1,0:T(8,128)(2,1)S(1)} %get-tuple-element.91.ready), channel_id=1, source_target_pairs={{0,8},{1,0},{2,12},{3,4},{4,9},{5,1},{6,13},{7,5},{8,10},{9,2},{10... | collective-permute-start | bytes 196616 | tf_op jit(solution)/shard_map/ppermute | solution.py:504
  75.1 7.8 %collective-permute-start.16 = (f32[16,2048]{1,0:T(8,128)S(1)}, f32[16,2048]{1,0:T(8,128)S(1)}, u32[]{:S(2)}, u32[]{:S(2)}) collective-permute-start(f32[16,2048]{1,0:T(8,128)S(1)} %forward_two.1.rest_0_), channel_id=1, source_target_pairs={{0,2},{2,0},{1,3},{3,1},{4,6},{6,4},{5,7},{7,5},{8,10},{10,8},{9,1... | collective-permute-start | bytes 393224 | tf_op jit(solution)/shard_map/ppermute | solution.py:370
  77.9 7.9 %collective-permute-start.18 = (bf16[8,2048]{1,0:T(8,128)(2,1)S(1)}, bf16[8,2048]{1,0:T(8,128)(2,1)S(1)}, u32[]{:S(2)}, u32[]{:S(2)}) collective-permute-start(bf16[8,2048]{1,0:T(8,128)(2,1)S(1)} %get-tuple-element.109), channel_id=1, source_target_pairs={{0,0},{1,4},{2,8},{3,12},{4,1},{5,5},{6,9},{7,13},{8,2},{9,6},{10,... | collective-permute-start | bytes 98312 | tf_op jit(solution)/shard_map/ppermute | solution.py:530
  78.6 7.2 %collective-permute-start.19 = (bf16[8,2048]{1,0:T(8,128)(2,1)S(1)}, bf16[8,2048]{1,0:T(8,128)(2,1)S(1)}, u32[]{:S(2)}, u32[]{:S(2)}) collective-permute-start(bf16[8,2048]{1,0:T(8,128)(2,1)S(1)} %get-tuple-element.110), channel_id=1, source_target_pairs={{0,1},{1,5},{2,9},{3,13},{4,0},{5,4},{6,8},{7,12},{8,3},{9,7},{10,... | collective-permute-start | bytes 98312 | tf_op jit(solution)/shard_map/ppermute | solution.py:530
  79.8 8.5 %collective-permute-start.20 = (bf16[8,2048]{1,0:T(8,128)(2,1)S(1)}, bf16[8,2048]{1,0:T(8,128)(2,1)S(1)}, u32[]{:S(2)}, u32[]{:S(2)}) collective-permute-start(bf16[8,2048]{1,0:T(8,128)(2,1)S(1)} %get-tuple-element.111), channel_id=1, source_target_pairs={{0,2},{1,6},{2,10},{3,14},{4,3},{5,7},{6,11},{7,15},{8,0},{9,4},{1... | collective-permute-start | bytes 98312 | tf_op jit(solution)/shard_map/ppermute | solution.py:530
  81.7 6.5 %collective-permute-start.21 = (bf16[8,2048]{1,0:T(8,128)(2,1)S(1)}, bf16[8,2048]{1,0:T(8,128)(2,1)S(1)}, u32[]{:S(2)}, u32[]{:S(2)}) collective-permute-start(bf16[8,2048]{1,0:T(8,128)(2,1)S(1)} %get-tuple-element.112), channel_id=1, source_target_pairs={{0,3},{1,7},{2,11},{3,15},{4,2},{5,6},{6,10},{7,14},{8,1},{9,5},{1... | collective-permute-start | bytes 98312 | tf_op jit(solution)/shard_map/ppermute | solution.py:530
  84.5 3.7 %collective-permute-start.17 = (f32[16,128]{1,0:T(8,128)S(1)}, f32[16,128]{1,0:T(8,128)S(1)}, u32[]{:S(2)}, u32[]{:S(2)}) collective-permute-start(f32[16,128]{1,0:T(8,128)S(1)} %get-tuple-element.106), channel_id=1, source_target_pairs={{0,1},{1,0},{2,3},{3,2},{4,5},{5,4},{6,7},{7,6},{8,9},{9,8},{10,11... | collective-permute-start | bytes 24584 | tf_op jit(solution)/shard_map/ppermute | solution.py:367
  88.2 7.7 %collective-permute-start.22 = (f32[16,2048]{1,0:T(8,128)S(1)}, f32[16,2048]{1,0:T(8,128)S(1)}, u32[]{:S(2)}, u32[]{:S(2)}) collective-permute-start(f32[16,2048]{1,0:T(8,128)S(1)} %get-tuple-element.113), channel_id=1, source_target_pairs={{0,1},{1,0},{2,3},{3,2},{4,5},{5,4},{6,7},{7,6},{8,9},{9,8},{10,11... | collective-permute-start | bytes 393224 | tf_op jit(solution)/shard_map/ppermute | solution.py:367
  88.4 4.7 %collective-permute-start.26 = (f32[8,2048]{1,0:T(8,128)S(1)}, f32[8,2048]{1,0:T(8,128)S(1)}, u32[]{:S(2)}, u32[]{:S(2)}) collective-permute-start(f32[8,2048]{1,0:T(8,128)S(1)} %copy-done.3), channel_id=1, source_target_pairs={{0,1},{1,0},{2,3},{3,2},{4,5},{5,4},{6,7},{7,6},{8,9},{9,8},{10,11... | collective-permute-start | bytes 196616 | tf_op jit(solution)/shard_map/ppermute | solution.py:367
  88.7 6.0 %collective-permute-start.23 = (f32[16,128]{1,0:T(8,128)S(1)}, f32[16,128]{1,0:T(8,128)S(1)}, u32[]{:S(2)}, u32[]{:S(2)}) collective-permute-start(f32[16,128]{1,0:T(8,128)S(1)} %add.26.rest_0_), channel_id=1, source_target_pairs={{0,4},{4,0},{8,12},{12,8},{1,5},{5,1},{9,13},{13,9},{2,6},{6,2},{1... | collective-permute-start | bytes 24584 | tf_op jit(solution)/shard_map/ppermute | solution.py:545
  89.0 5.8 %collective-permute-start.24 = (f32[16,128]{1,0:T(8,128)S(1)}, f32[16,128]{1,0:T(8,128)S(1)}, u32[]{:S(2)}, u32[]{:S(2)}) collective-permute-start(f32[16,128]{1,0:T(8,128)S(1)} %add.26.rest_0_), channel_id=1, source_target_pairs={{0,8},{4,12},{8,0},{12,4},{1,9},{5,13},{9,1},{13,5},{2,10},{6,14},... | collective-permute-start | bytes 24584 | tf_op jit(solution)/shard_map/ppermute | solution.py:545
  90.5 5.4 %collective-permute-start.25 = (f32[16,128]{1,0:T(8,128)S(1)}, f32[16,128]{1,0:T(8,128)S(1)}, u32[]{:S(2)}, u32[]{:S(2)}) collective-permute-start(f32[16,128]{1,0:T(8,128)S(1)} %add.26.rest_0_), channel_id=1, source_target_pairs={{0,12},{4,8},{8,4},{12,0},{1,13},{5,9},{9,5},{13,1},{2,14},{6,10},... | collective-permute-start | bytes 24584 | tf_op jit(solution)/shard_map/ppermute | solution.py:545
  (7 other events, 86.3 us)
